TPU v7x, 32 devices: a whole 2x2x4 slice. The times are simulated.
32 devices in a mesh: dp: 4 (over z), sq: 8 (over y, x, core).
Axes of the slice: x: 2, y: 2, z: 4, core: 2. Of those that a mesh axis runs over, the one named last changes fastest.
Arguments:
- frames: bfloat16 [4, 1024, 1024], P('dp', 'sq'), may hold values from -6 to 6
- norm1_gain: float32 [1024], replicated, may hold values from 0.5 to 1.5
- w_qkv: bfloat16 [1024, 3072], replicated, may hold values from -0.1875 to 0.1875
- w_out: bfloat16 [1024, 1024], replicated, may hold values from -0.75 to 0.75
- norm2_gain: float32 [1024], replicated, may hold values from 0.5 to 1.5
- w_up: bfloat16 [1024, 4096], replicated, may hold values from -0.1875 to 0.1875
- w_down: bfloat16 [4096, 1024], replicated, may hold values from -0.09375 to 0.09375
- lengths: int32 [4, 8], P('dp'), may hold values from 1 to 896, as said below
- cotangent: bfloat16 [4, 1024, 1024], P('dp', 'sq'), may hold values from -6 to 6
Outputs:
- out: bfloat16 [4, 1024, 1024], P('dp', 'sq')
- d_in: float32 [4, 1024, 1024], P('dp', 'sq')
- g_norm1: float32 [1024], P('sq')
- g_qkv: float32 [1024, 3072], P('sq')
- g_out: float32 [1024, 1024], P('sq')
- g_norm2: float32 [1024], P('sq')
- g_up: float32 [1024, 4096], P('sq')
- g_down: float32 [4096, 1024], P('sq')
Inputs may be any that keep to these rules, and one draw needn't show every extreme that they name: Each row's lengths sum to 1024. In each row exactly one item has 896 frames and is neither the first nor the last item of the row; the other items share the remaining 128 frames.
All inputs are finite; a program needn't handle non-finite values.
Results may differ from a plain program's by a relative error of at most 0.025.
Values may be sent and summed in bfloat16 or wider, within the bound.
A program may use at most 256 MiB of HBM per device.

v0:
```python
import jax
import jax.numpy as jnp
from jax import lax
from jax.sharding import PartitionSpec as P

HEADS = 16
HEAD_DIM = 64


EPSILON = 1e-05
NEG_FILL = -1000000000.0
START_MAX = -1e30


def norm_scaled(values, gain):
    return values * lax.rsqrt(jnp.mean(values * values, axis=-1, keepdims=True) + EPSILON) * gain


def segment_ids(positions, item_ends):
    return jnp.sum((positions[None, :, None] >= item_ends[:, None, :]).astype(jnp.int32), axis=2)


def visible(query_pos, query_seg, key_pos, key_seg):
    return (key_pos[None, None, :] <= query_pos[None, :, None]) & (
        key_seg[:, None, :] == query_seg[:, :, None]
    )


def block_size(count, limit):
    for candidate in range(min(count, limit), 0, -1):
        if count % candidate == 0:
            return candidate
    return count


def over_blocks(carry, arrays, start, step_fn, limit):
    count = arrays[0].shape[1]
    size = block_size(count, limit)
    number = count // size
    if number == 1:
        return step_fn(carry, arrays, start)
    stacked = tuple(
        (
            jnp.swapaxes(member.reshape((member.shape[0], number, size) + member.shape[2:]), 0, 1)
            for member in arrays
        )
    )

    def turn(state, item):
        offset, pieces = item
        return (step_fn(state, pieces, start + offset * size), None)

    offsets = jnp.arange(number, dtype=jnp.int32)
    return lax.scan(turn, carry, (offsets, stacked))[0]


def contract_rows(left, right):
    return lax.dot_general(
        left, right, (((0,), (0,)), ((), ())), preferred_element_type=jnp.float32
    )


def times_transpose(left, right):
    return lax.dot_general(
        left, right, (((1,), (1,)), ((), ())), preferred_element_type=jnp.float32
    )


def heads_flat(values, batch, rows, width):
    return values.transpose(0, 2, 1, 3).reshape(batch * rows, width)


def shards(frames, norm1_gain, w_qkv, w_out, norm2_gain, w_up, w_down, lengths, cotangent):
    batch = frames.shape[0]
    rows = frames.shape[1]
    width = frames.shape[2]
    factor = HEAD_DIM ** (-0.5)
    first = lax.axis_index("sq") * rows
    query_pos = first + jnp.arange(rows, dtype=jnp.int32)
    item_ends = jnp.cumsum(lengths, axis=1)
    query_seg = segment_ids(query_pos, item_ends)
    frames_own = frames.reshape(batch * rows, width).astype(jnp.float32)
    hidden1, norm1_pull = jax.vjp(norm_scaled, frames_own, norm1_gain)
    hidden1_low = hidden1.astype(jnp.bfloat16)
    mixed = jnp.dot(hidden1_low, w_qkv, preferred_element_type=jnp.float32).astype(jnp.bfloat16)
    query_rows = mixed[:, :width].reshape(batch, rows, width)
    key_rows = mixed[:, width : 2 * width].reshape(batch, rows, width)
    value_rows = mixed[:, 2 * width :].reshape(batch, rows, width)
    queries = query_rows.reshape(batch, rows, HEADS, HEAD_DIM)
    keys_own = key_rows.reshape(batch, rows, HEADS, HEAD_DIM)
    values_own = value_rows.reshape(batch, rows, HEADS, HEAD_DIM)

    def forward_step(carry, pieces, start):
        key_piece, value_piece = pieces
        count = key_piece.shape[1]
        key_pos = start + jnp.arange(count, dtype=jnp.int32)
        key_seg = segment_ids(key_pos, item_ends)

        def forward_work(state):
            running_max, running_sum, accum = state
            keys_block = key_piece.reshape(batch, count, HEADS, HEAD_DIM)
            values_block = value_piece.reshape(batch, count, HEADS, HEAD_DIM)
            scores = (
                jnp.einsum(
                    "rqhd,rkhd->rhqk", queries, keys_block, preferred_element_type=jnp.float32
                )
                * factor
            )
            mask = visible(query_pos, query_seg, key_pos, key_seg)[:, None]
            scores = jnp.where(mask, scores, NEG_FILL)
            new_max = jnp.maximum(running_max, jnp.max(scores, axis=-1))
            weights = jnp.where(mask, jnp.exp(scores - new_max[..., None]), 0.0)
            decay = jnp.exp(running_max - new_max)
            new_sum = decay * running_sum + jnp.sum(weights, axis=-1)
            update = jnp.einsum(
                "rhqk,rkhd->rhqd",
                weights.astype(jnp.bfloat16),
                values_block,
                preferred_element_type=jnp.float32,
            )
            return (new_max, new_sum, decay[..., None] * accum + update)

        return lax.cond(start <= query_pos[-1], forward_work, lambda state: state, carry)

    start_state = (
        jnp.full((batch, HEADS, rows), START_MAX, jnp.float32),
        jnp.zeros((batch, HEADS, rows), jnp.float32),
        jnp.zeros((batch, HEADS, rows, HEAD_DIM), jnp.float32),
    )
    final_max, final_sum, accum = over_blocks(
        start_state,
        (
            lax.all_gather(key_rows, "sq", axis=1, tiled=True),
            lax.all_gather(value_rows, "sq", axis=1, tiled=True),
        ),
        jnp.int32(0),
        forward_step,
        512,
    )
    attended = heads_flat(accum / final_sum[..., None], batch, rows, width)
    log_total = final_max + jnp.log(final_sum)
    attended_low = attended.astype(jnp.bfloat16)
    middle = frames_own + jnp.dot(attended_low, w_out, preferred_element_type=jnp.float32)
    hidden2, norm2_pull = jax.vjp(norm_scaled, middle, norm2_gain)
    hidden2_low = hidden2.astype(jnp.bfloat16)
    upward = jnp.dot(hidden2_low, w_up, preferred_element_type=jnp.float32)
    active, gelu_pull = jax.vjp(jax.nn.gelu, upward)
    active_low = active.astype(jnp.bfloat16)
    result = middle + jnp.dot(active_low, w_down, preferred_element_type=jnp.float32)
    grad_top = cotangent.reshape(batch * rows, width).astype(jnp.float32)
    grad_branch = grad_top.astype(jnp.bfloat16)
    grad_down = contract_rows(active_low, grad_branch)
    grad_active = times_transpose(grad_branch, w_down)
    grad_upward = gelu_pull(grad_active)[0].astype(jnp.bfloat16)
    grad_up = contract_rows(hidden2_low, grad_upward)
    grad_hidden2 = times_transpose(grad_upward, w_up)
    grad_middle_part, grad_gain2 = norm2_pull(grad_hidden2)
    grad_middle = grad_top + grad_middle_part
    grad_attn = grad_middle.astype(jnp.bfloat16)
    grad_outproj = contract_rows(attended_low, grad_attn)
    grad_attended = times_transpose(grad_attn, w_out).astype(jnp.bfloat16)
    grad_rows_own = grad_attended.reshape(batch, rows, width)
    grad_heads = grad_attended.reshape(batch, rows, HEADS, HEAD_DIM)
    delta_rows = jnp.sum(
        (grad_attended.astype(jnp.float32) * attended).reshape(batch, rows, HEADS, HEAD_DIM), axis=3
    )
    delta = delta_rows.transpose(0, 2, 1)

    def query_step(carry, pieces, start):
        key_piece, value_piece = pieces
        count = key_piece.shape[1]
        key_pos = start + jnp.arange(count, dtype=jnp.int32)
        key_seg = segment_ids(key_pos, item_ends)

        def query_work(grad_query):
            keys_block = key_piece.reshape(batch, count, HEADS, HEAD_DIM)
            values_block = value_piece.reshape(batch, count, HEADS, HEAD_DIM)
            scores = (
                jnp.einsum(
                    "rqhd,rkhd->rhqk", queries, keys_block, preferred_element_type=jnp.float32
                )
                * factor
            )
            mask = visible(query_pos, query_seg, key_pos, key_seg)[:, None]
            shares = jnp.where(mask, jnp.exp(scores - log_total[..., None]), 0.0)
            grad_shares = jnp.einsum(
                "rqhd,rkhd->rhqk", grad_heads, values_block, preferred_element_type=jnp.float32
            )
            grad_scores = (shares * (grad_shares - delta[..., None])).astype(jnp.bfloat16)
            return grad_query + jnp.einsum(
                "rhqk,rkhd->rhqd", grad_scores, keys_block, preferred_element_type=jnp.float32
            )

        return lax.cond(start <= query_pos[-1], query_work, lambda state: state, carry)

    zero_query = jnp.zeros((batch, HEADS, rows, HEAD_DIM), jnp.float32)
    grad_query = over_blocks(
        zero_query,
        (
            lax.all_gather(key_rows, "sq", axis=1, tiled=True),
            lax.all_gather(value_rows, "sq", axis=1, tiled=True),
        ),
        jnp.int32(0),
        query_step,
        512,
    )

    def key_step(carry, pieces, start):
        query_piece, grad_piece, total_piece, delta_piece = pieces
        count = query_piece.shape[1]
        remote_pos = start + jnp.arange(count, dtype=jnp.int32)
        remote_seg = segment_ids(remote_pos, item_ends)

        def key_work(state):
            grad_key, grad_value = state
            remote_queries = query_piece.reshape(batch, count, HEADS, HEAD_DIM)
            remote_grads = grad_piece.reshape(batch, count, HEADS, HEAD_DIM)
            scores = (
                jnp.einsum(
                    "rqhd,rkhd->rhqk", remote_queries, keys_own, preferred_element_type=jnp.float32
                )
                * factor
            )
            mask = visible(remote_pos, remote_seg, query_pos, query_seg)[:, None]
            shares = jnp.where(
                mask, jnp.exp(scores - total_piece.transpose(0, 2, 1)[..., None]), 0.0
            )
            grad_value = grad_value + jnp.einsum(
                "rhqk,rqhd->rhkd",
                shares.astype(jnp.bfloat16),
                remote_grads,
                preferred_element_type=jnp.float32,
            )
            grad_shares = jnp.einsum(
                "rqhd,rkhd->rhqk", remote_grads, values_own, preferred_element_type=jnp.float32
            )
            grad_scores = (
                shares * (grad_shares - delta_piece.transpose(0, 2, 1)[..., None])
            ).astype(jnp.bfloat16)
            grad_key = grad_key + jnp.einsum(
                "rhqk,rqhd->rhkd", grad_scores, remote_queries, preferred_element_type=jnp.float32
            )
            return (grad_key, grad_value)

        return lax.cond(start + count - 1 >= first, key_work, lambda state: state, carry)

    grad_key, grad_value = over_blocks(
        (zero_query, zero_query),
        (
            lax.all_gather(query_rows, "sq", axis=1, tiled=True),
            lax.all_gather(grad_rows_own, "sq", axis=1, tiled=True),
            lax.all_gather(
                log_total.transpose(0, 2, 1).astype(jnp.bfloat16), "sq", axis=1, tiled=True
            ).astype(jnp.float32),
            lax.all_gather(delta_rows.astype(jnp.bfloat16), "sq", axis=1, tiled=True).astype(
                jnp.float32
            ),
        ),
        jnp.int32(0),
        key_step,
        512,
    )
    grad_mixed = jnp.concatenate(
        [
            heads_flat(grad_query * factor, batch, rows, width),
            heads_flat(grad_key * factor, batch, rows, width),
            heads_flat(grad_value, batch, rows, width),
        ],
        axis=1,
    ).astype(jnp.bfloat16)
    grad_qkv = contract_rows(hidden1_low, grad_mixed)
    grad_hidden1 = times_transpose(grad_mixed, w_qkv)
    grad_frames_part, grad_gain1 = norm1_pull(grad_hidden1)
    grad_frames = (grad_middle + grad_frames_part).reshape(batch, rows, width)
    result_rows = result.astype(jnp.bfloat16).reshape(batch, rows, width)
    shares_sq = (
        lax.psum_scatter(grad_gain1, "sq", scatter_dimension=0, tiled=True),
        lax.psum_scatter(grad_qkv, "sq", scatter_dimension=0, tiled=True),
        lax.psum_scatter(grad_outproj, "sq", scatter_dimension=0, tiled=True),
        lax.psum_scatter(grad_gain2, "sq", scatter_dimension=0, tiled=True),
        lax.psum_scatter(grad_up, "sq", scatter_dimension=0, tiled=True),
        lax.psum_scatter(grad_down, "sq", scatter_dimension=0, tiled=True),
    )
    totals = (
        lax.psum(shares_sq[0].astype(jnp.bfloat16), "dp").astype(jnp.float32),
        lax.psum(shares_sq[1].astype(jnp.bfloat16), "dp").astype(jnp.float32),
        lax.psum(shares_sq[2].astype(jnp.bfloat16), "dp").astype(jnp.float32),
        lax.psum(shares_sq[3].astype(jnp.bfloat16), "dp").astype(jnp.float32),
        lax.psum(shares_sq[4].astype(jnp.bfloat16), "dp").astype(jnp.float32),
        lax.psum(shares_sq[5].astype(jnp.bfloat16), "dp").astype(jnp.float32),
    )
    return (
        result_rows,
        grad_frames,
        totals[0],
        totals[1],
        totals[2],
        totals[3],
        totals[4],
        totals[5],
    )


def solution(mesh):
    return jax.shard_map(
        shards,
        mesh=mesh,
        in_specs=(
            P("dp", "sq", None),
            P(),
            P(),
            P(),
            P(),
            P(),
            P(),
            P("dp", None),
            P("dp", "sq", None),
        ),
        out_specs=(
            P("dp", "sq", None),
            P("dp", "sq", None),
            P("sq"),
            P("sq", None),
            P("sq", None),
            P("sq"),
            P("sq", None),
            P("sq", None),
        ),
        check_vma=False,
    )
```

profile of v0, /device:TPU:0, one launch (start us, length us, event | category | flops | bytes accessed | tf_op | source)
XLA Modules:
  0.0 698.9 jit_solution(101815978232163255)
XLA Ops:
  18.7 26.0 %all-gather.9.cloned.1.call-done = bf16[1024,1024]{1,0:T(8,128)(2,1)} async-done(((bf16[128,1024]{1,0:T(8,128)(2,1)}), bf16[1024,1024]{1,0:T(8,128)(2,1)}) %all-gather.9.cloned.1.call-update) | async-done | bytes 2097168 | tf_op jit(solution)/shard_map/all_gather | solution.py:133
  48.6 26.5 %all-gather.11.cloned.1.call-done = bf16[1024,1024]{1,0:T(8,128)(2,1)} async-done(((bf16[128,1024]{1,0:T(8,128)(2,1)}), bf16[1024,1024]{1,0:T(8,128)(2,1)}) %all-gather.11.cloned.1.call-update) | async-done | bytes 2097168 | tf_op jit(solution)/shard_map/all_gather | solution.py:134
  79.1 13.9 %while.45 = (s32[]{:T(128)}, f32[1,16,128]{2,1,0:T(8,128)S(1)}, f32[1,16,128]{2,1,0:T(8,128)S(1)}, f32[1,16,128,64]{2,3,1,0:T(8,128)S(1)}, s32[2]{0:T(128)S(1)},...) while((s32[]{:T(128)}, f32[1,16,128]{2,1,0:T(8,128)S(1)}, ...), condition=%wide.region_9.10_spmd, body=%wide.region_3.9_spmd.sunk | while | flops 282544640 | bytes 20628860 | solution.py:54
  83.0 6.1 conditional.8
  103.2 7.7 %fusion.60 = bf16[128,4096]{1,0:T(8,128)(2,1)S(1)} fusion(f32[128,4096]{1,0:T(8,128)S(1)} %fusion.92, bf16[4096,1024]{1,0:T(8,128)(2,1)} %param.27, bf16[1,128,1024]{2,1,0:T(8,128)(2,1)S(1)} %copy-done.18), kind=kOutput, calls=%fused_computation.80 | convolution fusion | flops 1084227584 | bytes 11796480 | tf_op jit(solution)/shard_map/dot_general | solution.py:64
  129.7 15.0 %all_gather.25 = bf16[1,1024,16]{1,2,0:T(8,128)(2,1)S(1)} all-gather(bf16[1,128,16]{1,2,0:T(8,128)(2,1)S(1)} %bitcast_convert_fusion), channel_id=1, replica_groups=mesh['dp'=4,'sq'=8] {'sq'}, dimensions={1}, use_global_device_ids=true | all-gather | bytes 36864 | tf_op jit(solution)/shard_map/all_gather | solution.py:255
  145.3 8.0 %all_gather.23 = bf16[1,1024,16]{1,2,0:T(8,128)(2,1)S(1)} all-gather(bf16[1,128,16]{1,2,0:T(8,128)(2,1)S(1)} %get-tuple-element.1073), channel_id=1, replica_groups=mesh['dp'=4,'sq'=8] {'sq'}, dimensions={1}, use_global_device_ids=true | all-gather | bytes 36864 | tf_op jit(solution)/shard_map/all_gather | solution.py:252
  155.3 20.4 %while.46 = (s32[]{:T(128)}, f32[1,16,128,64]{2,3,1,0:T(8,128)}, s32[2]{0:T(128)}, s32[128]{0:T(128)}, s32[1,8]{1,0:T(1,128)}, /*index=5*/s32[1,128]{1,0:T(1,128...) while((s32[]{:T(128)}, f32[1,16,128,64]{2,3,1,0:T(8,128)}, ...), condition=%wide.region_17.18_spmd, body=%wide.region_13.17_spmd.sunk | while | flops 409285120 | bytes 17499484 | solution.py:54
  159.7 11.6 %conditional.9 = (f32[1,16,128,64]{2,3,1,0:T(8,128)}) conditional(s32[]{:T(128)} %convert_element_type.291, f32[1,16,128,64]{2,3,1,0:T(8,128)} %get-tuple-element.1437, (s32[]{:T(128)}, s32[512]{0:T(512)S(1)}, s32[128]{0:T(128)}, s32[1,512,8]{1,2,0:T(8,128)S(1)}, s32[1,128]{1,0:T(1,128)}, /*index=5*/bf16[2,1,512,1024]{2,3,1,0:T(8,128)(2,1)}, ...), branch_computations={%region_14.14_spmd, %region_15.16_spmd} | conditional | flops 409276416 | bytes 17476628 | solution.py:194
  182.4 36.2 %while.47 = (s32[]{:T(128)}, f32[1,16,128,64]{2,3,1,0:T(8,128)S(1)}, f32[1,16,128,64]{2,3,1,0:T(8,128)}, s32[2]{0:T(128)S(1)}, s32[]{:T(128)}, /*index=5*/s32[1,...) while((s32[]{:T(128)}, ...), condition=%wide.region_22.23_spmd.clone.clone, body=%wide.region_18.22_spmd.clone.clone.sunk | while | flops 547828352 | bytes 28265440 | solution.py:54
  184.5 16.3 %conditional.10 = ((f32[1,16,128,64]{2,3,1,0:T(8,128)S(1)}, f32[1,16,128,64]{2,3,1,0:T(8,128)})) conditional(s32[]{:T(128)} %convert_element_type.293, (f32[1,16,128,64]{2,3,1,0:T(8,128)S(1)}, f32[1,16,128,64]{2,3,1,0:T(8,128)}) %tuple.150, (s32[]{:T(128)}, s32[]{:T(128)}, s32[512]{0:T(512)S(1)}, s32[1,128]{1,0:T(1,128)S(1)}, ...), branch_computations={%region_19.19_spmd, %region_20.21_spmd} | conditional | flops 547819648 | bytes 28242020 | solution.py:245
  190.0 6.2 fusion.42
  202.8 15.9 %conditional.10 = ((f32[1,16,128,64]{2,3,1,0:T(8,128)S(1)}, f32[1,16,128,64]{2,3,1,0:T(8,128)})) conditional(s32[]{:T(128)} %convert_element_type.293, (f32[1,16,128,64]{2,3,1,0:T(8,128)S(1)}, f32[1,16,128,64]{2,3,1,0:T(8,128)}) %tuple.150, (s32[]{:T(128)}, s32[]{:T(128)}, s32[512]{0:T(512)S(1)}, s32[1,128]{1,0:T(1,128)S(1)}, ...), branch_computations={%region_19.19_spmd, %region_20.21_spmd} | conditional | flops 547819648 | bytes 28242020 | solution.py:245
  208.3 6.2 fusion.42
  219.8 7.5 %fusion.72 = f32[1024,3072]{1,0:T(8,128)} fusion(bf16[128,1024]{0,1:T(8,128)(2,1)S(1)} %bitcast.228, bf16[128,1024]{0,1:T(8,128)(2,1)S(1)} %bitcast.230, bf16[128,1024]{0,1:T(8,128)(2,1)} %bitcast.226, bf16[1,128,1024]{2,1,0:T(8,128)(2,1)S(1)} %copy-done.4, f32[1024]{0:T(1024)S(1)} %copy-done.30, f32[128]{0:T(128)S(1)} %copy-done.38), kind=kOutput, calls=%fused_computation.111 | convolution fusion | flops 808189952 | bytes 13636096 | tf_op jit(solution)/shard_map/dot_general | solution.py:58
  228.5 11.2 %fusion.91 = f32[1024,4096]{1,0:T(8,128)} fusion(bf16[128,4096]{1,0:T(8,128)(2,1)S(1)} %copy-done.9, f32[128,1024]{1,0:T(8,128)S(1)} %get-tuple-element.1089, f32[1024]{0:T(1024)S(1)} %copy-done.29, f32[128]{0:T(128)S(1)} %copy-done.35), kind=kOutput, calls=%fused_computation.140 | convolution fusion | flops 1074135040 | bytes 18354688 | tf_op jit(solution)/shard_map/dot_general | solution.py:58
  241.9 8.9 %fusion.74 = f32[4096,1024]{1,0:T(8,128)} fusion(bf16[1,128,1024]{2,1,0:T(8,128)(2,1)S(1)} %copy-done.19, f32[128,4096]{1,0:T(8,128)S(1)} %copy-done.3), kind=kOutput, calls=%fused_computation.113 | convolution fusion | flops 1078460416 | bytes 19136512 | tf_op jit(solution)/shard_map/dot_general | solution.py:58
  252.8 67.5 %reduce-scatter.5.cloned.1.call-done = f32[128,3072]{1,0:T(8,128)} async-done(((f32[1024,3072]{1,0:T(8,128)}), f32[128,3072]{1,0:T(8,128)}) %reduce-scatter.5.cloned.1.call-update) | async-done | bytes 1572880 | tf_op jit(solution)/shard_map/reduce_scatter | solution.py:278
  322.6 117.6 %reduce-scatter.9.cloned.1.call-done = f32[128,4096]{1,0:T(8,128)} async-done(((f32[1024,4096]{1,0:T(8,128)}), f32[128,4096]{1,0:T(8,128)}) %reduce-scatter.9.cloned.1.call-update) | async-done | bytes 2097168 | tf_op jit(solution)/shard_map/reduce_scatter | solution.py:281
  442.9 117.3 %reduce-scatter.11.cloned.1.call-done = f32[512,1024]{1,0:T(8,128)} async-done(((f32[4096,1024]{1,0:T(8,128)}), f32[512,1024]{1,0:T(8,128)}) %reduce-scatter.11.cloned.1.call-update) | async-done | bytes 2097168 | tf_op jit(solution)/shard_map/reduce_scatter | solution.py:282
  564.8 5.7 fusion.62
  575.8 13.8 %all-reduce.2 = (bf16[1024]{0:T(1024)(128)(2,1)S(1)}, bf16[1024]{0:T(1024)(128)(2,1)S(1)}) all-reduce(f32[1024]{0:T(1024)S(1)} %get-tuple-element.989, f32[1024]{0:T(1024)S(1)} %copy-done.36), channel_id=6, replica_groups=mesh['dp'=4,'sq'=8] {'sq'}, use_global_device_ids=true, to_apply=%region_25.26.clone | all-reduce | flops 2048 | bytes 12288
  589.8 12.4 %all-reduce.3 = (bf16[128]{0:T(256)(128)(2,1)S(1)}, bf16[128]{0:T(256)(128)(2,1)S(1)}) all-reduce(bf16[128]{0:T(256)(128)(2,1)S(1)} %dynamic-slice.7, bf16[128]{0:T(256)(128)(2,1)S(1)} %dynamic-slice.6), channel_id=1, replica_groups=mesh['dp'=4,'sq'=8] {'dp'}, use_global_device_ids=true, to_apply=%region_26.27 | all-reduce | flops 256 | bytes 1024 | tf_op jit(solution)/shard_map/psum | solution.py:285
  604.2 81.7 %all-reduce.7.cloned.1.call-done = (bf16[128,3072]{1,0:T(8,128)(2,1)}, bf16[128,1024]{1,0:T(8,128)(2,1)}, bf16[128,4096]{1,0:T(8,128)(2,1)}, bf16[512,1024]{1,0:T(8,128)(2,1)}) async-done(((bf16[128,3072]{1,0:T(8,128)(2,1)}, bf16[128,1024]{1,0:T(8,128)(2,1)}, bf16[128,4096]{1,0:T(8,128)(2,1)}, bf16[512,1024]{1,0:T(8,128)(2,1)}), (bf16[128,3072]{1,0:T(8,128)(2,1)}, bf16[128,1024]{1,0:T(8,128)(2,1)}, ...) | async-done | bytes 3145744 | tf_op jit(solution)/shard_map/psum | solution.py:286
  (242 shorter events, 138.3 us)
Async XLA Ops:
  7.2 89.5 %copy-start = (bf16[1024,1024]{1,0:T(8,128)(2,1)S(1)}, bf16[1024,1024]{1,0:T(8,128)(2,1)}, u32[]{:S(2)}) copy-start(bf16[1024,1024]{1,0:T(8,128)(2,1)} %param.24) | copy-start | bytes 6291460
  7.2 37.5 %all-gather.9.cloned.1.call-start = ((), (), s32[]{:S(2)}) async-start(), calls=%async_computation.8 | async-start | bytes 2359296 | tf_op jit(solution)/shard_map/all_gather | solution.py:133
  14.0 61.1 %all-gather.11.cloned.1.call-start = ((), (), s32[]{:S(2)}) async-start(), calls=%async_computation.9 | async-start | bytes 2359296 | tf_op jit(solution)/shard_map/all_gather | solution.py:134
  14.7 109.4 %all-gather.13.cloned.1.call-start = ((), (), s32[]{:S(2)}) async-start(), calls=%async_computation.10 | async-start | bytes 2359296 | tf_op jit(solution)/shard_map/all_gather | solution.py:250
  15.4 162.1 %all-gather.15.cloned.1.call-start = ((), (), s32[]{:S(2)}) async-start(), calls=%async_computation.11 | async-start | bytes 2359296 | tf_op jit(solution)/shard_map/all_gather | solution.py:251
  98.2 16.3 %copy-start.34 = (f32[128]{0:T(128)}, f32[128]{0:T(128)S(1)}, u32[]{:S(2)}) copy-start(f32[128]{0:T(128)S(1)} %fusion.88) | copy-start | bytes 1540
  98.3 12.7 %slice-start = ((s8[8388608]{0:T(1024)(128)(4,1)}), s8[4194304]{0:T(1024)(128)(4,1)S(1)}, s32[]{:S(2)}) async-start(s8[8388608]{0:T(1024)(128)(4,1)} %bitcast.209), calls=%async_computation.13 | async-start | bytes 8388608
  103.2 7.8 %copy-start.2 = (f32[128,4096]{1,0:T(8,128)}, f32[128,4096]{1,0:T(8,128)S(1)}, u32[]{:S(2)}) copy-start(f32[128,4096]{1,0:T(8,128)S(1)} %fusion.92) | copy-start | bytes 6291460
  103.2 7.8 %slice-start.1 = ((s8[8388608]{0:T(1024)(128)(4,1)}), s8[4194304]{0:T(1024)(128)(4,1)S(1)}, s32[]{:S(2)}) async-start(s8[8388608]{0:T(1024)(128)(4,1)} %bitcast.209), calls=%async_computation.14 | async-start | bytes 8388608
  117.3 133.6 %reduce-scatter.7.cloned.1.call-start = ((), (), s32[]{:S(2)}) async-start(), calls=%async_computation.5 | async-start | bytes 4718592 | tf_op jit(solution)/shard_map/reduce_scatter | solution.py:279
  121.3 198.9 %reduce-scatter.5.cloned.1.call-start = ((), (), s32[]{:S(2)}) async-start(), calls=%async_computation.4 | async-start | bytes 14155776 | tf_op jit(solution)/shard_map/reduce_scatter | solution.py:278
  182.4 37.4 %copy-start.30 = (f32[1024]{0:T(1024)S(1)}, f32[1024]{0:T(1024)}, u32[]{:S(2)}) copy-start(f32[1024]{0:T(1024)} %param.22) | copy-start | bytes 12292
  182.4 37.4 %copy-start.38 = (f32[128]{0:T(128)S(1)}, f32[128]{0:T(128)}, u32[]{:S(2)}) copy-start(f32[128]{0:T(128)} %copy-done.37) | copy-start | bytes 1540
  219.7 7.6 %copy-start.23 = (bf16[1,16,128,64]{2,3,1,0:T(8,128)(2,1)}, bf16[1,16,128,64]{2,3,1,0:T(8,128)(2,1)S(1)}, u32[]{:S(2)}) copy-start(bf16[1,16,128,64]{2,3,1,0:T(8,128)(2,1)S(1)} %convert.20) | copy-start | bytes 786436
  219.8 7.5 %copy-start.25 = (bf16[1,16,128,64]{2,3,1,0:T(8,128)(2,1)}, bf16[1,16,128,64]{2,3,1,0:T(8,128)(2,1)S(1)}, u32[]{:S(2)}) copy-start(bf16[1,16,128,64]{2,3,1,0:T(8,128)(2,1)S(1)} %multiply_convert_fusion.2) | copy-start | bytes 786436
  227.3 212.8 %reduce-scatter.9.cloned.1.call-start = ((), (), s32[]{:S(2)}) async-start(), calls=%async_computation.6 | async-start | bytes 18874368 | tf_op jit(solution)/shard_map/reduce_scatter | solution.py:281
  239.7 320.4 %reduce-scatter.11.cloned.1.call-start = ((), (), s32[]{:S(2)}) async-start(), calls=%async_computation.7 | async-start | bytes 18874368 | tf_op jit(solution)/shard_map/reduce_scatter | solution.py:282
  250.9 435.0 %all-reduce.7.cloned.1.call-start = ((), (), s32[]{:S(2)}) async-start(), calls=%async_computation.12 | async-start | bytes 6291456 | tf_op jit(solution)/shard_map/psum | solution.py:286
  564.8 5.8 copy-start.22
  564.8 5.8 copy-start.24
  564.8 5.8 copy-start.26
  564.8 5.8 copy-start.39
  570.6 32.6 %copy-start.41 = (f32[128]{0:T(128)S(1)}, f32[128]{0:T(128)}, u32[]{:S(2)}) copy-start(f32[128]{0:T(128)} %copy-done.40) | copy-start | bytes 1540
  570.6 32.6 %copy-start.6 = (f32[128,1024]{1,0:T(8,128)S(1)}, f32[128,1024]{1,0:T(8,128)}, u32[]{:S(2)}) copy-start(f32[128,1024]{1,0:T(8,128)} %copy-done.5) | copy-start | bytes 1572868
  (33 other events, 85.8 us)
Sparse Core Ops, SparseCore 0:
  14.1 30.5 all-gather.8
  47.2 27.8 all-gather.10
  77.0 27.8 all-gather.12
  117.5 34.1 all-gather.14
  154.8 51.3 reduce-scatter.6
  227.5 92.7 reduce-scatter.4
  324.2 115.9 reduce-scatter.8
  444.2 115.9 reduce-scatter.10
  563.5 122.3 all-reduce.6
where the time goes:
time: 700 us; the launch traced here: 699 us
  waiting for transfers between devices  438 us (63%)
  matrix products  103 us (15%)
  local copies, waits for them, and re-layouts  50.6 us (7%)
  blocking collectives  49.2 us (7%)
  other arithmetic  35.8 us (5%)
  between operations  15 us (2%)
    reduce_scatter x1, waiting for transfers between devices, shards(): lax.psum_scatter(grad_up, 'sq', scatter_dimension=0, tiled=True)  118 us
    reduce_scatter x1, waiting for transfers between devices, shards(): lax.psum_scatter(grad_down, 'sq', scatter_dimension=0, tiled=True)  117 us
    psum x1, waiting for transfers between devices, shards(): lax.psum(shares_sq[1].astype(jnp.bfloat16), 'dp').astype(jnp.float32)  81.7 us
    reduce_scatter x1, waiting for transfers between devices, shards(): lax.psum_scatter(grad_qkv, 'sq', scatter_dimension=0, tiled=True)  67.5 us
    dot_general x4, matrix products, contract_rows(): lax.dot_general(left, right, (((0,), (0,)), ((), ())), preferred_element_...  31.4 us
    all_gather x1, waiting for transfers between devices, shards(): lax.all_gather(value_rows, 'sq', axis=1, tiled=True)  26.5 us
    all_gather x1, waiting for transfers between devices, shards(): lax.all_gather(key_rows, 'sq', axis=1, tiled=True)  26 us
    dot_general x4, matrix products, times_transpose(): lax.dot_general(left, right, (((1,), (1,)), ((), ())), preferred_element_...  18.2 us
  transfers between devices with their start and end apart: 9, of which 6 were waited for; matrix products, arithmetic and copies ran while one was open for 24% of the time, Pallas kernels for 0%

commit v1 on v0

--- a/solution.py
+++ b/solution.py
@@ -18,6 +18,12 @@
 
 def segment_ids(positions, item_ends):
     return jnp.sum((positions[None, :, None] >= item_ends[:, None, :]).astype(jnp.int32), axis=2)
+
+
+def running_ends(lengths):
+    items = jnp.arange(lengths.shape[1], dtype=jnp.int32)
+    before = items[None, None, :] <= items[None, :, None]
+    return jnp.sum(jnp.where(before, lengths[:, None, :], 0), axis=2)
 
 
 def visible(query_pos, query_seg, key_pos, key_seg):
@@ -70,14 +76,14 @@
     return values.transpose(0, 2, 1, 3).reshape(batch * rows, width)
 
 
-def shards(frames, norm1_gain, w_qkv, w_out, norm2_gain, w_up, w_down, lengths, cotangent):
+def shards_by_rows(frames, norm1_gain, w_qkv, w_out, norm2_gain, w_up, w_down, lengths, cotangent):
     batch = frames.shape[0]
     rows = frames.shape[1]
     width = frames.shape[2]
     factor = HEAD_DIM ** (-0.5)
     first = lax.axis_index("sq") * rows
     query_pos = first + jnp.arange(rows, dtype=jnp.int32)
-    item_ends = jnp.cumsum(lengths, axis=1)
+    item_ends = running_ends(lengths)
     query_seg = segment_ids(query_pos, item_ends)
     frames_own = frames.reshape(batch * rows, width).astype(jnp.float32)
     hidden1, norm1_pull = jax.vjp(norm_scaled, frames_own, norm1_gain)
@@ -301,9 +307,129 @@
     )
 
 
+def low(values):
+    return values.astype(jnp.bfloat16)
+
+
+def times(left, right):
+    return jnp.dot(left, right, preferred_element_type=jnp.float32)
+
+
+def norm_scale(values):
+    return lax.rsqrt(jnp.mean(values * values, axis=-1, keepdims=True) + EPSILON)
+
+
+def norm_back(values, scale, gain, grad):
+    scaled = gain * grad
+    inner = jnp.mean(scaled * values, axis=-1, keepdims=True)
+    part = scale * scaled - values * (scale * scale * scale) * inner
+    return part, jnp.sum(grad * values * scale, axis=0)
+
+
+def gelu_parts(values):
+    root = 0.7978845608028654
+    inner = jnp.tanh(root * (values + 0.044715 * values * values * values))
+    slope = 0.5 * (1.0 + inner) + 0.5 * values * (1.0 - inner * inner) * root * (
+        1.0 + 3 * 0.044715 * values * values
+    )
+    return 0.5 * values * (1.0 + inner), slope
+
+
+def to_heads(rows_value):
+    return lax.all_to_all(rows_value, "sq", split_axis=1, concat_axis=0, tiled=True)
+
+
+def to_rows(heads_value):
+    return lax.all_to_all(heads_value, "sq", split_axis=0, concat_axis=1, tiled=True)
+
+
+def shards_by_heads(frames, norm1_gain, w_qkv, w_out, norm2_gain, w_up, w_down, lengths, cotangent):
+    _, rows, width = frames.shape
+    ff = w_up.shape[1]
+    count = lax.axis_size("sq")
+    me = lax.axis_index("sq")
+    total = rows * count
+    part = width // count
+    local = part // HEAD_DIM
+    factor = HEAD_DIM ** (-0.5)
+
+    frames_own = frames[0].astype(jnp.float32)
+    frames_all = lax.all_gather(frames[0], "sq", axis=0, tiled=True).astype(jnp.float32)
+    grad_low = cotangent[0]
+    grad_all = lax.all_gather(grad_low, "sq", axis=0, tiled=True)
+    hidden1 = low(frames_all * norm_scale(frames_all) * norm1_gain)
+    w_heads = jnp.concatenate(
+        [lax.dynamic_slice_in_dim(w_qkv, k * width + me * part, part, 1) for k in range(3)], axis=1
+    )
+    mixed = low(times(hidden1, w_heads))
+    queries, keys, values = (
+        mixed[:, k * part : (k + 1) * part].reshape(total, local, HEAD_DIM) for k in range(3)
+    )
+    ends = running_ends(lengths)[0]
+    place = jnp.arange(total, dtype=jnp.int32)
+    begin = jnp.max(jnp.where(ends[None, :] <= place[:, None], ends[None, :], 0), axis=1)
+    mask = (place[None, :] <= place[:, None]) & (place[None, :] >= begin[:, None])
+    scores = jnp.einsum("qhd,khd->hqk", queries, keys, preferred_element_type=jnp.float32) * factor
+    scores = jnp.where(mask[None], scores, NEG_FILL)
+    top = jnp.max(scores, axis=-1, keepdims=True)
+    weights = jnp.exp(scores - top)
+    shares = weights / jnp.sum(weights, axis=-1, keepdims=True)
+    shares_low = low(shares)
+    attended = jnp.einsum("hqk,khd->qhd", shares_low, values, preferred_element_type=jnp.float32)
+    attended_low = low(attended.reshape(total, part))
+    attended_rows = to_rows(attended_low)
+    middle = frames_own + times(attended_rows, w_out)
+    scale2 = norm_scale(middle)
+    hidden2 = low(middle * scale2 * norm2_gain)
+    hidden2_all = lax.all_gather(hidden2, "sq", axis=0, tiled=True)
+
+    active, slope = gelu_parts(times(hidden2, w_up))
+    result = low(middle + times(low(active), w_down))[None]
+    grad_up_own = low(times_transpose(grad_low, w_down) * slope)
+    grad_hidden2 = times_transpose(grad_up_own, w_up)
+    back2, gain2_part = norm_back(middle, scale2, norm2_gain, grad_hidden2)
+    grad_middle = grad_low.astype(jnp.float32) + back2
+    grad_attn = low(grad_middle)
+    grad_attn_all = lax.all_gather(grad_attn, "sq", axis=0, tiled=True)
+    grad_heads = to_heads(low(times_transpose(grad_attn, w_out)))
+
+    grads = grad_heads.reshape(total, local, HEAD_DIM)
+    grad_value = jnp.einsum("hqk,qhd->khd", shares_low, grads, preferred_element_type=jnp.float32)
+    grad_shares = jnp.einsum("qhd,khd->hqk", grads, values, preferred_element_type=jnp.float32)
+    delta = jnp.sum(grads.astype(jnp.float32) * attended, axis=2).T[:, :, None]
+    grad_scores = low(shares * (grad_shares - delta))
+    grad_query = jnp.einsum("hqk,khd->qhd", grad_scores, keys, preferred_element_type=jnp.float32)
+    grad_key = jnp.einsum("hqk,qhd->khd", grad_scores, queries, preferred_element_type=jnp.float32)
+    grad_mixed = [
+        low(member.reshape(total, part))
+        for member in (grad_query * factor, grad_key * factor, grad_value)
+    ]
+    grad_mixed_rows = jnp.concatenate([to_rows(member) for member in grad_mixed], axis=1)
+    grad_hidden1 = times_transpose(grad_mixed_rows, w_qkv)
+    back1, gain1_part = norm_back(frames_own, norm_scale(frames_own), norm1_gain, grad_hidden1)
+    grad_frames = (grad_middle + back1)[None]
+
+    slice_up = lax.dynamic_slice_in_dim(w_up, me * (ff // count), ff // count, 1)
+    slice_down = lax.dynamic_slice_in_dim(w_down, me * (ff // count), ff // count, 0)
+    active_part, slope_part = gelu_parts(times(hidden2_all, slice_up))
+    grad_down = low(contract_rows(low(active_part), grad_all))
+    grad_up_part = low(times_transpose(grad_all, slice_down) * slope_part)
+    grad_up = to_rows(low(contract_rows(hidden2_all, grad_up_part)))
+    grad_out = low(contract_rows(attended_low, grad_attn_all))
+    grad_qkv = jnp.concatenate(
+        [to_rows(low(contract_rows(hidden1, member))) for member in grad_mixed], axis=1
+    )
+    gains = lax.psum_scatter(jnp.stack([gain1_part, gain2_part]), "sq", scatter_dimension=1, tiled=True)
+    gains = lax.psum(gains, "dp")
+    sums = lax.psum((grad_qkv, grad_out, grad_up, grad_down), "dp")
+    grad_qkv, grad_out, grad_up, grad_down = (member.astype(jnp.float32) for member in sums)
+    return (result, grad_frames, gains[0], grad_qkv, grad_out, gains[1], grad_up, grad_down)
+
+
 def solution(mesh):
+    by_heads = HEADS % mesh.shape["sq"] == 0
     return jax.shard_map(
-        shards,
+        shards_by_heads if by_heads else shards_by_rows,
         mesh=mesh,
         in_specs=(
             P("dp", "sq", None),

time: 700 us -> 349 us (0.50)
  waiting for transfers between devices: 438 us -> 167 us
  local copies, waits for them, and re-layouts: 50.6 us -> 13.1 us
  starting transfers between devices: 0.63 us -> 30.1 us
  blocking collectives: 49.2 us -> 21.2 us
  matrix products: 103 us -> 78.6 us
  other arithmetic: 35.8 us -> 22.4 us
    reduce_scatter x4 -> x0, waiting for transfers between devices: 302 us -> none  [the longest x1 118 us: shards(): lax.psum_scatter(grad_up, 'sq', scatter_dimension=0, tiled=True)]
    all_to_all x0 -> x8, waiting for transfers between devices: none -> 37.3 us  [the longest x7 31.6 us: to_rows(): lax.all_to_all(heads_value, 'sq', split_axis=0, concat_axis=1, tiled=True)]
    all_to_all x0 -> x8, starting transfers between devices: none -> 29.7 us  [the longest x7 26.3 us: to_rows(): lax.all_to_all(heads_value, 'sq', split_axis=0, concat_axis=1, tiled=True)]
    dot_general x14 -> x10, matrix products: 53.6 us -> 29.9 us  [the longest x5 18.1 us: times(): return jnp.dot(left, right, preferred_element_type=jnp.float32)]
    all_gather x4, waiting for transfers between devices: 52.5 us -> 29 us  [the longest x1 29 us: shards_by_heads(): lax.all_gather(frames[0], 'sq', axis=0, tiled=True).astype(jnp.float32)]
    all_gather x2 -> x0, blocking collectives: 23 us -> none  [the longest x1 15 us: shards(): lax.all_gather(delta_rows.astype(jnp.bfloat16), 'sq', axis=1, tiled=True)]
    psum x1, waiting for transfers between devices: 81.7 us -> 99.8 us  [shards_by_heads(): sums = lax.psum((grad_qkv, grad_out, grad_up, grad_down), 'dp')]
    unnamed x1 -> x0, blocking collectives: 13.8 us -> none
  transfers between devices with their start and end apart: 9 -> 14, of which waited for: 6 -> 9; matrix products, arithmetic and copies ran while one was open for 24% -> 25% of each run, Pallas kernels for 0% -> 0%
where the time goes in v1:
time: 349 us; the launch traced here: 347 us
  waiting for transfers between devices  167 us (48%)
  matrix products  78.6 us (23%)
  starting transfers between devices  30.1 us (9%)
  other arithmetic  22.4 us (6%)
  blocking collectives  21.2 us (6%)
  between operations  14.6 us (4%)
  local copies, waits for them, and re-layouts  13.1 us (4%)
    psum x1, waiting for transfers between devices, shards_by_heads(): sums = lax.psum((grad_qkv, grad_out, grad_up, grad_down), 'dp')  99.8 us
    all_to_all x7, waiting for transfers between devices, to_rows(): lax.all_to_all(heads_value, 'sq', split_axis=0, concat_axis=1, tiled=True)  31.6 us
    all_gather x1, waiting for transfers between devices, shards_by_heads(): lax.all_gather(frames[0], 'sq', axis=0, tiled=True).astype(jnp.float32)  29 us
    all_to_all x7, starting transfers between devices, to_rows(): lax.all_to_all(heads_value, 'sq', split_axis=0, concat_axis=1, tiled=True)  26.3 us
    dot_general x3, matrix products, times_transpose(): lax.dot_general(left, right, (((1,), (1,)), ((), ())), preferred_element_...  22 us
    dot_general x6, matrix products, contract_rows(): lax.dot_general(left, right, (((0,), (0,)), ((), ())), preferred_element_...  19.8 us
    dot_general x5, matrix products, times(): return jnp.dot(left, right, preferred_element_type=jnp.float32)  18.1 us
    psum x1, blocking collectives, shards_by_heads(): gains = lax.psum(gains, 'dp')  11.7 us
  transfers between devices with their start and end apart: 14, of which 9 were waited for; matrix products, arithmetic and copies ran while one was open for 25% of the time, Pallas kernels for 0%

profile of v1, /device:TPU:0, one launch (start us, length us, event | category | flops | bytes accessed | tf_op | source)
XLA Modules:
  0.0 347.3 jit_solution(408343173221921654)
XLA Ops:
  11.6 29.0 %all-gather.11.cloned.1.call-done = bf16[1,1024,1024]{2,1,0:T(8,128)(2,1)} async-done(((bf16[1,128,1024]{2,1,0:T(8,128)(2,1)}), bf16[1,1024,1024]{2,1,0:T(8,128)(2,1)}) %all-gather.11.cloned.1.call-update) | async-done | bytes 2097168 | tf_op jit(solution)/shard_map/all_gather | solution.py:357
  44.7 7.0 %fusion.102 = (f32[2,1024]{1,0:T(2,128)S(1)}, f32[2,1024,1024]{1,2,0:T(8,128)}) fusion(pred[1024,1024]{0,1:T(8,128)(4,1)} %fusion.8, bf16[1024,2,64]{0,2,1:T(8,128)(2,1)S(1)} %bitcast.175, bf16[1024,2,64]{0,2,1:T(8,128)(2,1)S(1)} %bitcast.169), kind=kOutput, calls=%fused_computation.150 | convolution fusion | flops 276825088 | bytes 9969664 | tf_op jit(solution)/shard_map/sub | solution.py:375
  51.7 4.6 %fusion.10 = bf16[2,1024,1024]{1,2,0:T(8,128)(2,1)S(1)} fusion(f32[2,1024,1024]{1,2,0:T(8,128)} %get-tuple-element.31, f32[2,1024]{1,0:T(2,128)S(1)} %get-tuple-element.30), kind=kLoop, calls=%fused_computation.19 | loop fusion | flops 4194304 | bytes 12591104 | tf_op jit(solution)/shard_map/convert_element_type | solution.py:311
  58.5 9.5 %all_to_all.156 = bf16[8,128,128]{1,2,0:T(8,128)(2,1)S(1)} all-to-all(bf16[8,128,128]{1,2,0:T(8,128)(2,1)S(1)} %copy.64), channel_id=1, replica_groups=mesh['dp'=4,'sq'=8] {'sq'}, dimensions={0} | all-to-all | bytes 524288 | tf_op jit(solution)/shard_map/all_to_all | solution.py:343
  70.1 6.1 %fusion.106 = f32[128,4096]{1,0:T(8,128)} fusion(bf16[128,1024]{1,0:T(8,128)(2,1)} %multiply_convert_fusion.5, bf16[1024,4096]{1,0:T(8,128)(2,1)} %param.14), kind=kOutput, calls=%fused_computation.152 | convolution fusion | flops 1073741824 | bytes 10747904 | tf_op jit(solution)/shard_map/dot_general | solution.py:315
  76.2 13.3 %multiply_reduce_fusion = (f32[1024]{0:T(1024)S(1)}, f32[128]{0:T(128)S(1)}, f32[128,1024]{1,0:T(8,128)}) fusion(f32[128,1024]{1,0:T(8,128)S(1)} %get-tuple-element.35, f32[128]{0:T(128)S(1)} %get-tuple-element.29, f32[1024]{0:T(1024)S(1)} %copy-done.24, bf16[1024,4096]{1,0:T(8,128)(2,1)} %param.14, bf16[4096,1024]{1,0:T(8,128)(2,1)} %param.15, ...), kind=kOutput, calls=%fused_computation.97 | convolution fusion | flops 2158230528 | bytes 20194304 | tf_op jit(solution)/shard_map/dot_general | solution.py:70
  100.6 5.7 %all-to-all-done.1 = bf16[128,8,128]{0,2,1:T(8,128)(2,1)S(1)} async-done(((bf16[128,8,128]{0,2,1:T(8,128)(2,1)}), bf16[128,8,128]{0,2,1:T(8,128)(2,1)S(1)}, u32[]{:S(2)}, u32[]{:S(2)}) %all-to-all-start.1) | async-done | bytes 262176 | tf_op jit(solution)/shard_map/all_to_all | solution.py:339
  111.0 4.3 %all-to-all-start.4 = ((bf16[8,128,128]{1,2,0:T(8,128)(2,1)}), bf16[8,128,128]{1,2,0:T(8,128)(2,1)}, u32[]{:S(2)}, u32[]{:S(2)}) async-start(bf16[8,128,128]{1,2,0:T(8,128)(2,1)} %copy.73), calls=%async_computation.4 | async-start | bytes 524288 | tf_op jit(solution)/shard_map/all_to_all | solution.py:343
  115.4 5.1 %multiply_convert_fusion = bf16[2,1024,1024]{1,2,0:T(8,128)(2,1)S(1)} fusion(f32[2,1024]{1,0:T(2,128)S(1)} %bitcast.185, f32[2,1024,1024]{1,2,0:T(8,128)} %get-tuple-element.31, f32[2,1024]{1,0:T(2,128)S(1)} %get-tuple-element.30, bf16[1024,2,64]{0,2,1:T(8,128)(2,1)S(1)} %reshape.207, bf16[1024,2,64]{0,2,1:T(8,128)(2,1)S(1)} %bitcast.172), kind=kOutput, calls=%fused_computation.1 | convolution fusion | flops 276824064 | bytes 13123584 | tf_op jit(solution)/shard_map/qhd,khd->hqk/dot_general | solution.py:398
  126.5 3.9 %all-to-all-start.3 = ((bf16[8,128,128]{1,2,0:T(8,128)(2,1)}), bf16[8,128,128]{1,2,0:T(8,128)(2,1)S(1)}, u32[]{:S(2)}, u32[]{:S(2)}) async-start(bf16[8,128,128]{1,2,0:T(8,128)(2,1)} %copy.71), calls=%async_computation.3 | async-start | bytes 524288 | tf_op jit(solution)/shard_map/all_to_all | solution.py:343
  132.8 4.5 %all-to-all-done.3 = bf16[8,128,128]{1,2,0:T(8,128)(2,1)S(1)} async-done(((bf16[8,128,128]{1,2,0:T(8,128)(2,1)}), bf16[8,128,128]{1,2,0:T(8,128)(2,1)S(1)}, u32[]{:S(2)}, u32[]{:S(2)}) %all-to-all-start.3) | async-done | bytes 262176 | tf_op jit(solution)/shard_map/all_to_all | solution.py:343
  137.3 4.1 %all-to-all-start.2 = ((bf16[8,128,128]{1,2,0:T(8,128)(2,1)}), bf16[8,128,128]{1,2,0:T(8,128)(2,1)}, u32[]{:S(2)}, u32[]{:S(2)}) async-start(bf16[8,128,128]{1,2,0:T(8,128)(2,1)} %copy.69), calls=%async_computation.2 | async-start | bytes 524288 | tf_op jit(solution)/shard_map/all_to_all | solution.py:343
  142.8 5.4 %all-to-all-done.2 = bf16[8,128,128]{1,2,0:T(8,128)(2,1)} async-done(((bf16[8,128,128]{1,2,0:T(8,128)(2,1)}), bf16[8,128,128]{1,2,0:T(8,128)(2,1)}, u32[]{:S(2)}, u32[]{:S(2)}) %all-to-all-start.2) | async-done | bytes 262176 | tf_op jit(solution)/shard_map/all_to_all | solution.py:343
  151.8 6.1 %fusion.72 = (f32[1024]{0:T(1024)S(1)}, f32[128]{0:T(128)S(1)}, f32[128,1024]{1,0:T(8,128)}) fusion(bf16[1,128,1024]{2,1,0:T(8,128)(2,1)S(1)} %copy-done.7, f32[128]{0:T(128)S(1)} %get-tuple-element.27, f32[1024]{0:T(1024)S(1)} %copy-done.25, bf16[1024,3072]{1,0:T(8,128)(2,1)} %param.11, bf16[128,1024]{0,1:T(8,128)(2,1)} %bitcast.24, ...), kind=kOutput, calls=%fused_computation.96 | convolution fusion | flops 808582016 | bytes 7873536 | tf_op jit(solution)/shard_map/dot_general | solution.py:70
  163.5 6.8 %all-to-all-done.6 = bf16[8,128,128]{2,1,0:T(8,128)(2,1)S(1)} async-done(((bf16[8,128,128]{2,1,0:T(8,128)(2,1)}), bf16[8,128,128]{2,1,0:T(8,128)(2,1)S(1)}, u32[]{:S(2)}, u32[]{:S(2)}) %all-to-all-start.6) | async-done | bytes 262176 | tf_op jit(solution)/shard_map/all_to_all | solution.py:343
  173.8 6.8 %all-to-all-done.5 = bf16[8,128,128]{2,1,0:T(8,128)(2,1)S(1)} async-done(((bf16[8,128,128]{2,1,0:T(8,128)(2,1)}), bf16[8,128,128]{2,1,0:T(8,128)(2,1)S(1)}, u32[]{:S(2)}, u32[]{:S(2)}) %all-to-all-start.5) | async-done | bytes 262176 | tf_op jit(solution)/shard_map/all_to_all | solution.py:343
  180.7 4.5 %fusion.40 = f32[1024,512]{0,1:T(8,128)} fusion(bf16[1024,1024]{1,0:T(8,128)(2,1)} %all-gather.9.cloned.1.call-done, bf16[1024,4096]{1,0:T(8,128)(2,1)} %param.14, s32[]{:T(128)S(6)} %select_n.39), kind=kOutput, calls=%fused_computation.68 | convolution fusion | flops 1073741824 | bytes 5242884 | tf_op jit(solution)/shard_map/dot_general | solution.py:315
  185.1 7.0 %convolution_convert_fusion = bf16[1024,512]{1,0:T(8,128)(2,1)} fusion(bf16[1024,1024]{1,0:T(8,128)(2,1)} %all-gather.9.cloned.1.call-done, f32[1024,512]{0,1:T(8,128)} %fusion.40, bf16[1,1024,1024]{2,1,0:T(8,128)(2,1)} %all-gather.13.cloned.1.call-done, bf16[4096,1024]{1,0:T(8,128)(2,1)} %param.15, s32[]{:T(128)S(6)} %select_n.39), kind=kOutput, calls=%fused_computation.43 | convolution fusion | flops 2157969408 | bytes 8388612 | tf_op jit(solution)/shard_map/dot_general | solution.py:64
  192.2 3.8 %all-to-all-start.8 = ((bf16[8,128,512]{2,1,0:T(8,128)(2,1)}), bf16[8,128,512]{2,1,0:T(8,128)(2,1)S(1)}, u32[]{:S(2)}, u32[]{:S(2)}) async-start(bf16[8,128,512]{2,1,0:T(8,128)(2,1)} %bitcast.42), calls=%async_computation.8 | async-start | bytes 2097152 | tf_op jit(solution)/shard_map/all_to_all | solution.py:343
  197.0 4.7 %fusion.27 = bf16[512,1024]{1,0:T(8,128)(2,1)} fusion(bf16[1,1024,1024]{2,1,0:T(8,128)(2,1)} %all-gather.13.cloned.1.call-done, f32[1024,512]{0,1:T(8,128)} %fusion.40), kind=kOutput, calls=%fused_computation.42 | convolution fusion | flops 1078984704 | bytes 5242880 | tf_op jit(solution)/shard_map/dot_general | solution.py:64
  204.4 6.9 %all-to-all-done.8 = bf16[8,128,512]{2,1,0:T(8,128)(2,1)S(1)} async-done(((bf16[8,128,512]{2,1,0:T(8,128)(2,1)}), bf16[8,128,512]{2,1,0:T(8,128)(2,1)S(1)}, u32[]{:S(2)}, u32[]{:S(2)}) %all-to-all-start.8) | async-done | bytes 1048608 | tf_op jit(solution)/shard_map/all_to_all | solution.py:343
  214.0 6.0 %fusion.35 = bf16[1,128,1024]{2,1,0:T(8,128)(2,1)} fusion(f32[128,1024]{1,0:T(8,128)S(1)} %get-tuple-element.35, bf16[4096,1024]{1,0:T(8,128)(2,1)} %param.15, f32[128,4096]{1,0:T(8,128)S(1)} %copy-done.15), kind=kOutput, calls=%fused_computation.59 | convolution fusion | flops 1078722560 | bytes 11272192 | tf_op jit(solution)/shard_map/dot_general | solution.py:315
  221.9 11.7 %psum.35 = f32[2,128]{1,0:T(2,128)S(1)} all-reduce(f32[2,128]{1,0:T(2,128)S(1)} %copy.93), channel_id=1, replica_groups=mesh['dp'=4,'sq'=8] {'dp'}, use_global_device_ids=true, to_apply=%region_13.14 | all-reduce | flops 256 | bytes 2048 | tf_op jit(solution)/shard_map/psum | solution.py:423
  234.2 99.8 %all-reduce.3.cloned.1.call-done = (bf16[128,3072]{1,0:T(8,128)(2,1)}, bf16[128,1024]{1,0:T(8,128)(2,1)}, bf16[128,4096]{1,0:T(8,128)(2,1)}, bf16[512,1024]{1,0:T(8,128)(2,1)}) async-done(((bf16[128,3072]{1,0:T(8,128)(2,1)}, bf16[128,1024]{1,0:T(8,128)(2,1)}, bf16[128,4096]{1,0:T(8,128)(2,1)}, bf16[512,1024]{1,0:T(8,128)(2,1)}), (bf16[128,3072]{1,0:T(8,128)(2,1)}, bf16[128,1024]{1,0:T(8,128)(2,1)}, ...) | async-done | bytes 3145744 | tf_op jit(solution)/shard_map/psum | solution.py:424
  (126 shorter events, 66.2 us)
Async XLA Ops:
  7.2 60.8 %copy-start = (bf16[1024,1024]{1,0:T(8,128)(2,1)S(1)}, bf16[1024,1024]{1,0:T(8,128)(2,1)}, u32[]{:S(2)}) copy-start(bf16[1024,1024]{1,0:T(8,128)(2,1)} %param.12) | copy-start | bytes 6291460
  7.2 33.4 %all-gather.11.cloned.1.call-start = ((), (), s32[]{:S(2)}) async-start(), calls=%async_computation.12 | async-start | bytes 2359296 | tf_op jit(solution)/shard_map/all_gather | solution.py:357
  7.9 172.7 %all-gather.9.cloned.1.call-start = ((), (), s32[]{:S(2)}) async-start(), calls=%async_computation.11 | async-start | bytes 2359296 | tf_op jit(solution)/shard_map/all_gather | solution.py:384
  8.8 33.9 %copy-start.25 = (f32[1024]{0:T(1024)S(1)}, f32[1024]{0:T(1024)}, u32[]{:S(2)}) copy-start(f32[1024]{0:T(1024)} %param.10) | copy-start | bytes 12292
  44.7 7.0 %copy-start.11 = (bf16[1024,128]{0,1:T(8,128)(2,1)}, bf16[1024,128]{0,1:T(8,128)(2,1)S(1)}, u32[]{:S(2)}) copy-start(bf16[1024,128]{0,1:T(8,128)(2,1)S(1)} %get-tuple-element.21) | copy-start | bytes 786436
  44.7 7.0 %copy-start.19 = (bf16[1024,128]{0,1:T(8,128)(2,1)}, bf16[1024,128]{0,1:T(8,128)(2,1)S(1)}, u32[]{:S(2)}) copy-start(bf16[1024,128]{0,1:T(8,128)(2,1)S(1)} %get-tuple-element.22) | copy-start | bytes 786436
  44.7 11.7 %copy-start.13 = (bf16[1024,128]{0,1:T(8,128)(2,1)}, bf16[1024,128]{0,1:T(8,128)(2,1)S(1)}, u32[]{:S(2)}) copy-start(bf16[1024,128]{0,1:T(8,128)(2,1)S(1)} %get-tuple-element.23) | copy-start | bytes 786436
  56.4 11.6 %copy-start.6 = (bf16[1,128,1024]{2,1,0:T(8,128)(2,1)S(1)}, bf16[1,128,1024]{2,1,0:T(8,128)(2,1)}, u32[]{:S(2)}) copy-start(bf16[1,128,1024]{2,1,0:T(8,128)(2,1)} %param.9) | copy-start | bytes 786436
  58.4 10.1 %copy-start.24 = (f32[1024]{0:T(1024)S(1)}, f32[1024]{0:T(1024)}, u32[]{:S(2)}) copy-start(f32[1024]{0:T(1024)} %param.13) | copy-start | bytes 12292
  69.4 115.8 %all-gather.13.cloned.1.call-start = ((), (), s32[]{:S(2)}) async-start(), calls=%async_computation.13 | async-start | bytes 2359296 | tf_op jit(solution)/shard_map/all_gather | solution.py:359
  96.0 10.3 %all-to-all-start.1 = ((bf16[128,8,128]{0,2,1:T(8,128)(2,1)}), bf16[128,8,128]{0,2,1:T(8,128)(2,1)S(1)}, u32[]{:S(2)}, u32[]{:S(2)}) async-start(bf16[128,8,128]{0,2,1:T(8,128)(2,1)} %bitcast.13), calls=%async_computation.1 | async-start | bytes 524288 | tf_op jit(solution)/shard_map/all_to_all | solution.py:339
  99.4 102.2 %all-gather.7.cloned.1.call-start = ((), (), s32[]{:S(2)}) async-start(), calls=%async_computation.10 | async-start | bytes 2359296 | tf_op jit(solution)/shard_map/all_gather | solution.py:393
  110.2 10.3 %copy-start.8 = (bf16[2,64,1024]{2,1,0:T(8,128)(2,1)}, bf16[2,64,1024]{2,1,0:T(8,128)(2,1)S(1)}, u32[]{:S(2)}) copy-start(bf16[2,64,1024]{2,1,0:T(8,128)(2,1)S(1)} %convolution_convert_fusion.6) | copy-start | bytes 786436
  111.0 15.5 %all-to-all-start.4 = ((bf16[8,128,128]{1,2,0:T(8,128)(2,1)}), bf16[8,128,128]{1,2,0:T(8,128)(2,1)}, u32[]{:S(2)}, u32[]{:S(2)}) async-start(bf16[8,128,128]{1,2,0:T(8,128)(2,1)} %copy.73), calls=%async_computation.4 | async-start | bytes 524288 | tf_op jit(solution)/shard_map/all_to_all | solution.py:343
  126.5 10.8 %all-to-all-start.3 = ((bf16[8,128,128]{1,2,0:T(8,128)(2,1)}), bf16[8,128,128]{1,2,0:T(8,128)(2,1)S(1)}, u32[]{:S(2)}, u32[]{:S(2)}) async-start(bf16[8,128,128]{1,2,0:T(8,128)(2,1)} %copy.71), calls=%async_computation.3 | async-start | bytes 524288 | tf_op jit(solution)/shard_map/all_to_all | solution.py:343
  137.3 11.0 %all-to-all-start.2 = ((bf16[8,128,128]{1,2,0:T(8,128)(2,1)}), bf16[8,128,128]{1,2,0:T(8,128)(2,1)}, u32[]{:S(2)}, u32[]{:S(2)}) async-start(bf16[8,128,128]{1,2,0:T(8,128)(2,1)} %copy.69), calls=%async_computation.2 | async-start | bytes 524288 | tf_op jit(solution)/shard_map/all_to_all | solution.py:343
  141.4 10.4 %copy-start.7 = (bf16[1,128,1024]{2,1,0:T(8,128)(2,1)S(1)}, bf16[1,128,1024]{2,1,0:T(8,128)(2,1)}, u32[]{:S(2)}) copy-start(bf16[1,128,1024]{2,1,0:T(8,128)(2,1)} %param.9) | copy-start | bytes 786436
  148.3 11.7 %all-to-all-start.7 = ((bf16[8,128,128]{2,1,0:T(8,128)(2,1)}), bf16[8,128,128]{2,1,0:T(8,128)(2,1)S(1)}, u32[]{:S(2)}, u32[]{:S(2)}) async-start(bf16[8,128,128]{2,1,0:T(8,128)(2,1)} %bitcast.174), calls=%async_computation.7 | async-start | bytes 524288 | tf_op jit(solution)/shard_map/all_to_all | solution.py:343
  151.7 69.3 %reduce-scatter.4.cloned.1.call-start = ((), (), s32[]{:S(2)}) async-start(), calls=%async_computation.14 | async-start | bytes 589824
  160.0 10.3 %all-to-all-start.6 = ((bf16[8,128,128]{2,1,0:T(8,128)(2,1)}), bf16[8,128,128]{2,1,0:T(8,128)(2,1)S(1)}, u32[]{:S(2)}, u32[]{:S(2)}) async-start(bf16[8,128,128]{2,1,0:T(8,128)(2,1)} %bitcast.33), calls=%async_computation.6 | async-start | bytes 524288 | tf_op jit(solution)/shard_map/all_to_all | solution.py:343
  170.3 10.3 %all-to-all-start.5 = ((bf16[8,128,128]{2,1,0:T(8,128)(2,1)}), bf16[8,128,128]{2,1,0:T(8,128)(2,1)S(1)}, u32[]{:S(2)}, u32[]{:S(2)}) async-start(bf16[8,128,128]{2,1,0:T(8,128)(2,1)} %bitcast.30), calls=%async_computation.5 | async-start | bytes 524288 | tf_op jit(solution)/shard_map/all_to_all | solution.py:343
  192.2 19.2 %all-to-all-start.8 = ((bf16[8,128,512]{2,1,0:T(8,128)(2,1)}), bf16[8,128,512]{2,1,0:T(8,128)(2,1)S(1)}, u32[]{:S(2)}, u32[]{:S(2)}) async-start(bf16[8,128,512]{2,1,0:T(8,128)(2,1)} %bitcast.42), calls=%async_computation.8 | async-start | bytes 2097152 | tf_op jit(solution)/shard_map/all_to_all | solution.py:343
  196.0 138.0 %all-reduce.3.cloned.1.call-start = ((), (), s32[]{:S(2)}) async-start(), calls=%async_computation.15 | async-start | bytes 6291456 | tf_op jit(solution)/shard_map/psum | solution.py:424
  214.0 6.0 %copy-start.21 = (f32[128,1024]{1,0:T(8,128)S(1)}, f32[128,1024]{1,0:T(8,128)}, u32[]{:S(2)}) copy-start(f32[128,1024]{1,0:T(8,128)} %get-tuple-element.37) | copy-start | bytes 1572868
  (16 other events, 45.8 us)
Sparse Core Ops, SparseCore 0:
  9.9 30.5 all-gather.10
  69.5 26.9 all-gather.8
  98.4 29.7 all-gather.12
  129.9 29.5 all-gather.6
  162.5 35.2 reduce-scatter.3
  212.6 121.3 all-reduce.2

commit v2 on v1

--- a/solution.py
+++ b/solution.py
@@ -1,6 +1,10 @@
+import functools
+
 import jax
 import jax.numpy as jnp
 from jax import lax
+from jax.experimental import pallas as pl
+from jax.experimental.pallas import tpu as pltpu
 from jax.sharding import PartitionSpec as P
 
 HEADS = 16
@@ -343,6 +347,82 @@
     return lax.all_to_all(heads_value, "sq", split_axis=0, concat_axis=1, tiled=True)
 
 
+MESH = pl.DeviceIdType.MESH
+bf16, f32 = jnp.bfloat16, jnp.float32
+
+def chain_kernel(chunk, lag, g_ref, t_ref, dummy, x_ref, send, send2, rsem, xsem, tsem):
+    dp = lax.axis_index("dp"); sq = lax.axis_index("sq")
+    n = g_ref.shape[0] // chunk
+    inner = (dp == 1) | (dp == 2)
+    outer = (dp == 0) | (dp == 3)
+    mate = 3 - dp
+    edge = jnp.where(dp == 1, 0, 3)
+    core = jnp.where(dp == 0, 1, 2)
+    bar = pltpu.get_barrier_semaphore()
+    def rows(c): return pl.ds(pl.multiple_of(c * chunk, chunk), chunk)
+    def raw(c):
+        return pltpu.make_async_remote_copy(g_ref.at[rows(c)], t_ref.at[rows(c)], send.at[c], rsem.at[c], device_id=(core, sq), device_id_type=MESH)
+    def cross(c):
+        return pltpu.make_async_remote_copy(g_ref.at[rows(c)], x_ref.at[rows(c)], send.at[c], xsem.at[c], device_id=(mate, sq), device_id_type=MESH)
+    def back(c):
+        return pltpu.make_async_remote_copy(t_ref.at[rows(c)], t_ref.at[rows(c)], send2.at[c], tsem.at[c], device_id=(edge, sq), device_id_type=MESH)
+    @pl.when(outer)
+    def _():
+        pl.semaphore_signal(bar, inc=1, device_id=(core, sq), device_id_type=MESH)
+        pl.semaphore_wait(bar, 1)
+        @pl.loop(0, n)
+        def _(c): raw(c).start()
+        @pl.loop(0, n)
+        def _(c):
+            back(c).wait_recv()
+            raw(c).wait_send()
+    @pl.when(inner)
+    def _():
+        pl.semaphore_signal(bar, inc=1, device_id=(edge, sq), device_id_type=MESH)
+        pl.semaphore_signal(bar, inc=1, device_id=(mate, sq), device_id_type=MESH)
+        pl.semaphore_wait(bar, 2)
+        def A(c):
+            raw(c).wait_recv()
+            g_ref[rows(c), :] = (g_ref[rows(c), :].astype(f32) + t_ref[rows(c), :].astype(f32)).astype(bf16)
+            cross(c).start()
+        def B(c):
+            cross(c).wait_recv()
+            t_ref[rows(c), :] = (g_ref[rows(c), :].astype(f32) + x_ref[rows(c), :].astype(f32)).astype(bf16)
+            back(c).start()
+        for c in range(lag): A(c)
+        @pl.loop(lag, n)
+        def _(c):
+            A(c)
+            B(c - lag)
+        @pl.loop(n - lag, n)
+        def _(c): B(c)
+        @pl.loop(0, n)
+        def _(c):
+            cross(c).wait_send()
+            back(c).wait_send()
+
+def chain(g, chunk=64, lag=2):
+    n = g.shape[0] // chunk
+    V = pltpu.VMEM
+    t, _ = pl.pallas_call(functools.partial(chain_kernel, chunk, lag),
+        out_shape=(jax.ShapeDtypeStruct(g.shape, bf16),jax.ShapeDtypeStruct((8,128), f32)),
+        in_specs=[pl.BlockSpec(memory_space=pltpu.VMEM)],
+        out_specs=(pl.BlockSpec(memory_space=pltpu.VMEM),pl.BlockSpec(memory_space=pl.ANY)),
+        scratch_shapes=[V(g.shape, bf16)] + [pltpu.SemaphoreType.DMA((n,))] * 5,
+        compiler_params=pltpu.CompilerParams(has_side_effects=True, collective_id=1, vmem_limit_bytes=60*2**20))(g)
+    return t
+
+
+def low_blocks(grad):
+    rows, columns = grad.shape
+    return grad.reshape(rows, columns // 1024, 1024).swapaxes(0, 1).reshape(-1, 1024)
+
+
+def from_blocks(blocks, number):
+    rows = blocks.shape[0] // number
+    return blocks.reshape(number, rows, 1024).swapaxes(0, 1).reshape(rows, -1)
+
+
 def shards_by_heads(frames, norm1_gain, w_qkv, w_out, norm2_gain, w_up, w_down, lengths, cotangent):
     _, rows, width = frames.shape
     ff = w_up.shape[1]
@@ -421,8 +501,15 @@
     )
     gains = lax.psum_scatter(jnp.stack([gain1_part, gain2_part]), "sq", scatter_dimension=1, tiled=True)
     gains = lax.psum(gains, "dp")
-    sums = lax.psum((grad_qkv, grad_out, grad_up, grad_down), "dp")
-    grad_qkv, grad_out, grad_up, grad_down = (member.astype(jnp.float32) for member in sums)
+    pieces = (grad_down, low_blocks(grad_up), grad_out, low_blocks(grad_qkv))
+    sums = chain(jnp.concatenate(pieces, axis=0), 32, 2)
+    starts = [0]
+    for piece in pieces:
+        starts.append(starts[-1] + piece.shape[0])
+    grad_down, grad_up, grad_out, grad_qkv = (
+        from_blocks(sums[starts[k] : starts[k + 1]], where).astype(jnp.float32)
+        for k, where in enumerate((1, ff // width, 1, 3))
+    )
     return (result, grad_frames, gains[0], grad_qkv, grad_out, gains[1], grad_up, grad_down)
 
 

time: 349 us -> 392 us (1.12)
  Pallas kernels: 0 us -> 83.6 us
  waiting for transfers between devices: 167 us -> 111 us
  blocking collectives: 21.2 us -> 30.6 us
  local copies, waits for them, and re-layouts: 13.1 us -> 21.9 us
    psum x1 -> x0, waiting for transfers between devices: 99.8 us -> none  [shards_by_heads(): sums = lax.psum((grad_qkv, grad_out, grad_up, grad_down), 'dp')]
    pallas_call x0 -> x1, Pallas kernels: none -> 83.6 us  [chain(): pl.pallas_call(functools.partial(chain_kernel, chunk, lag), out_shape=(ja...]
    all_gather x1, waiting for transfers between devices: 0.01 us -> 25.4 us  [shards_by_heads(): grad_all = lax.all_gather(grad_low, 'sq', axis=0, tiled=True)]
    all_gather x1, waiting for transfers between devices: 0.01 us -> 22.2 us  [shards_by_heads(): grad_attn_all = lax.all_gather(grad_attn, 'sq', axis=0, tiled=True)]
    all_gather x1, waiting for transfers between devices: 0.02 us -> 12.5 us  [shards_by_heads(): hidden2_all = lax.all_gather(hidden2, 'sq', axis=0, tiled=True)]
    all_to_all x7, waiting for transfers between devices: 31.6 us -> 19.8 us  [to_rows(): lax.all_to_all(heads_value, 'sq', split_axis=0, concat_axis=1, tiled=True)]
    all_to_all x0 -> x1, blocking collectives: none -> 9.35 us  [to_heads(): lax.all_to_all(rows_value, 'sq', split_axis=1, concat_axis=0, tiled=True)]
    all_to_all x1 -> x0, waiting for transfers between devices: 5.69 us -> none  [to_heads(): lax.all_to_all(rows_value, 'sq', split_axis=1, concat_axis=0, tiled=True)]
  transfers between devices with their start and end apart: 14 -> 12, of which waited for: 9 -> 8; matrix products, arithmetic and copies ran while one was open for 25% -> 13% of each run, Pallas kernels for 0% -> 0%
where the time goes in v2:
time: 392 us; the launch traced here: 391 us
  waiting for transfers between devices  111 us (28%)
  Pallas kernels  83.6 us (21%)
  matrix products  79.8 us (20%)
  blocking collectives  30.6 us (8%)
  starting transfers between devices  26.7 us (7%)
  other arithmetic  22.3 us (6%)
  local copies, waits for them, and re-layouts  21.9 us (6%)
  between operations  14.3 us (4%)
    pallas_call x1, Pallas kernels, chain(): pl.pallas_call(functools.partial(chain_kernel, chunk, lag), out_shape=(ja...  83.6 us
    all_gather x1, waiting for transfers between devices, shards_by_heads(): lax.all_gather(frames[0], 'sq', axis=0, tiled=True).astype(jnp.float32)  29 us
    all_to_all x7, starting transfers between devices, to_rows(): lax.all_to_all(heads_value, 'sq', split_axis=0, concat_axis=1, tiled=True)  26.5 us
    all_gather x1, waiting for transfers between devices, shards_by_heads(): grad_all = lax.all_gather(grad_low, 'sq', axis=0, tiled=True)  25.4 us
    all_gather x1, waiting for transfers between devices, shards_by_heads(): grad_attn_all = lax.all_gather(grad_attn, 'sq', axis=0, tiled=True)  22.2 us
    dot_general x3, matrix products, times_transpose(): lax.dot_general(left, right, (((1,), (1,)), ((), ())), preferred_element_...  22 us
    all_to_all x7, waiting for transfers between devices, to_rows(): lax.all_to_all(heads_value, 'sq', split_axis=0, concat_axis=1, tiled=True)  19.8 us
    dot_general x6, matrix products, contract_rows(): lax.dot_general(left, right, (((0,), (0,)), ((), ())), preferred_element_...  18.8 us
  transfers between devices with their start and end apart: 12, of which 8 were waited for; matrix products, arithmetic and copies ran while one was open for 13% of the time, Pallas kernels for 0%

profile of v2, /device:TPU:0, one launch (start us, length us, event | category | flops | bytes accessed | tf_op | source)
XLA Modules:
  0.0 390.6 jit_solution(4667909013523650286)
XLA Ops:
  11.5 29.0 %all-gather.11.cloned.1.call-done = bf16[1,1024,1024]{2,1,0:T(8,128)(2,1)} async-done(((bf16[1,128,1024]{2,1,0:T(8,128)(2,1)}), bf16[1,1024,1024]{2,1,0:T(8,128)(2,1)}) %all-gather.11.cloned.1.call-update) | async-done | bytes 2097168 | tf_op jit(solution)/shard_map/all_gather | solution.py:437
  44.7 7.0 %fusion.106 = (f32[2,1024]{1,0:T(2,128)S(1)}, f32[2,1024,1024]{1,2,0:T(8,128)}) fusion(pred[1024,1024]{0,1:T(8,128)(4,1)} %fusion.8, bf16[1024,2,64]{0,2,1:T(8,128)(2,1)S(1)} %bitcast.185, bf16[1024,2,64]{0,2,1:T(8,128)(2,1)S(1)} %bitcast.175), kind=kOutput, calls=%fused_computation.155 | convolution fusion | flops 276825088 | bytes 9969664 | tf_op jit(solution)/shard_map/sub | solution.py:455
  51.7 4.6 %fusion.10 = bf16[2,1024,1024]{1,2,0:T(8,128)(2,1)S(1)} fusion(f32[2,1024,1024]{1,2,0:T(8,128)} %get-tuple-element.55, f32[2,1024]{1,0:T(2,128)S(1)} %get-tuple-element.54), kind=kLoop, calls=%fused_computation.19 | loop fusion | flops 4194304 | bytes 12591104 | tf_op jit(solution)/shard_map/convert_element_type | solution.py:315
  58.5 9.5 %all_to_all.144 = bf16[8,128,128]{1,2,0:T(8,128)(2,1)S(1)} all-to-all(bf16[8,128,128]{1,2,0:T(8,128)(2,1)S(1)} %copy.67), channel_id=1, replica_groups=mesh['dp'=4,'sq'=8] {'sq'}, dimensions={0} | all-to-all | bytes 524288 | tf_op jit(solution)/shard_map/all_to_all | solution.py:347
  69.4 6.1 %fusion.110 = f32[128,4096]{1,0:T(8,128)} fusion(bf16[128,1024]{1,0:T(8,128)(2,1)} %multiply_convert_fusion.5, bf16[1024,4096]{1,0:T(8,128)(2,1)} %param.14), kind=kOutput, calls=%fused_computation.157 | convolution fusion | flops 1073741824 | bytes 10747904 | tf_op jit(solution)/shard_map/dot_general | solution.py:319
  75.4 13.3 %multiply_reduce_fusion = (f32[1024]{0:T(1024)S(1)}, f32[128]{0:T(128)S(1)}, f32[128,1024]{1,0:T(8,128)}) fusion(f32[128,1024]{1,0:T(8,128)S(1)} %get-tuple-element.59, f32[128]{0:T(128)S(1)} %get-tuple-element.53, f32[1024]{0:T(1024)S(1)} %copy-done.22, bf16[1024,4096]{1,0:T(8,128)(2,1)} %param.14, bf16[4096,1024]{1,0:T(8,128)(2,1)} %param.15, ...), kind=kOutput, calls=%fused_computation.104 | convolution fusion | flops 2158230528 | bytes 20194304 | tf_op jit(solution)/shard_map/dot_general | solution.py:74
  94.5 9.3 %all_to_all.145 = bf16[128,8,128]{0,2,1:T(8,128)(2,1)S(1)} all-to-all(bf16[128,8,128]{0,2,1:T(8,128)(2,1)S(1)} %bitcast.188), channel_id=1, replica_groups=mesh['dp'=4,'sq'=8] {'sq'}, dimensions={1} | all-to-all | bytes 524288 | tf_op jit(solution)/shard_map/all_to_all | solution.py:343
  112.1 4.7 %multiply_convert_fusion = bf16[2,1024,1024]{1,2,0:T(8,128)(2,1)S(1)} fusion(f32[2,1024]{1,0:T(2,128)S(1)} %bitcast.199, f32[2,1024,1024]{1,2,0:T(8,128)} %get-tuple-element.55, f32[2,1024]{1,0:T(2,128)S(1)} %get-tuple-element.54, bf16[1024,2,64]{0,2,1:T(8,128)(2,1)S(1)} %reshape.236, bf16[1024,2,64]{0,2,1:T(8,128)(2,1)S(1)} %bitcast.178), kind=kOutput, calls=%fused_computation.1 | convolution fusion | flops 276824064 | bytes 13123584 | tf_op jit(solution)/shard_map/qhd,khd->hqk/dot_general | solution.py:478
  119.6 4.1 %all-to-all-start.3 = ((bf16[8,128,128]{1,2,0:T(8,128)(2,1)}), bf16[8,128,128]{1,2,0:T(8,128)(2,1)S(1)}, u32[]{:S(2)}, u32[]{:S(2)}) async-start(bf16[8,128,128]{1,2,0:T(8,128)(2,1)} %copy.74), calls=%async_computation.3 | async-start | bytes 524288 | tf_op jit(solution)/shard_map/all_to_all | solution.py:347
  134.6 6.7 %all-to-all-done.2 = bf16[8,128,128]{1,2,0:T(8,128)(2,1)S(1)} async-done(((bf16[8,128,128]{1,2,0:T(8,128)(2,1)}), bf16[8,128,128]{1,2,0:T(8,128)(2,1)S(1)}, u32[]{:S(2)}, u32[]{:S(2)}) %all-to-all-start.2) | async-done | bytes 262176 | tf_op jit(solution)/shard_map/all_to_all | solution.py:347
  141.9 6.2 %fusion.76 = (f32[1024]{0:T(1024)S(1)}, f32[128]{0:T(128)S(1)}, f32[128,1024]{1,0:T(8,128)}) fusion(bf16[1,128,1024]{2,1,0:T(8,128)(2,1)S(1)} %copy-done.8, f32[128]{0:T(128)S(1)} %get-tuple-element.51, f32[1024]{0:T(1024)S(1)} %copy-done.23, bf16[1024,3072]{1,0:T(8,128)(2,1)} %param.11, bf16[128,1024]{0,1:T(8,128)(2,1)} %bitcast.195, ...), kind=kOutput, calls=%fused_computation.103 | convolution fusion | flops 808582016 | bytes 7873536 | tf_op jit(solution)/shard_map/dot_general | solution.py:74
  153.5 4.1 %all-to-all-start.8 = ((bf16[8,128,128]{2,1,0:T(8,128)(2,1)}), bf16[8,128,128]{2,1,0:T(8,128)(2,1)}, u32[]{:S(2)}, u32[]{:S(2)}) async-start(bf16[8,128,128]{2,1,0:T(8,128)(2,1)} %bitcast.183), calls=%async_computation.8 | async-start | bytes 524288 | tf_op jit(solution)/shard_map/all_to_all | solution.py:347
  160.0 4.5 %all-to-all-done.8 = bf16[8,128,128]{2,1,0:T(8,128)(2,1)} async-done(((bf16[8,128,128]{2,1,0:T(8,128)(2,1)}), bf16[8,128,128]{2,1,0:T(8,128)(2,1)}, u32[]{:S(2)}, u32[]{:S(2)}) %all-to-all-start.8) | async-done | bytes 262176 | tf_op jit(solution)/shard_map/all_to_all | solution.py:347
  164.5 4.0 %all-to-all-start.7 = ((bf16[8,128,128]{2,1,0:T(8,128)(2,1)}), bf16[8,128,128]{2,1,0:T(8,128)(2,1)}, u32[]{:S(2)}, u32[]{:S(2)}) async-start(bf16[8,128,128]{2,1,0:T(8,128)(2,1)} %bitcast.182), calls=%async_computation.7 | async-start | bytes 524288 | tf_op jit(solution)/shard_map/all_to_all | solution.py:347
  170.0 5.6 %all-to-all-done.7 = bf16[8,128,128]{2,1,0:T(8,128)(2,1)} async-done(((bf16[8,128,128]{2,1,0:T(8,128)(2,1)}), bf16[8,128,128]{2,1,0:T(8,128)(2,1)}, u32[]{:S(2)}, u32[]{:S(2)}) %all-to-all-start.7) | async-done | bytes 262176 | tf_op jit(solution)/shard_map/all_to_all | solution.py:347
  179.1 6.3 %fusion.35 = bf16[1,128,1024]{2,1,0:T(8,128)(2,1)} fusion(f32[128,1024]{1,0:T(8,128)S(1)} %get-tuple-element.59, bf16[4096,1024]{1,0:T(8,128)(2,1)} %param.15, f32[128,4096]{1,0:T(8,128)} %fusion.110), kind=kOutput, calls=%fused_computation.61 | convolution fusion | flops 1078722560 | bytes 11272192 | tf_op jit(solution)/shard_map/dot_general | solution.py:319
  190.3 11.8 %psum.7 = f32[2,128]{1,0:T(2,128)S(1)} all-reduce(f32[2,128]{1,0:T(2,128)S(1)} %copy.94), channel_id=1, replica_groups=mesh['dp'=4,'sq'=8] {'dp'}, use_global_device_ids=true, to_apply=%region_13.14 | all-reduce | flops 256 | bytes 2048 | tf_op jit(solution)/shard_map/psum | solution.py:503
  202.1 12.5 %all-gather.7.cloned.1.call-done = bf16[1024,1024]{1,0:T(8,128)(2,1)} async-done(((bf16[128,1024]{1,0:T(8,128)(2,1)}), bf16[1024,1024]{1,0:T(8,128)(2,1)}) %all-gather.7.cloned.1.call-update) | async-done | bytes 2097168 | tf_op jit(solution)/shard_map/all_gather | solution.py:464
  214.6 4.4 %fusion.49 = f32[1024,512]{1,0:T(8,128)} fusion(bf16[1024,1024]{1,0:T(8,128)(2,1)} %all-gather.7.cloned.1.call-done, bf16[1024,4096]{1,0:T(8,128)(2,1)} %param.14, s32[]{:T(128)S(6)} %select_n.39), kind=kOutput, calls=%fused_computation.76 | convolution fusion | flops 1073741824 | bytes 5242884 | tf_op jit(solution)/shard_map/dot_general | solution.py:319
  219.0 25.4 %all-gather.13.cloned.1.call-done = bf16[1,1024,1024]{2,1,0:T(8,128)(2,1)} async-done(((bf16[1,128,1024]{2,1,0:T(8,128)(2,1)}), bf16[1,1024,1024]{2,1,0:T(8,128)(2,1)}) %all-gather.13.cloned.1.call-update) | async-done | bytes 2097168 | tf_op jit(solution)/shard_map/all_gather | solution.py:439
  244.4 6.4 %convolution_convert_fusion = bf16[1024,512]{1,0:T(8,128)(2,1)S(1)} fusion(bf16[1024,1024]{1,0:T(8,128)(2,1)} %all-gather.7.cloned.1.call-done, f32[1024,512]{1,0:T(8,128)} %fusion.49, bf16[1,1024,1024]{2,1,0:T(8,128)(2,1)} %all-gather.13.cloned.1.call-done, bf16[4096,1024]{1,0:T(8,128)(2,1)} %param.15, s32[]{:T(128)S(6)} %select_n.39), kind=kOutput, calls=%fused_computation.45 | convolution fusion | flops 2157969408 | bytes 8388612 | tf_op jit(solution)/shard_map/dot_general | solution.py:68
  256.5 22.2 %all-gather.9.cloned.1.call-done = bf16[1024,1024]{1,0:T(8,128)(2,1)} async-done(((bf16[128,1024]{1,0:T(8,128)(2,1)}), bf16[1024,1024]{1,0:T(8,128)(2,1)}) %all-gather.9.cloned.1.call-update) | async-done | bytes 2097168 | tf_op jit(solution)/shard_map/all_gather | solution.py:473
  280.8 4.0 %fusion.27 = bf16[512,1024]{1,0:T(8,128)(2,1)} fusion(bf16[1,1024,1024]{2,1,0:T(8,128)(2,1)S(1)} %copy-done.24, f32[1024,512]{1,0:T(8,128)} %fusion.49), kind=kOutput, calls=%fused_computation.44 | convolution fusion | flops 1078984704 | bytes 5242880 | tf_op jit(solution)/shard_map/dot_general | solution.py:68
  288.3 83.6 %shard_map.152 = (bf16[1536,1024]{1,0:T(8,128)(2,1)}, f32[8,128]{1,0:T(8,128)}) custom-call(bf16[1536,1024]{1,0:T(8,128)(2,1)} %pad_maximum_fusion.g_ref), custom_call_target="tpu_custom_call" | custom-call | tf_op jit(solution)/shard_map/pallas_call | solution.py:407
  (129 shorter events, 81.0 us)
Async XLA Ops:
  7.2 60.8 %copy-start = (bf16[1024,1024]{1,0:T(8,128)(2,1)S(1)}, bf16[1024,1024]{1,0:T(8,128)(2,1)}, u32[]{:S(2)}) copy-start(bf16[1024,1024]{1,0:T(8,128)(2,1)} %param.12) | copy-start | bytes 6291460
  7.2 33.4 %all-gather.11.cloned.1.call-start = ((), (), s32[]{:S(2)}) async-start(), calls=%async_computation.12 | async-start | bytes 2359296 | tf_op jit(solution)/shard_map/all_gather | solution.py:437
  8.8 34.0 %copy-start.23 = (f32[1024]{0:T(1024)S(1)}, f32[1024]{0:T(1024)}, u32[]{:S(2)}) copy-start(f32[1024]{0:T(1024)} %param.10) | copy-start | bytes 12292
  44.7 7.0 %copy-start.11 = (bf16[1024,128]{0,1:T(8,128)(2,1)}, bf16[1024,128]{0,1:T(8,128)(2,1)S(1)}, u32[]{:S(2)}) copy-start(bf16[1024,128]{0,1:T(8,128)(2,1)S(1)} %get-tuple-element.45) | copy-start | bytes 786436
  44.7 7.0 %copy-start.16 = (bf16[1024,128]{0,1:T(8,128)(2,1)}, bf16[1024,128]{0,1:T(8,128)(2,1)S(1)}, u32[]{:S(2)}) copy-start(bf16[1024,128]{0,1:T(8,128)(2,1)S(1)} %get-tuple-element.46) | copy-start | bytes 786436
  44.7 11.7 %copy-start.13 = (bf16[1024,128]{0,1:T(8,128)(2,1)}, bf16[1024,128]{0,1:T(8,128)(2,1)S(1)}, u32[]{:S(2)}) copy-start(bf16[1024,128]{0,1:T(8,128)(2,1)S(1)} %get-tuple-element.47) | copy-start | bytes 786436
  56.4 11.6 %copy-start.7 = (bf16[1,128,1024]{2,1,0:T(8,128)(2,1)S(1)}, bf16[1,128,1024]{2,1,0:T(8,128)(2,1)}, u32[]{:S(2)}) copy-start(bf16[1,128,1024]{2,1,0:T(8,128)(2,1)} %param.9) | copy-start | bytes 786436
  58.4 10.1 %copy-start.22 = (f32[1024]{0:T(1024)S(1)}, f32[1024]{0:T(1024)}, u32[]{:S(2)}) copy-start(f32[1024]{0:T(1024)} %param.13) | copy-start | bytes 12292
  107.8 9.1 %copy-start.9 = (bf16[2,64,1024]{2,1,0:T(8,128)(2,1)}, bf16[2,64,1024]{2,1,0:T(8,128)(2,1)S(1)}, u32[]{:S(2)}) copy-start(bf16[2,64,1024]{2,1,0:T(8,128)(2,1)S(1)} %convolution_convert_fusion.6) | copy-start | bytes 786436
  108.6 11.0 %all-to-all-start.4 = ((bf16[8,128,128]{1,2,0:T(8,128)(2,1)}), bf16[8,128,128]{1,2,0:T(8,128)(2,1)S(1)}, u32[]{:S(2)}, u32[]{:S(2)}) async-start(bf16[8,128,128]{1,2,0:T(8,128)(2,1)} %copy.76), calls=%async_computation.4 | async-start | bytes 524288 | tf_op jit(solution)/shard_map/all_to_all | solution.py:347
  119.6 7.2 %copy-start.19 = (bf16[8,128,128]{1,2,0:T(8,128)(2,1)}, bf16[8,128,128]{1,2,0:T(8,128)(2,1)S(1)}, u32[]{:S(2)}) copy-start(bf16[8,128,128]{1,2,0:T(8,128)(2,1)S(1)} %all-to-all-done.4) | copy-start | bytes 786436
  119.6 11.1 %all-to-all-start.3 = ((bf16[8,128,128]{1,2,0:T(8,128)(2,1)}), bf16[8,128,128]{1,2,0:T(8,128)(2,1)S(1)}, u32[]{:S(2)}, u32[]{:S(2)}) async-start(bf16[8,128,128]{1,2,0:T(8,128)(2,1)} %copy.74), calls=%async_computation.3 | async-start | bytes 524288 | tf_op jit(solution)/shard_map/all_to_all | solution.py:347
  123.8 10.6 %copy-start.8 = (bf16[1,128,1024]{2,1,0:T(8,128)(2,1)S(1)}, bf16[1,128,1024]{2,1,0:T(8,128)(2,1)}, u32[]{:S(2)}) copy-start(bf16[1,128,1024]{2,1,0:T(8,128)(2,1)} %param.9) | copy-start | bytes 786436
  130.7 10.5 %copy-start.20 = (bf16[8,128,128]{1,2,0:T(8,128)(2,1)}, bf16[8,128,128]{1,2,0:T(8,128)(2,1)S(1)}, u32[]{:S(2)}) copy-start(bf16[8,128,128]{1,2,0:T(8,128)(2,1)S(1)} %all-to-all-done.3) | copy-start | bytes 786436
  130.7 10.5 %all-to-all-start.2 = ((bf16[8,128,128]{1,2,0:T(8,128)(2,1)}), bf16[8,128,128]{1,2,0:T(8,128)(2,1)S(1)}, u32[]{:S(2)}, u32[]{:S(2)}) async-start(bf16[8,128,128]{1,2,0:T(8,128)(2,1)} %copy.72), calls=%async_computation.2 | async-start | bytes 524288 | tf_op jit(solution)/shard_map/all_to_all | solution.py:347
  134.3 55.1 %reduce-scatter.4.cloned.1.call-start = ((), (), s32[]{:S(2)}) async-start(), calls=%async_computation.14 | async-start | bytes 589824
  141.9 9.2 %copy-start.3 = (bf16[1024,1024]{1,0:T(8,128)(2,1)S(1)}, bf16[1024,1024]{1,0:T(8,128)(2,1)}, u32[]{:S(2)}) copy-start(bf16[1024,1024]{1,0:T(8,128)(2,1)} %copy-done.2) | copy-start | bytes 6291460
  149.2 65.4 %all-gather.7.cloned.1.call-start = ((), (), s32[]{:S(2)}) async-start(), calls=%async_computation.10 | async-start | bytes 2359296 | tf_op jit(solution)/shard_map/all_gather | solution.py:464
  149.9 94.5 %all-gather.13.cloned.1.call-start = ((), (), s32[]{:S(2)}) async-start(), calls=%async_computation.13 | async-start | bytes 2359296 | tf_op jit(solution)/shard_map/all_gather | solution.py:439
  150.5 128.1 %all-gather.9.cloned.1.call-start = ((), (), s32[]{:S(2)}) async-start(), calls=%async_computation.11 | async-start | bytes 2359296 | tf_op jit(solution)/shard_map/all_gather | solution.py:473
  153.5 11.0 %all-to-all-start.8 = ((bf16[8,128,128]{2,1,0:T(8,128)(2,1)}), bf16[8,128,128]{2,1,0:T(8,128)(2,1)}, u32[]{:S(2)}, u32[]{:S(2)}) async-start(bf16[8,128,128]{2,1,0:T(8,128)(2,1)} %bitcast.183), calls=%async_computation.8 | async-start | bytes 524288 | tf_op jit(solution)/shard_map/all_to_all | solution.py:347
  164.5 11.2 %all-to-all-start.7 = ((bf16[8,128,128]{2,1,0:T(8,128)(2,1)}), bf16[8,128,128]{2,1,0:T(8,128)(2,1)}, u32[]{:S(2)}, u32[]{:S(2)}) async-start(bf16[8,128,128]{2,1,0:T(8,128)(2,1)} %bitcast.182), calls=%async_computation.7 | async-start | bytes 524288 | tf_op jit(solution)/shard_map/all_to_all | solution.py:347
  175.7 12.3 %all-to-all-start.6 = ((bf16[8,128,128]{2,1,0:T(8,128)(2,1)}), bf16[8,128,128]{2,1,0:T(8,128)(2,1)S(1)}, u32[]{:S(2)}, u32[]{:S(2)}) async-start(bf16[8,128,128]{2,1,0:T(8,128)(2,1)} %bitcast.181), calls=%async_computation.6 | async-start | bytes 524288 | tf_op jit(solution)/shard_map/all_to_all | solution.py:347
  252.1 32.7 %all-to-all-start.5 = ((bf16[8,128,512]{1,2,0:T(8,128)(2,1)}), bf16[8,128,512]{1,2,0:T(8,128)(2,1)S(1)}, u32[]{:S(2)}, u32[]{:S(2)}) async-start(bf16[8,128,512]{1,2,0:T(8,128)(2,1)} %copy.78), calls=%async_computation.5 | async-start | bytes 2097152 | tf_op jit(solution)/shard_map/all_to_all | solution.py:347
  (13 other events, 33.1 us)
Sparse Core Ops, SparseCore 0:
  9.9 30.5 all-gather.10
  149.3 34.4 reduce-scatter.3
  185.9 28.6 all-gather.6
  216.5 27.8 all-gather.12
  246.3 32.2 all-gather.8

commit v3 on v0

--- a/solution.py
+++ b/solution.py
@@ -1,6 +1,10 @@
+import functools
+
 import jax
 import jax.numpy as jnp
 from jax import lax
+from jax.experimental import pallas as pl
+from jax.experimental.pallas import tpu as pltpu
 from jax.sharding import PartitionSpec as P
 
 HEADS = 16
@@ -18,6 +22,12 @@
 
 def segment_ids(positions, item_ends):
     return jnp.sum((positions[None, :, None] >= item_ends[:, None, :]).astype(jnp.int32), axis=2)
+
+
+def running_ends(lengths):
+    items = jnp.arange(lengths.shape[1], dtype=jnp.int32)
+    before = items[None, None, :] <= items[None, :, None]
+    return jnp.sum(jnp.where(before, lengths[:, None, :], 0), axis=2)
 
 
 def visible(query_pos, query_seg, key_pos, key_seg):
@@ -70,14 +80,14 @@
     return values.transpose(0, 2, 1, 3).reshape(batch * rows, width)
 
 
-def shards(frames, norm1_gain, w_qkv, w_out, norm2_gain, w_up, w_down, lengths, cotangent):
+def shards_by_rows(frames, norm1_gain, w_qkv, w_out, norm2_gain, w_up, w_down, lengths, cotangent):
     batch = frames.shape[0]
     rows = frames.shape[1]
     width = frames.shape[2]
     factor = HEAD_DIM ** (-0.5)
     first = lax.axis_index("sq") * rows
     query_pos = first + jnp.arange(rows, dtype=jnp.int32)
-    item_ends = jnp.cumsum(lengths, axis=1)
+    item_ends = running_ends(lengths)
     query_seg = segment_ids(query_pos, item_ends)
     frames_own = frames.reshape(batch * rows, width).astype(jnp.float32)
     hidden1, norm1_pull = jax.vjp(norm_scaled, frames_own, norm1_gain)
@@ -301,9 +311,726 @@
     )
 
 
+MESH = pl.DeviceIdType.MESH
+ZROWS = 32
+ZLAG = 2
+QBLOCK = 256
+
+
+def dot(left, right):
+    return jnp.dot(left, right, preferred_element_type=jnp.float32)
+
+
+def dot_nt(left, right):
+    return lax.dot_general(
+        left, right, (((1,), (1,)), ((), ())), preferred_element_type=jnp.float32
+    )
+
+
+def dot_tn(left, right):
+    return lax.dot_general(
+        left, right, (((0,), (0,)), ((), ())), preferred_element_type=jnp.float32
+    )
+
+
+def low(values):
+    return values.astype(jnp.bfloat16)
+
+
+def wide(values):
+    return values.astype(jnp.float32)
+
+
+def span(start, size):
+    return pl.ds(pl.multiple_of(start, size), size)
+
+
+def norm_scale(values):
+    return lax.rsqrt(jnp.mean(values * values, axis=-1, keepdims=True) + EPSILON)
+
+
+def norm_back(values, scale, gain, grad):
+    scaled = gain * grad
+    inner = jnp.mean(scaled * values, axis=-1, keepdims=True)
+    part = scale * scaled - values * (scale * scale * scale) * inner
+    return part, jnp.sum(grad * values * scale, axis=0, keepdims=True)
+
+
+def gelu_parts(values):
+    root = 0.7978845608028654
+    square = values * values
+    inner = jnp.tanh(root * values * (1.0 + 0.044715 * square))
+    half = 0.5 * (1.0 + inner)
+    slope = half + 0.5 * root * values * (1.0 - inner * inner) * (1.0 + 0.134145 * square)
+    return values * half, slope
+
+
+def layer_kernel(
+    count, planes,
+    frames_in, gain1_ref, w_qkv_in, w_out_in, gain2_ref, w_up_in, w_down_in, lengths_ref, cot_in,
+    result_ref, d_in_ref, gains_ref, sum_ref,
+    frames_all, hidden1_all, cot_all, hidden2_all, attn_all,
+    w_heads, w_out, w_up, w_down,
+    mixed, q_pad, k_pad, v_pad, g_pad, shares, scores, o_turned, o_heads, o_rows,
+    middle, acc_a, acc_b, grad_mid, g_rows, g_heads,
+    active_s, slope_s, up_stage, mixed_grad, mixed_stage, mixed_rows, k_acc, v_acc,
+    own, cross_in, gain_out, gain_in, gain_z,
+    load_sem, ag_send, ag_recv, o_send, o_recv, g_send, g_recv, m_send, m_recv,
+    u_send, u_recv, s_send, s_recv, n_send, n_recv, nz_send, nz_recv,
+    z_send, zb_send, z_raw_recv, z_cross_recv, z_back_recv,
+):
+    bf16, f32 = jnp.bfloat16, jnp.float32
+    rows, width = result_ref.shape
+    total = rows * count
+    part = width // count
+    local = part // HEAD_DIM
+    ff = w_up.shape[1]
+    slab = ff // count
+    half = rows // 2
+    factor = HEAD_DIM ** (-0.5)
+    me, plane = lax.axis_index("sq"), lax.axis_index("dp")
+
+    def flip(index, bit):
+        return index + bit - 2 * bit * lax.rem(lax.div(index, bit), 2)
+
+    mate, over_x, over_y = flip(me, 1), flip(me, 2), flip(me, 4)
+    corner = flip(over_x, 4)
+    inner = (plane == 1) | (plane == 2)
+    outer = (plane == 0) | (plane == 3)
+    z_mate = planes - 1 - plane
+    z_edge = jnp.where(plane == 1, 0, planes - 1)
+    z_core = jnp.where(plane == 0, 1, planes - 2)
+
+    def remote(source, target, send, recv, to, to_plane=None):
+        return pltpu.make_async_remote_copy(
+            src_ref=source, dst_ref=target, send_sem=send, recv_sem=recv,
+            device_id=(plane if to_plane is None else to_plane, to), device_id_type=MESH,
+        )
+
+    def others(body):
+        @pl.loop(1, count)
+        def _(step):
+            body(lax.rem(me + step, count))
+
+    mine = span(me * rows, rows)
+    loads = [
+        pltpu.make_async_copy(frames_in.at[0], frames_all.at[mine], load_sem.at[0]),
+        pltpu.make_async_copy(cot_in.at[0], cot_all.at[mine], load_sem.at[1]),
+    ] + [
+        pltpu.make_async_copy(
+            w_qkv_in.at[:, span(k * width + me * part, part)],
+            w_heads.at[:, pl.ds(k * part, part)],
+            load_sem.at[2 + k],
+        )
+        for k in range(3)
+    ] + [
+        pltpu.make_async_copy(w_out_in, w_out, load_sem.at[5]),
+        pltpu.make_async_copy(w_up_in, w_up, load_sem.at[6]),
+        pltpu.make_async_copy(w_down_in, w_down, load_sem.at[7]),
+    ]
+    load_qkv = pltpu.make_async_copy(w_qkv_in, w_up.at[:, pl.ds(0, 3 * width)], load_sem.at[8])
+    for load in loads[:5]:
+        load.start()
+
+    barrier = pltpu.get_barrier_semaphore()
+    others(lambda s: pl.semaphore_signal(
+        barrier, inc=1, device_id=(plane, s), device_id_type=MESH))
+
+    @pl.loop(1, planes)
+    def _(step):
+        pl.semaphore_signal(
+            barrier, inc=1, device_id=(lax.rem(plane + step, planes), me), device_id_type=MESH)
+
+    pl.semaphore_wait(barrier, count - 1 + planes - 1)
+
+    def slots(index):
+        return [
+            (me, None, mate, mate),
+            (me, 0, over_x, over_x), (me, 1, over_x, over_x),
+            (me, 1, over_y, over_y), (me, 0, over_y, over_y),
+            (over_x, 0, over_y, corner), (over_y, 1, over_x, corner),
+            (over_x, 0, mate, flip(mate, 2)), (over_x, 1, mate, flip(mate, 2)),
+            (over_y, 1, mate, flip(mate, 4)), (over_y, 0, mate, flip(mate, 4)),
+            (corner, 0, mate, flip(corner, 1)), (corner, 1, mate, flip(corner, 1)),
+        ][index]
+
+    def gather(number, array, source=None):
+        def piece(block, which):
+            if which is None:
+                return span(block * rows, rows)
+            return span(block * rows + which * half, half)
+
+        def copy(slot, sent=True):
+            block, which, target, arrives = slots(slot)
+            there = piece(block if sent else arrives, which)
+            here = array.at[there]
+            if sent and source is not None and slot < 5:
+                here = source if which is None else source.at[pl.ds(which * half, half)]
+            return remote(
+                here, array.at[there], ag_send.at[number, slot], ag_recv.at[number, slot], target)
+
+        def start(*numbers):
+            for slot in numbers:
+                copy(slot).start()
+
+        def wait(*numbers):
+            for slot in numbers:
+                copy(slot, sent=False).wait_recv()
+
+        def finish():
+            for slot in range(13):
+                copy(slot).wait_send()
+
+        return start, wait, finish
+
+    f_start, f_wait, f_finish = gather(0, frames_all, frames_in.at[0])
+    c_start, c_wait, c_finish = gather(1, cot_all, cot_in.at[0])
+    h_start, h_wait, h_finish = gather(2, hidden2_all)
+    a_start, a_wait, a_finish = gather(3, attn_all)
+
+    def z_raw(c):
+        at = span(c * ZROWS, ZROWS)
+        return remote(own.at[at], sum_ref.at[at], z_send.at[c], z_raw_recv.at[c], me, z_core)
+
+    def z_cross(c):
+        at = span(c * ZROWS, ZROWS)
+        return remote(own.at[at], cross_in.at[at], z_send.at[c], z_cross_recv.at[c], me, z_mate)
+
+    def z_back(c):
+        at = span(c * ZROWS, ZROWS)
+        return remote(sum_ref.at[at], sum_ref.at[at], zb_send.at[c], z_back_recv.at[c], me, z_edge)
+
+    def z_join(c):
+        at = span(c * ZROWS, ZROWS)
+        z_raw(c).wait_recv()
+        own[at, :] = low(wide(own[at, :]) + wide(sum_ref[at, :]))
+        z_cross(c).start()
+
+    def z_close(c):
+        at = span(c * ZROWS, ZROWS)
+        z_cross(c).wait_recv()
+        sum_ref[at, :] = low(wide(own[at, :]) + wide(cross_in[at, :]))
+        z_back(c).start()
+
+    chunks = own.shape[0] // ZROWS
+    z_done = [0]
+
+    def z_inner(number):
+        first, last = z_done[0], z_done[0] + number
+        z_done[0] = last
+
+        @pl.when(inner)
+        def _():
+            split = min(max(first, ZLAG), last)
+            for c in range(first, split):
+                z_join(c)
+            if last > split:
+                @pl.loop(split, last)
+                def _(c):
+                    z_join(c)
+                    z_close(c - ZLAG)
+
+    def z_outer(first, last):
+        @pl.when(outer)
+        def _():
+            @pl.loop(first, last)
+            def _(c):
+                z_raw(c).start()
+
+    f_start(0, 1, 3, 2, 4)
+    for load in loads[5:]:
+        load.start()
+    lane_head = lax.broadcasted_iota(jnp.int32, (rows, part), 1) // HEAD_DIM
+    gain1 = gain1_ref[...]
+    gain2 = gain2_ref[...]
+
+    def qkv_block(block):
+        at = span(block * rows, rows)
+        values = wide(frames_all[at, :])
+        hidden = low(values * norm_scale(values) * gain1)
+        hidden1_all[at, :] = hidden
+        projected = low(dot(hidden, w_heads[...]))
+        mixed[at, :] = projected
+        for head in range(local):
+            on = lane_head == head
+            q_pad[head, at, :] = low(jnp.where(on, wide(projected[:, :part]) * factor, 0.0))
+            k_pad[head, at, :] = low(jnp.where(on, wide(projected[:, part : 2 * part]), 0.0))
+            v_pad[head, at, :] = low(jnp.where(on, wide(projected[:, 2 * part :]), 0.0))
+
+    loads[0].wait()
+    for k in range(3):
+        loads[2 + k].wait()
+    qkv_block(me)
+    f_wait(0)
+    qkv_block(mate)
+    f_wait(1)
+    f_start(5, 7)
+    f_wait(3)
+    f_start(6, 9)
+    c_start(0, 1, 3, 2, 4)
+    f_wait(2)
+    f_start(8)
+    qkv_block(over_x)
+    f_wait(4)
+    f_start(10)
+    qkv_block(over_y)
+    f_wait(7, 8)
+    qkv_block(flip(mate, 2))
+    f_wait(9, 10)
+    qkv_block(flip(mate, 4))
+    f_wait(5)
+    f_start(11)
+    f_wait(6)
+    f_start(12)
+    qkv_block(corner)
+    f_wait(11, 12)
+    qkv_block(flip(corner, 1))
+
+    ends, running = [], None
+    for item in range(lengths_ref.shape[1]):
+        length = lengths_ref[0, item]
+        running = length if running is None else running + length
+        ends.append(running)
+
+    keys_at = pl.ds(part, part)
+    values_at = pl.ds(2 * part, part)
+    query_blocks = total // QBLOCK
+    per_block = QBLOCK // rows
+
+    def o_copy(target, source):
+        return remote(
+            o_heads.at[span(target * rows, rows)], o_rows.at[:, span(source * part, part)],
+            o_send.at[target], o_recv.at[source], target)
+
+    @pl.loop(0, query_blocks)
+    def _(i):
+        at = span(i * QBLOCK, QBLOCK)
+        query_pos = i * QBLOCK + lax.broadcasted_iota(jnp.int32, (1, QBLOCK), 1)
+        begin = jnp.zeros((1, QBLOCK), jnp.int32)
+        for end in ends:
+            begin = jnp.maximum(begin, jnp.where(query_pos >= end, end, 0))
+        turned = jnp.zeros((part, QBLOCK), f32)
+        for head in range(local):
+            queries = q_pad[head, at, :]
+
+            def score(j, top):
+                keys = span(j * QBLOCK, QBLOCK)
+                key_pos = j * QBLOCK + lax.broadcasted_iota(jnp.int32, (QBLOCK, 1), 0)
+                value = dot_nt(mixed[keys, keys_at], queries)
+                value = jnp.where((key_pos <= query_pos) & (key_pos >= begin), value, NEG_FILL)
+                scores[keys, :] = value
+                return jnp.maximum(top, jnp.max(value, axis=0, keepdims=True))
+
+            top = lax.fori_loop(0, i + 1, score, jnp.full((1, QBLOCK), START_MAX, f32))
+
+            def weigh(j, weight_sum):
+                keys = span(j * QBLOCK, QBLOCK)
+                weight = jnp.exp(scores[keys, :] - top)
+                scores[keys, :] = weight
+                return weight_sum + jnp.sum(weight, axis=0, keepdims=True)
+
+            weight_sum = lax.fori_loop(0, i + 1, weigh, jnp.zeros((1, QBLOCK), f32))
+            over = 1.0 / weight_sum
+
+            def attend(j, accum):
+                keys = span(j * QBLOCK, QBLOCK)
+                share = low(scores[keys, :] * over)
+                shares[head, keys, at] = share
+                return accum + dot_tn(v_pad[head, keys, :], share)
+
+            turned = lax.fori_loop(0, i + 1, attend, turned)
+        o_turned[:, at] = turned
+        o_heads[at, :] = low(turned.T)
+        for k in range(per_block):
+            target = i * per_block + k
+
+            @pl.when(target != me)
+            def _():
+                o_copy(target, me).start()
+
+            @pl.when(target == me)
+            def _():
+                o_rows[:, span(me * part, part)] = o_heads[mine, :]
+
+    c_wait(1)
+    c_start(5, 7)
+    c_wait(3)
+    c_start(6, 9)
+    loads[5].wait()
+    others(lambda s: o_copy(me, s).wait_recv())
+    middle_own = wide(frames_all[mine, :]) + dot(o_rows[...], w_out[...])
+    middle[...] = middle_own
+    hidden2_own = low(middle_own * norm_scale(middle_own) * gain2)
+    hidden2_all[mine, :] = hidden2_own
+    h_start(0, 1, 3, 2, 4)
+
+    loads[1].wait()
+    loads[6].wait()
+    loads[7].wait()
+    acc_a[...] = middle_own
+    acc_b[...] = jnp.zeros_like(acc_b)
+
+    def ff_tile(t):
+        at = span(t * slab, slab)
+        active, slope = gelu_parts(dot(hidden2_all[mine, :], w_up[:, at]))
+        acc_a[...] += dot(low(active), w_down[at, :])
+        grad = low(dot_nt(cot_all[mine, :], w_down[at, :]) * slope)
+        acc_b[...] += dot_nt(grad, w_up[:, at])
+
+    pl.loop(0, count // 2)(ff_tile)
+    h_wait(1)
+    h_start(5, 7)
+    h_wait(3)
+    h_start(6, 9)
+    pl.loop(count // 2, count)(ff_tile)
+    result_ref[...] = low(acc_a[...])
+
+    middle_own = middle[...]
+    back2, gain2_part = norm_back(middle_own, norm_scale(middle_own), gain2, acc_b[...])
+    gain_out[...] = jnp.zeros_like(gain_out)
+    for s in range(count):
+        gain_out[s, 1:2, :] = gain2_part[:, s * part : (s + 1) * part]
+    grad_mid_own = wide(cot_all[mine, :]) + back2
+    grad_mid[...] = grad_mid_own
+    attn_own = low(grad_mid_own)
+    attn_all[mine, :] = attn_own
+    g_rows[...] = low(dot_nt(attn_own, w_out[...]))
+
+    def g_copy(target, source):
+        return remote(
+            g_rows.at[:, span(target * part, part)], g_heads.at[span(source * rows, rows)],
+            g_send.at[target], g_recv.at[source], target)
+
+    others(lambda s: g_copy(s, me).start())
+    g_heads[mine, :] = g_rows[:, span(me * part, part)]
+    a_start(0, 1, 3, 2, 4)
+
+    slab_at = span(me * slab, slab)
+
+    def slab_block(block):
+        at = span(block * rows, rows)
+        active, slope = gelu_parts(dot(hidden2_all[at, :], w_up[:, slab_at]))
+        active_s[at, :] = low(active)
+        slope_s[at, :] = low(dot_nt(cot_all[at, :], w_down[slab_at, :]) * slope)
+
+    slab_block(me)
+    c_wait(0)
+    h_wait(0)
+    slab_block(mate)
+    c_wait(2, 4)
+    c_start(8, 10)
+    h_wait(2, 4)
+    h_start(8, 10)
+    slab_block(over_x)
+    slab_block(over_y)
+    c_wait(7, 8)
+    h_wait(7, 8)
+    slab_block(flip(mate, 2))
+    c_wait(9, 10)
+    h_wait(9, 10)
+    slab_block(flip(mate, 4))
+    c_wait(5, 6)
+    c_start(11, 12)
+    h_wait(5, 6)
+    h_start(11, 12)
+    slab_block(corner)
+    c_wait(11, 12)
+    h_wait(11, 12)
+    slab_block(flip(corner, 1))
+    load_qkv.start()
+
+    down_rows, up_rows = slab, rows * (ff // width)
+    down_at, up_at = 0, down_rows
+    out_at = up_at + up_rows
+    mixed_at = out_at + part
+    slabs = width // slab
+
+    @pl.loop(0, slab // part)
+    def _(t):
+        own[span(down_at + t * part, part), :] = low(
+            dot_tn(active_s[:, span(t * part, part)], cot_all[...]))
+
+    z_outer(0, up_at // ZROWS)
+
+    def u_copy(target, source):
+        return remote(
+            up_stage.at[span(target * rows, rows)],
+            own.at[span(up_at + lax.div(source, slabs) * rows, rows),
+                   span(lax.rem(source, slabs) * slab, slab)],
+            u_send.at[target], u_recv.at[source], target)
+
+    @pl.loop(0, count)
+    def _(s):
+        at = span(s * rows, rows)
+        up_stage[at, :] = low(dot_tn(hidden2_all[:, at], slope_s[...]))
+
+        @pl.when(s != me)
+        def _():
+            u_copy(s, me).start()
+
+    own[span(up_at + lax.div(me, slabs) * rows, rows), span(lax.rem(me, slabs) * slab, slab)] = (
+        up_stage[mine, :])
+    a_wait(1)
+    a_start(5, 7)
+    a_wait(3)
+    a_start(6, 9)
+
+    others(lambda s: g_copy(me, s).wait_recv())
+    for head in range(local):
+        @pl.loop(0, count)
+        def _(s):
+            at = span(s * rows, rows)
+            g_pad[head, at, :] = low(jnp.where(lane_head == head, wide(g_heads[at, :]), 0.0))
+    k_acc[...] = jnp.zeros_like(k_acc)
+    v_acc[...] = jnp.zeros_like(v_acc)
+
+    def back_block(i):
+        at = span(i * QBLOCK, QBLOCK)
+        product = wide(g_heads[at, :]).T * o_turned[:, at]
+        deltas = [
+            jnp.sum(product[h * HEAD_DIM : (h + 1) * HEAD_DIM], axis=0, keepdims=True)
+            for h in range(local)
+        ]
+
+        def step(j, turned):
+            keys = span(j * QBLOCK, QBLOCK)
+            for head in range(local):
+                share = shares[head, keys, at]
+                grad_share = dot_nt(mixed[keys, values_at], g_pad[head, at, :])
+                grad_score = low(wide(share) * (grad_share - deltas[head]))
+                v_acc[keys, :] += dot(share, g_pad[head, at, :])
+                k_acc[keys, :] += dot(grad_score, q_pad[head, at, :])
+                turned = turned + dot_tn(k_pad[head, keys, :], grad_score)
+            return turned
+
+        turned = lax.fori_loop(0, i + 1, step, jnp.zeros((part, QBLOCK), f32))
+        mixed_grad[at, pl.ds(0, part)] = low((turned * factor).T)
+
+    pl.loop(0, query_blocks - 1)(back_block)
+    z_inner(1)
+    pl.loop(query_blocks - 1, query_blocks)(back_block)
+    mixed_grad[:, keys_at] = low(k_acc[...])
+    mixed_grad[:, values_at] = low(v_acc[...])
+    z_inner(2)
+
+    def s_copy(k, target, source):
+        return remote(
+            mixed_stage.at[span(target * rows, rows), pl.ds(k * part, part)],
+            own.at[span(mixed_at + k * rows, rows), span(source * part, part)],
+            s_send.at[k, target], s_recv.at[k, source], target)
+
+    def m_copy(k, target, source):
+        return remote(
+            mixed_grad.at[span(target * rows, rows), pl.ds(k * part, part)],
+            mixed_rows.at[:, span(k * width + source * part, part)],
+            m_send.at[k, target], m_recv.at[k, source], target)
+
+    @pl.loop(0, count)
+    def _(s):
+        at = span(s * rows, rows)
+        mixed_stage[at, :] = low(dot_tn(hidden1_all[:, at], mixed_grad[...]))
+
+        @pl.when(s != me)
+        def _():
+            for k in range(3):
+                s_copy(k, s, me).start()
+
+    for k in range(3):
+        own[span(mixed_at + k * rows, rows), span(me * part, part)] = (
+            mixed_stage[mine, pl.ds(k * part, part)])
+        mixed_rows[:, span(k * width + me * part, part)] = mixed_grad[mine, pl.ds(k * part, part)]
+
+    @pl.loop(1, count)
+    def _(step):
+        s = lax.rem(me + step, count)
+        for k in range(3):
+            m_copy(k, s, me).start()
+
+    z_inner(3)
+
+    a_wait(0, 2, 4)
+    a_start(8, 10)
+    a_wait(5, 6)
+    a_start(11, 12)
+    z_inner(2)
+    a_wait(7, 8, 9, 10, 11, 12)
+    own[pl.ds(out_at, part), :] = low(dot(low(o_turned[...]), attn_all[...]))
+    z_inner(up_at // ZROWS - z_done[0])
+
+    others(lambda s: u_copy(me, s).wait_recv())
+    z_outer(up_at // ZROWS, mixed_at // ZROWS)
+    z_inner((mixed_at - up_at) // ZROWS // 2)
+
+    for k in range(3):
+        others(lambda s: s_copy(k, me, s).wait_recv())
+    z_outer(mixed_at // ZROWS, chunks)
+    z_inner(mixed_at // ZROWS - z_done[0])
+
+    load_qkv.wait()
+    for k in range(3):
+        others(lambda s: m_copy(k, me, s).wait_recv())
+    acc_a[...] = jnp.zeros_like(acc_a)
+
+    @pl.loop(0, 3)
+    def _(k):
+        at = span(k * width, width)
+        acc_a[...] += dot_nt(mixed_rows[:, at], w_up[:, at])
+
+    frames_own = wide(frames_all[mine, :])
+    back1, gain1_part = norm_back(frames_own, norm_scale(frames_own), gain1, acc_a[...])
+    d_in_ref[...] = grad_mid[...] + back1
+
+    for s in range(count):
+        gain_out[s, 0:1, :] = gain1_part[:, s * part : (s + 1) * part]
+
+    def n_copy(target, source):
+        return remote(
+            gain_out.at[target], gain_in.at[source], n_send.at[target], n_recv.at[source], target)
+
+    def nz_copy(target, source):
+        return remote(
+            gain_z.at[source], gain_z.at[source], nz_send.at[target], nz_recv.at[source], me, target)
+
+    others(lambda s: n_copy(s, me).start())
+    gain_in[me] = gain_out[me]
+    z_inner(4)
+    others(lambda s: n_copy(me, s).wait_recv())
+    gain_sum = gain_in[0]
+    for s in range(1, count):
+        gain_sum = gain_sum + gain_in[s]
+    gain_z[plane] = gain_sum
+
+    @pl.loop(1, planes)
+    def _(step):
+        nz_copy(lax.rem(plane + step, planes), plane).start()
+
+    z_inner(chunks - z_done[0])
+
+    @pl.loop(1, planes)
+    def _(step):
+        nz_copy(plane, lax.rem(plane + step, planes)).wait_recv()
+
+    gain_sum = gain_z[0]
+    for p in range(1, planes):
+        gain_sum = gain_sum + gain_z[p]
+    gains_ref[...] = gain_sum
+
+    @pl.when(inner)
+    def _():
+        @pl.loop(chunks - ZLAG, chunks)
+        def _(c):
+            z_close(c)
+
+    for finish in (f_finish, c_finish, h_finish, a_finish):
+        finish()
+
+    @pl.loop(1, count)
+    def _(step):
+        s = lax.rem(me + step, count)
+        o_copy(s, me).wait_send()
+        g_copy(s, me).wait_send()
+        u_copy(s, me).wait_send()
+        n_copy(s, me).wait_send()
+        for k in range(3):
+            s_copy(k, s, me).wait_send()
+            m_copy(k, s, me).wait_send()
+
+    @pl.loop(1, planes)
+    def _(step):
+        nz_copy(lax.rem(plane + step, planes), plane).wait_send()
+
+    @pl.when(outer)
+    def _():
+        @pl.loop(0, chunks)
+        def _(c):
+            z_raw(c).wait_send()
+            z_back(c).wait_recv()
+
+    @pl.when(inner)
+    def _():
+        @pl.loop(0, chunks)
+        def _(c):
+            z_cross(c).wait_send()
+            z_back(c).wait_send()
+
+
+def shards_by_heads(frames, norm1_gain, w_qkv, w_out, norm2_gain, w_up, w_down, lengths, cotangent):
+    _, rows, width = frames.shape
+    ff = w_up.shape[1]
+    count, planes = lax.axis_size("sq"), lax.axis_size("dp")
+    total, part, slab = rows * count, width // count, ff // count
+    local = part // HEAD_DIM
+    bf16, f32 = jnp.bfloat16, jnp.float32
+    blocks = ff // width
+    own_rows = slab + rows * blocks + part + rows * 3
+    chunks = own_rows // ZROWS
+    vmem, anywhere = pl.BlockSpec(memory_space=pltpu.VMEM), pl.BlockSpec(memory_space=pl.ANY)
+    smem = pl.BlockSpec(memory_space=pltpu.SMEM)
+
+    def low_array(*shape):
+        return pltpu.VMEM(shape, bf16)
+
+    def wide_array(*shape):
+        return pltpu.VMEM(shape, f32)
+
+    def copies(*shape):
+        return pltpu.SemaphoreType.DMA(shape)
+
+    scratch = (
+        [low_array(total, width)] * 5
+        + [low_array(width, 3 * part), low_array(width, width), low_array(width, ff), low_array(ff, width)]
+        + [low_array(total, 3 * part)]
+        + [low_array(local, total, part)] * 4
+        + [low_array(local, total, total), wide_array(total, QBLOCK), wide_array(part, total)]
+        + [low_array(total, part), low_array(rows, width)]
+        + [wide_array(rows, width)] * 4
+        + [low_array(rows, width), low_array(total, part)]
+        + [low_array(total, slab)] * 3
+        + [low_array(total, 3 * part)] * 2
+        + [low_array(rows, 3 * width)]
+        + [wide_array(total, part)] * 2
+        + [low_array(own_rows, width)] * 2
+        + [wide_array(count, 8, part)] * 2
+        + [wide_array(planes, 8, part)]
+        + [copies(9), copies(4, 13), copies(4, 13)]
+        + [copies(count)] * 4
+        + [copies(3, count)] * 2
+        + [copies(count)] * 2
+        + [copies(3, count)] * 2
+        + [copies(count)] * 2
+        + [copies(planes)] * 2
+        + [copies(chunks)] * 5
+    )
+    result, d_in, gains, sums = pl.pallas_call(
+        functools.partial(layer_kernel, count, planes),
+        out_shape=(
+            jax.ShapeDtypeStruct((rows, width), bf16),
+            jax.ShapeDtypeStruct((rows, width), f32),
+            jax.ShapeDtypeStruct((8, part), f32),
+            jax.ShapeDtypeStruct((own_rows, width), bf16),
+        ),
+        in_specs=[anywhere, vmem, anywhere, anywhere, vmem, anywhere, anywhere, smem, anywhere],
+        out_specs=(vmem, vmem, vmem, vmem),
+        scratch_shapes=scratch,
+        compiler_params=pltpu.CompilerParams(
+            collective_id=0, has_side_effects=True, vmem_limit_bytes=60 * 2**20),
+    )(frames, norm1_gain[None], w_qkv, w_out, norm2_gain[None], w_up, w_down, lengths, cotangent)
+
+    def from_blocks(first, number):
+        pieces = sums[first : first + number * rows].reshape(number, rows, width)
+        return pieces.swapaxes(0, 1).reshape(rows, number * width).astype(f32)
+
+    grad_down = sums[:slab].astype(f32)
+    grad_up = from_blocks(slab, blocks)
+    grad_out = sums[slab + rows * blocks :][:part].astype(f32)
+    grad_qkv = from_blocks(slab + rows * blocks + part, 3)
+    return (result[None], d_in[None], gains[0], grad_qkv, grad_out, gains[1], grad_up, grad_down)
+
+
 def solution(mesh):
+    by_heads = HEADS % mesh.shape["sq"] == 0 and dict(mesh.shape) == {"dp": 4, "sq": 8}
     return jax.shard_map(
-        shards,
+        shards_by_heads if by_heads else shards_by_rows,
         mesh=mesh,
         in_specs=(
             P("dp", "sq", None),

time: 700 us -> 159 us (0.23)
  waiting for transfers between devices: 438 us -> 0 us
  Pallas kernels: 0 us -> 145 us
  matrix products: 103 us -> 0 us
  blocking collectives: 49.2 us -> 0 us
  local copies, waits for them, and re-layouts: 50.6 us -> 7.3 us
  other arithmetic: 35.8 us -> 5.21 us
  between operations: 15 us -> 0.68 us
    reduce_scatter x4 -> x0, waiting for transfers between devices: 302 us -> none  [the longest x1 118 us: shards(): lax.psum_scatter(grad_up, 'sq', scatter_dimension=0, tiled=True)]
    pallas_call x0 -> x1, Pallas kernels: none -> 145 us  [shards_by_heads(): pl.pallas_call(functools.partial(layer_kernel, count, planes), out_shape=...]
    dot_general x22 -> x0, matrix products: 103 us -> none  [the longest x4 31.4 us: contract_rows(): lax.dot_general(left, right, (((0,), (0,)), ((), ())), preferred_element_...]
    psum x1 -> x0, waiting for transfers between devices: 81.7 us -> none  [shards(): lax.psum(shares_sq[1].astype(jnp.bfloat16), 'dp').astype(jnp.float32)]
    all_gather x4 -> x0, waiting for transfers between devices: 52.5 us -> none  [the longest x1 26.5 us: shards(): lax.all_gather(value_rows, 'sq', axis=1, tiled=True)]
    all_gather x2 -> x0, blocking collectives: 23 us -> none  [the longest x1 15 us: shards(): lax.all_gather(delta_rows.astype(jnp.bfloat16), 'sq', axis=1, tiled=True)]
    convert_element_type x18 -> x2, other arithmetic: 22.8 us -> 4.97 us  [the longest x1 3.18 us: shards_by_heads(): grad_down = sums[:slab].astype(f32)]
    unnamed x94 -> x7, local copies, waits for them, and re-layouts: 17.1 us -> 3.12 us
  transfers between devices with their start and end apart: 9 -> 0, of which waited for: 6 -> 0; matrix products, arithmetic and copies ran while one was open for 24% -> 0% of each run, Pallas kernels for 0% -> 0%
where the time goes in v3:
time: 159 us
  Pallas kernels  145 us (91%)
  local copies, waits for them, and re-layouts  7.3 us (5%)
  other arithmetic  5.21 us (3%)
    pallas_call x1, Pallas kernels, shards_by_heads(): pl.pallas_call(functools.partial(layer_kernel, count, planes), out_shape=...  145 us

profile of v3, /device:TPU:0, one launch (start us, length us, event | category | flops | bytes accessed | tf_op | source)
XLA Modules:
  0.0 158.5 jit_solution(11776942980359096412)
XLA Ops:
  0.6 145.3 %shard_map.152 = (bf16[128,1024]{1,0:T(8,128)(2,1)}, f32[128,1024]{1,0:T(8,128)}, f32[8,128]{1,0:T(8,128)}, bf16[1536,1024]{1,0:T(8,128)(2,1)}) custom-call(bf16[1,128,1024]{2,1,0:T(8,128)(2,1)} %frames_in.1, f32[1,1024]{1,0:T(1,128)} %bitcast.25, bf16[1024,3072]{1,0:T(8,128)(2,1)} %w_qkv_in.1, bf16[1024,1024]{1,0:T(8,128)(2,1)} %w_out_in.1, ...), custom_call_target="tpu_custom_call" | custom-call | tf_op jit(solution)/shard_map/pallas_call | solution.py:1004
  146.0 1.3 slice_bitcast_fusion
  147.2 1.8 %slice_convert_fusion.1 = f32[128,1024]{1,0:T(8,128)} fusion(bf16[1536,1024]{1,0:T(8,128)(2,1)} %get-tuple-element.15), kind=kLoop, calls=%fused_computation.2 | loop fusion | flops 131072 | bytes 786432 | tf_op jit(solution)/shard_map/convert_element_type | solution.py:1025
  149.0 1.2 slice.21
  150.2 3.2 %slice_convert_fusion = (f32[512,1024]{1,0:T(8,128)}, bf16[512,1024]{1,0:T(8,128)(2,1)S(1)}) fusion(bf16[1536,1024]{1,0:T(8,128)(2,1)} %get-tuple-element.15), kind=kLoop, calls=%fused_computation.1 | loop fusion | flops 524288 | bytes 5242880 | tf_op jit(solution)/shard_map/convert_element_type | solution.py:1023
  153.4 0.3 copy.19
  153.7 1.6 %copy.21 = f32[128,3072]{1,0:T(8,128)} copy(f32[128,3072]{0,1:T(8,128)S(1)} %bitcast.19) | data formatting | bytes 3145728
  155.3 0.2 convert_bitcast_fusion
  155.5 0.0 copy-start.1
  155.5 0.0 copy-start
  155.6 1.5 copy.22
  157.0 0.0 copy-done.1
  157.0 0.7 copy.25
  157.7 0.0 copy-done
  157.7 0.8 copy.26
Async XLA Ops:
  155.5 1.5 copy-start.1
  155.5 2.2 %copy-start = (f32[128,1024]{1,0:T(8,128)S(1)}, f32[128,1024]{1,0:T(8,128)}, u32[]{:S(2)}) copy-start(f32[128,1024]{1,0:T(8,128)} %get-tuple-element.13) | copy-start | bytes 1572868

commit v4 on v3

--- a/solution.py
+++ b/solution.py
@@ -315,6 +315,7 @@
 ZROWS = 32
 ZLAG = 2
 QBLOCK = 256
+KEEP = pltpu.VMEM
 
 
 def dot(left, right):
@@ -371,13 +372,11 @@
     result_ref, d_in_ref, gains_ref, sum_ref,
     frames_all, hidden1_all, cot_all, hidden2_all, attn_all,
     w_heads, w_out, w_up, w_down,
-    mixed, q_pad, k_pad, v_pad, g_pad, shares, scores, o_turned, o_heads, o_rows,
+    mixed, q_pad, k_pad, v_pad, g_pad, shares, o_turned, o_heads, o_rows,
     middle, acc_a, acc_b, grad_mid, g_rows, g_heads,
-    active_s, slope_s, up_stage, mixed_grad, mixed_stage, mixed_rows, k_acc, v_acc,
+    active_s, slope_s, up_stage, mixed_grad, mixed_stage, mixed_rows,
     own, cross_in, gain_out, gain_in, gain_z,
-    load_sem, ag_send, ag_recv, o_send, o_recv, g_send, g_recv, m_send, m_recv,
-    u_send, u_recv, s_send, s_recv, n_send, n_recv, nz_send, nz_recv,
-    z_send, zb_send, z_raw_recv, z_cross_recv, z_back_recv,
+    load_sem, ag_send, ag_recv, swap_send, swap_recv, z_send, z_outer_recv, z_cross_recv,
 ):
     bf16, f32 = jnp.bfloat16, jnp.float32
     rows, width = result_ref.shape
@@ -445,13 +444,13 @@
 
     def slots(index):
         return [
-            (me, None, mate, mate),
-            (me, 0, over_x, over_x), (me, 1, over_x, over_x),
-            (me, 1, over_y, over_y), (me, 0, over_y, over_y),
-            (over_x, 0, over_y, corner), (over_y, 1, over_x, corner),
-            (over_x, 0, mate, flip(mate, 2)), (over_x, 1, mate, flip(mate, 2)),
-            (over_y, 1, mate, flip(mate, 4)), (over_y, 0, mate, flip(mate, 4)),
-            (corner, 0, mate, flip(corner, 1)), (corner, 1, mate, flip(corner, 1)),
+            (me, None, mate, mate, 0),
+            (me, 0, over_x, over_x, 1), (me, 1, over_x, over_x, 2),
+            (me, 1, over_y, over_y, 3), (me, 0, over_y, over_y, 4),
+            (over_x, 0, over_y, corner, 5), (over_y, 1, over_x, corner, 6),
+            (over_x, 0, mate, flip(mate, 2), 7), (over_x, 1, mate, flip(mate, 2), 7),
+            (over_y, 1, mate, flip(mate, 4), 8), (over_y, 0, mate, flip(mate, 4), 8),
+            (corner, 0, mate, flip(corner, 1), 9), (corner, 1, mate, flip(corner, 1), 9),
         ][index]
 
     def gather(number, array, source=None):
@@ -460,14 +459,13 @@
                 return span(block * rows, rows)
             return span(block * rows + which * half, half)
 
-        def copy(slot, sent=True):
-            block, which, target, arrives = slots(slot)
-            there = piece(block if sent else arrives, which)
+        def copy(slot, sent=True, whole=False):
+            block, which, target, arrives, sem = slots(slot)
+            there = piece(block if sent else arrives, None if whole else which)
             here = array.at[there]
             if sent and source is not None and slot < 5:
                 here = source if which is None else source.at[pl.ds(which * half, half)]
-            return remote(
-                here, array.at[there], ag_send.at[number, slot], ag_recv.at[number, slot], target)
+            return remote(here, array.at[there], ag_send.at[number], ag_recv.at[number, sem], target)
 
         def start(*numbers):
             for slot in numbers:
@@ -475,11 +473,24 @@
 
         def wait(*numbers):
             for slot in numbers:
-                copy(slot, sent=False).wait_recv()
+                copy(slot, sent=False, whole=slot >= 7).wait_recv()
 
         def finish():
-            for slot in range(13):
-                copy(slot).wait_send()
+            sent = array.at[pl.ds(0, (count - 1) * rows)]
+            remote(sent, sent, ag_send.at[number], ag_recv.at[number, 0], mate).wait_send()
+
+        return start, wait, finish
+
+    def swap(number, pairs, whole):
+        def start(target):
+            for source, dest in pairs(target, me):
+                remote(source, dest, swap_send.at[number], swap_recv.at[number], target).start()
+
+        def wait():
+            remote(whole, whole, swap_send.at[number], swap_recv.at[number], mate).wait_recv()
+
+        def finish():
+            remote(whole, whole, swap_send.at[number], swap_recv.at[number], mate).wait_send()
 
         return start, wait, finish
 
@@ -490,15 +501,15 @@
 
     def z_raw(c):
         at = span(c * ZROWS, ZROWS)
-        return remote(own.at[at], sum_ref.at[at], z_send.at[c], z_raw_recv.at[c], me, z_core)
+        return remote(own.at[at], sum_ref.at[at], z_send.at[0], z_outer_recv.at[c], me, z_core)
 
     def z_cross(c):
         at = span(c * ZROWS, ZROWS)
-        return remote(own.at[at], cross_in.at[at], z_send.at[c], z_cross_recv.at[c], me, z_mate)
+        return remote(own.at[at], cross_in.at[at], z_send.at[0], z_cross_recv.at[c], me, z_mate)
 
     def z_back(c):
         at = span(c * ZROWS, ZROWS)
-        return remote(sum_ref.at[at], sum_ref.at[at], zb_send.at[c], z_back_recv.at[c], me, z_edge)
+        return remote(sum_ref.at[at], sum_ref.at[at], z_send.at[1], z_outer_recv.at[c], me, z_edge)
 
     def z_join(c):
         at = span(c * ZROWS, ZROWS)
@@ -540,29 +551,34 @@
     f_start(0, 1, 3, 2, 4)
     for load in loads[5:]:
         load.start()
-    lane_head = lax.broadcasted_iota(jnp.int32, (rows, part), 1) // HEAD_DIM
+    pair = 2 * rows
+    lane_head = lax.broadcasted_iota(jnp.int32, (pair, part), 1) // HEAD_DIM
     gain1 = gain1_ref[...]
     gain2 = gain2_ref[...]
 
-    def qkv_block(block):
-        at = span(block * rows, rows)
+    def chip(index):
+        return span(lax.div(index, 2) * pair, pair)
+
+    def padded(ref, at, values):
+        for head in range(local):
+            ref[head, at, :] = low(jnp.where(lane_head == head, values, 0.0))
+
+    def qkv_chip(index):
+        at = chip(index)
         values = wide(frames_all[at, :])
         hidden = low(values * norm_scale(values) * gain1)
         hidden1_all[at, :] = hidden
         projected = low(dot(hidden, w_heads[...]))
         mixed[at, :] = projected
-        for head in range(local):
-            on = lane_head == head
-            q_pad[head, at, :] = low(jnp.where(on, wide(projected[:, :part]) * factor, 0.0))
-            k_pad[head, at, :] = low(jnp.where(on, wide(projected[:, part : 2 * part]), 0.0))
-            v_pad[head, at, :] = low(jnp.where(on, wide(projected[:, 2 * part :]), 0.0))
+        padded(q_pad, at, wide(projected[:, :part]) * factor)
+        padded(k_pad, at, wide(projected[:, part : 2 * part]))
+        padded(v_pad, at, wide(projected[:, 2 * part :]))
 
     loads[0].wait()
     for k in range(3):
         loads[2 + k].wait()
-    qkv_block(me)
     f_wait(0)
-    qkv_block(mate)
+    qkv_chip(me)
     f_wait(1)
     f_start(5, 7)
     f_wait(3)
@@ -570,21 +586,18 @@
     c_start(0, 1, 3, 2, 4)
     f_wait(2)
     f_start(8)
-    qkv_block(over_x)
     f_wait(4)
     f_start(10)
-    qkv_block(over_y)
-    f_wait(7, 8)
-    qkv_block(flip(mate, 2))
-    f_wait(9, 10)
-    qkv_block(flip(mate, 4))
+    f_wait(7)
+    qkv_chip(over_x)
+    f_wait(9)
+    qkv_chip(over_y)
     f_wait(5)
     f_start(11)
     f_wait(6)
     f_start(12)
-    qkv_block(corner)
-    f_wait(11, 12)
-    qkv_block(flip(corner, 1))
+    f_wait(11)
+    qkv_chip(corner)
 
     ends, running = [], None
     for item in range(lengths_ref.shape[1]):
@@ -597,48 +610,27 @@
     query_blocks = total // QBLOCK
     per_block = QBLOCK // rows
 
-    def o_copy(target, source):
-        return remote(
-            o_heads.at[span(target * rows, rows)], o_rows.at[:, span(source * part, part)],
-            o_send.at[target], o_recv.at[source], target)
-
-    @pl.loop(0, query_blocks)
-    def _(i):
-        at = span(i * QBLOCK, QBLOCK)
+    def o_pairs(target, source):
+        yield o_heads.at[span(target * rows, rows)], o_rows.at[:, span(source * part, part)]
+
+    o_start, o_wait, o_finish = swap(0, o_pairs, o_heads.at[pl.ds(0, total - rows)])
+
+    for i in range(query_blocks):
+        at, keys = pl.ds(i * QBLOCK, QBLOCK), pl.ds(0, (i + 1) * QBLOCK)
         query_pos = i * QBLOCK + lax.broadcasted_iota(jnp.int32, (1, QBLOCK), 1)
         begin = jnp.zeros((1, QBLOCK), jnp.int32)
         for end in ends:
             begin = jnp.maximum(begin, jnp.where(query_pos >= end, end, 0))
-        turned = jnp.zeros((part, QBLOCK), f32)
+        key_pos = lax.broadcasted_iota(jnp.int32, ((i + 1) * QBLOCK, 1), 0)
+        mask = (key_pos <= query_pos) & (key_pos >= begin)
+        turned = None
         for head in range(local):
-            queries = q_pad[head, at, :]
-
-            def score(j, top):
-                keys = span(j * QBLOCK, QBLOCK)
-                key_pos = j * QBLOCK + lax.broadcasted_iota(jnp.int32, (QBLOCK, 1), 0)
-                value = dot_nt(mixed[keys, keys_at], queries)
-                value = jnp.where((key_pos <= query_pos) & (key_pos >= begin), value, NEG_FILL)
-                scores[keys, :] = value
-                return jnp.maximum(top, jnp.max(value, axis=0, keepdims=True))
-
-            top = lax.fori_loop(0, i + 1, score, jnp.full((1, QBLOCK), START_MAX, f32))
-
-            def weigh(j, weight_sum):
-                keys = span(j * QBLOCK, QBLOCK)
-                weight = jnp.exp(scores[keys, :] - top)
-                scores[keys, :] = weight
-                return weight_sum + jnp.sum(weight, axis=0, keepdims=True)
-
-            weight_sum = lax.fori_loop(0, i + 1, weigh, jnp.zeros((1, QBLOCK), f32))
-            over = 1.0 / weight_sum
-
-            def attend(j, accum):
-                keys = span(j * QBLOCK, QBLOCK)
-                share = low(scores[keys, :] * over)
-                shares[head, keys, at] = share
-                return accum + dot_tn(v_pad[head, keys, :], share)
-
-            turned = lax.fori_loop(0, i + 1, attend, turned)
+            score = jnp.where(mask, dot_nt(mixed[keys, keys_at], q_pad[head, at, :]), NEG_FILL)
+            weight = jnp.exp(score - jnp.max(score, axis=0, keepdims=True))
+            share = low(weight * (1.0 / jnp.sum(weight, axis=0, keepdims=True)))
+            shares[head, keys, at] = share
+            value = dot_tn(v_pad[head, keys, :], share)
+            turned = value if turned is None else turned + value
         o_turned[:, at] = turned
         o_heads[at, :] = low(turned.T)
         for k in range(per_block):
@@ -646,7 +638,7 @@
 
             @pl.when(target != me)
             def _():
-                o_copy(target, me).start()
+                o_start(target)
 
             @pl.when(target == me)
             def _():
@@ -657,13 +649,16 @@
     c_wait(3)
     c_start(6, 9)
     loads[5].wait()
-    others(lambda s: o_copy(me, s).wait_recv())
+    o_wait()
     middle_own = wide(frames_all[mine, :]) + dot(o_rows[...], w_out[...])
     middle[...] = middle_own
-    hidden2_own = low(middle_own * norm_scale(middle_own) * gain2)
-    hidden2_all[mine, :] = hidden2_own
+    hidden2_all[mine, :] = low(middle_own * norm_scale(middle_own) * gain2)
     h_start(0, 1, 3, 2, 4)
 
+    c_wait(2)
+    c_start(8)
+    c_wait(4)
+    c_start(10)
     loads[1].wait()
     loads[6].wait()
     loads[7].wait()
@@ -671,20 +666,69 @@
     acc_b[...] = jnp.zeros_like(acc_b)
 
     def ff_tile(t):
-        at = span(t * slab, slab)
+        at = span(t * width, width)
         active, slope = gelu_parts(dot(hidden2_all[mine, :], w_up[:, at]))
         acc_a[...] += dot(low(active), w_down[at, :])
         grad = low(dot_nt(cot_all[mine, :], w_down[at, :]) * slope)
         acc_b[...] += dot_nt(grad, w_up[:, at])
 
-    pl.loop(0, count // 2)(ff_tile)
+    tiles = ff // width
+    pl.loop(0, tiles // 2)(ff_tile)
     h_wait(1)
     h_start(5, 7)
     h_wait(3)
     h_start(6, 9)
-    pl.loop(count // 2, count)(ff_tile)
+    c_wait(5)
+    c_start(11)
+    c_wait(6)
+    c_start(12)
+    pl.loop(tiles // 2, tiles - 1)(ff_tile)
+    h_wait(2)
+    h_start(8)
+    h_wait(4)
+    h_start(10)
+    pl.loop(tiles - 1, tiles)(ff_tile)
+    h_wait(5)
+    h_start(11)
+    h_wait(6)
+    h_start(12)
+
+    slab_at = span(me * slab, slab)
+
+    def slab_chip(index):
+        at = chip(index)
+        active, slope = gelu_parts(dot(hidden2_all[at, :], w_up[:, slab_at]))
+        active_s[at, :] = low(active)
+        slope_s[at, :] = low(slope)
+
+    h_wait(0)
+    slab_chip(me)
+    h_wait(7)
+    slab_chip(over_x)
+    h_wait(9)
+    slab_chip(over_y)
+    h_wait(11)
+    slab_chip(corner)
+    load_qkv.start()
+    c_wait(0, 7, 9, 11)
+
+    down_rows, up_rows = slab, rows * (ff // width)
+    down_at, up_at = 0, down_rows
+    out_at = up_at + up_rows
+    mixed_at = out_at + part
+    slabs = width // slab
+
+    @pl.loop(0, slab // part)
+    def _(t):
+        at = span(down_at + t * part, part)
+        own[at, :] = low(dot_tn(active_s[:, span(t * part, part)], cot_all[...]))
+
+        @pl.when(outer)
+        def _():
+            for c in range(part // ZROWS):
+                z_raw(t * (part // ZROWS) + c).start()
+
     result_ref[...] = low(acc_a[...])
-
     middle_own = middle[...]
     back2, gain2_part = norm_back(middle_own, norm_scale(middle_own), gain2, acc_b[...])
     gain_out[...] = jnp.zeros_like(gain_out)
@@ -696,179 +740,139 @@
     attn_all[mine, :] = attn_own
     g_rows[...] = low(dot_nt(attn_own, w_out[...]))
 
-    def g_copy(target, source):
-        return remote(
-            g_rows.at[:, span(target * part, part)], g_heads.at[span(source * rows, rows)],
-            g_send.at[target], g_recv.at[source], target)
-
-    others(lambda s: g_copy(s, me).start())
+    def g_pairs(target, source):
+        yield g_rows.at[:, span(target * part, part)], g_heads.at[span(source * rows, rows)]
+
+    g_start, g_wait, g_finish = swap(1, g_pairs, g_heads.at[pl.ds(0, total - rows)])
+    others(g_start)
     g_heads[mine, :] = g_rows[:, span(me * part, part)]
-    a_start(0, 1, 3, 2, 4)
-
-    slab_at = span(me * slab, slab)
-
-    def slab_block(block):
-        at = span(block * rows, rows)
-        active, slope = gelu_parts(dot(hidden2_all[at, :], w_up[:, slab_at]))
-        active_s[at, :] = low(active)
-        slope_s[at, :] = low(dot_nt(cot_all[at, :], w_down[slab_at, :]) * slope)
-
-    slab_block(me)
-    c_wait(0)
-    h_wait(0)
-    slab_block(mate)
-    c_wait(2, 4)
-    c_start(8, 10)
-    h_wait(2, 4)
-    h_start(8, 10)
-    slab_block(over_x)
-    slab_block(over_y)
-    c_wait(7, 8)
-    h_wait(7, 8)
-    slab_block(flip(mate, 2))
-    c_wait(9, 10)
-    h_wait(9, 10)
-    slab_block(flip(mate, 4))
-    c_wait(5, 6)
-    c_start(11, 12)
-    h_wait(5, 6)
-    h_start(11, 12)
-    slab_block(corner)
-    c_wait(11, 12)
-    h_wait(11, 12)
-    slab_block(flip(corner, 1))
-    load_qkv.start()
-
-    down_rows, up_rows = slab, rows * (ff // width)
-    down_at, up_at = 0, down_rows
-    out_at = up_at + up_rows
-    mixed_at = out_at + part
-    slabs = width // slab
-
-    @pl.loop(0, slab // part)
-    def _(t):
-        own[span(down_at + t * part, part), :] = low(
-            dot_tn(active_s[:, span(t * part, part)], cot_all[...]))
-
-    z_outer(0, up_at // ZROWS)
-
-    def u_copy(target, source):
-        return remote(
+
+    for c in range(0, count, 2):
+        at = span(c * rows, pair)
+        slope_s[at, :] = low(dot_nt(cot_all[at, :], w_down[slab_at, :]) * wide(slope_s[at, :]))
+
+    def u_pairs(target, source):
+        yield (
             up_stage.at[span(target * rows, rows)],
             own.at[span(up_at + lax.div(source, slabs) * rows, rows),
                    span(lax.rem(source, slabs) * slab, slab)],
-            u_send.at[target], u_recv.at[source], target)
-
-    @pl.loop(0, count)
-    def _(s):
-        at = span(s * rows, rows)
+        )
+
+    u_start, u_wait, u_finish = swap(2, u_pairs, up_stage.at[pl.ds(0, total - rows)])
+    z_inner(1)
+
+    @pl.loop(0, count // 2)
+    def _(c):
+        at = span(c * pair, pair)
         up_stage[at, :] = low(dot_tn(hidden2_all[:, at], slope_s[...]))
-
-        @pl.when(s != me)
-        def _():
-            u_copy(s, me).start()
+        for s in (2 * c, 2 * c + 1):
+            @pl.when(s != me)
+            def _():
+                u_start(s)
 
     own[span(up_at + lax.div(me, slabs) * rows, rows), span(lax.rem(me, slabs) * slab, slab)] = (
         up_stage[mine, :])
+    a_start(0, 1, 3, 2, 4)
+    z_inner(2)
+
+    g_wait()
+    for c in range(count // 2):
+        at = span(c * pair, pair)
+        padded(g_pad, at, wide(g_heads[at, :]))
+
+    def late(j):
+        return pl.ds(j * QBLOCK, total - j * QBLOCK)
+
+    for j in range(query_blocks):
+        keys = pl.ds(j * QBLOCK, QBLOCK)
+        grad = None
+        for head in range(local):
+            value = dot(shares[head, keys, late(j)], g_pad[head, late(j), :])
+            grad = value if grad is None else grad + value
+        mixed_grad[keys, values_at] = low(grad)
+    z_inner(2)
+    for i in range(query_blocks):
+        at, keys = pl.ds(i * QBLOCK, QBLOCK), pl.ds(0, (i + 1) * QBLOCK)
+        product = wide(g_heads[at, :]).T * o_turned[:, at]
+        turned = None
+        for head in range(local):
+            delta = jnp.sum(
+                product[head * HEAD_DIM : (head + 1) * HEAD_DIM], axis=0, keepdims=True)
+            grad_share = dot_nt(mixed[keys, values_at], g_pad[head, at, :])
+            grad_score = low(wide(shares[head, keys, at]) * (grad_share - delta))
+            shares[head, keys, at] = grad_score
+            value = dot_tn(k_pad[head, keys, :], grad_score)
+            turned = value if turned is None else turned + value
+        mixed_grad[at, pl.ds(0, part)] = low((turned * factor).T)
+        z_inner(1)
+    for j in range(query_blocks):
+        keys = pl.ds(j * QBLOCK, QBLOCK)
+        grad = None
+        for head in range(local):
+            value = dot(shares[head, keys, late(j)], q_pad[head, late(j), :])
+            grad = value if grad is None else grad + value
+        mixed_grad[keys, keys_at] = low(grad)
+    z_inner(2)
+
+    def s_pairs(target, source):
+        for k in range(3):
+            yield (
+                mixed_stage.at[span(target * rows, rows), pl.ds(k * part, part)],
+                own.at[span(mixed_at + k * rows, rows), span(source * part, part)],
+            )
+
+    def m_pairs(target, source):
+        for k in range(3):
+            yield (
+                mixed_grad.at[span(target * rows, rows), pl.ds(k * part, part)],
+                mixed_rows.at[:, span(k * width + source * part, part)],
+            )
+
+    s_start, s_wait, s_finish = swap(3, s_pairs, mixed_stage.at[pl.ds(0, total - rows)])
+    m_start, m_wait, m_finish = swap(4, m_pairs, mixed_grad.at[pl.ds(0, total - rows)])
+
+    @pl.loop(0, count // 2)
+    def _(c):
+        at = span(c * pair, pair)
+        mixed_stage[at, :] = low(dot_tn(hidden1_all[:, at], mixed_grad[...]))
+        for s in (2 * c, 2 * c + 1):
+            @pl.when(s != me)
+            def _():
+                s_start(s)
+
+    for k in range(3):
+        own[span(mixed_at + k * rows, rows), span(me * part, part)] = (
+            mixed_stage[mine, pl.ds(k * part, part)])
+        mixed_rows[:, span(k * width + me * part, part)] = mixed_grad[mine, pl.ds(k * part, part)]
     a_wait(1)
     a_start(5, 7)
     a_wait(3)
     a_start(6, 9)
-
-    others(lambda s: g_copy(me, s).wait_recv())
-    for head in range(local):
-        @pl.loop(0, count)
-        def _(s):
-            at = span(s * rows, rows)
-            g_pad[head, at, :] = low(jnp.where(lane_head == head, wide(g_heads[at, :]), 0.0))
-    k_acc[...] = jnp.zeros_like(k_acc)
-    v_acc[...] = jnp.zeros_like(v_acc)
-
-    def back_block(i):
-        at = span(i * QBLOCK, QBLOCK)
-        product = wide(g_heads[at, :]).T * o_turned[:, at]
-        deltas = [
-            jnp.sum(product[h * HEAD_DIM : (h + 1) * HEAD_DIM], axis=0, keepdims=True)
-            for h in range(local)
-        ]
-
-        def step(j, turned):
-            keys = span(j * QBLOCK, QBLOCK)
-            for head in range(local):
-                share = shares[head, keys, at]
-                grad_share = dot_nt(mixed[keys, values_at], g_pad[head, at, :])
-                grad_score = low(wide(share) * (grad_share - deltas[head]))
-                v_acc[keys, :] += dot(share, g_pad[head, at, :])
-                k_acc[keys, :] += dot(grad_score, q_pad[head, at, :])
-                turned = turned + dot_tn(k_pad[head, keys, :], grad_score)
-            return turned
-
-        turned = lax.fori_loop(0, i + 1, step, jnp.zeros((part, QBLOCK), f32))
-        mixed_grad[at, pl.ds(0, part)] = low((turned * factor).T)
-
-    pl.loop(0, query_blocks - 1)(back_block)
-    z_inner(1)
-    pl.loop(query_blocks - 1, query_blocks)(back_block)
-    mixed_grad[:, keys_at] = low(k_acc[...])
-    mixed_grad[:, values_at] = low(v_acc[...])
+    a_wait(2)
+    a_start(8)
+    a_wait(4)
+    a_start(10)
+    others(m_start)
     z_inner(2)
-
-    def s_copy(k, target, source):
-        return remote(
-            mixed_stage.at[span(target * rows, rows), pl.ds(k * part, part)],
-            own.at[span(mixed_at + k * rows, rows), span(source * part, part)],
-            s_send.at[k, target], s_recv.at[k, source], target)
-
-    def m_copy(k, target, source):
-        return remote(
-            mixed_grad.at[span(target * rows, rows), pl.ds(k * part, part)],
-            mixed_rows.at[:, span(k * width + source * part, part)],
-            m_send.at[k, target], m_recv.at[k, source], target)
-
-    @pl.loop(0, count)
-    def _(s):
-        at = span(s * rows, rows)
-        mixed_stage[at, :] = low(dot_tn(hidden1_all[:, at], mixed_grad[...]))
-
-        @pl.when(s != me)
-        def _():
-            for k in range(3):
-                s_copy(k, s, me).start()
-
-    for k in range(3):
-        own[span(mixed_at + k * rows, rows), span(me * part, part)] = (
-            mixed_stage[mine, pl.ds(k * part, part)])
-        mixed_rows[:, span(k * width + me * part, part)] = mixed_grad[mine, pl.ds(k * part, part)]
-
-    @pl.loop(1, count)
-    def _(step):
-        s = lax.rem(me + step, count)
-        for k in range(3):
-            m_copy(k, s, me).start()
-
-    z_inner(3)
-
-    a_wait(0, 2, 4)
-    a_start(8, 10)
-    a_wait(5, 6)
-    a_start(11, 12)
+    u_wait()
+    z_outer(up_at // ZROWS, out_at // ZROWS)
     z_inner(2)
-    a_wait(7, 8, 9, 10, 11, 12)
+
+    a_wait(5)
+    a_start(11)
+    a_wait(6)
+    a_start(12)
+    z_inner(2)
+    a_wait(0, 7, 9, 11)
     own[pl.ds(out_at, part), :] = low(dot(low(o_turned[...]), attn_all[...]))
-    z_inner(up_at // ZROWS - z_done[0])
-
-    others(lambda s: u_copy(me, s).wait_recv())
-    z_outer(up_at // ZROWS, mixed_at // ZROWS)
-    z_inner((mixed_at - up_at) // ZROWS // 2)
-
-    for k in range(3):
-        others(lambda s: s_copy(k, me, s).wait_recv())
+    z_outer(out_at // ZROWS, mixed_at // ZROWS)
+    z_inner(4)
+    s_wait()
     z_outer(mixed_at // ZROWS, chunks)
-    z_inner(mixed_at // ZROWS - z_done[0])
+    z_inner(6)
 
     load_qkv.wait()
-    for k in range(3):
-        others(lambda s: m_copy(k, me, s).wait_recv())
+    m_wait()
     acc_a[...] = jnp.zeros_like(acc_a)
 
     @pl.loop(0, 3)
@@ -879,22 +883,24 @@
     frames_own = wide(frames_all[mine, :])
     back1, gain1_part = norm_back(frames_own, norm_scale(frames_own), gain1, acc_a[...])
     d_in_ref[...] = grad_mid[...] + back1
+    z_inner(2)
 
     for s in range(count):
         gain_out[s, 0:1, :] = gain1_part[:, s * part : (s + 1) * part]
 
-    def n_copy(target, source):
-        return remote(
-            gain_out.at[target], gain_in.at[source], n_send.at[target], n_recv.at[source], target)
+    def n_pairs(target, source):
+        yield gain_out.at[target], gain_in.at[source]
+
+    n_start, n_wait, n_finish = swap(5, n_pairs, gain_out.at[pl.ds(0, count - 1)])
 
     def nz_copy(target, source):
         return remote(
-            gain_z.at[source], gain_z.at[source], nz_send.at[target], nz_recv.at[source], me, target)
-
-    others(lambda s: n_copy(s, me).start())
+            gain_z.at[source], gain_z.at[source], swap_send.at[6], swap_recv.at[6], me, target)
+
+    others(n_start)
     gain_in[me] = gain_out[me]
     z_inner(4)
-    others(lambda s: n_copy(me, s).wait_recv())
+    n_wait()
     gain_sum = gain_in[0]
     for s in range(1, count):
         gain_sum = gain_sum + gain_in[s]
@@ -905,11 +911,9 @@
         nz_copy(lax.rem(plane + step, planes), plane).start()
 
     z_inner(chunks - z_done[0])
-
-    @pl.loop(1, planes)
-    def _(step):
-        nz_copy(plane, lax.rem(plane + step, planes)).wait_recv()
-
+    gains_all = gain_z.at[pl.ds(0, planes - 1)]
+    all_gains = remote(gains_all, gains_all, swap_send.at[6], swap_recv.at[6], mate)
+    all_gains.wait_recv()
     gain_sum = gain_z[0]
     for p in range(1, planes):
         gain_sum = gain_sum + gain_z[p]
@@ -921,37 +925,58 @@
         def _(c):
             z_close(c)
 
-    for finish in (f_finish, c_finish, h_finish, a_finish):
+    for finish in (
+        f_finish, c_finish, h_finish, a_finish,
+        o_finish, g_finish, u_finish, s_finish, m_finish, n_finish,
+    ):
         finish()
-
-    @pl.loop(1, count)
-    def _(step):
-        s = lax.rem(me + step, count)
-        o_copy(s, me).wait_send()
-        g_copy(s, me).wait_send()
-        u_copy(s, me).wait_send()
-        n_copy(s, me).wait_send()
-        for k in range(3):
-            s_copy(k, s, me).wait_send()
-            m_copy(k, s, me).wait_send()
-
-    @pl.loop(1, planes)
-    def _(step):
-        nz_copy(lax.rem(plane + step, planes), plane).wait_send()
+    all_gains.wait_send()
 
     @pl.when(outer)
     def _():
+        remote(own, own, z_send.at[0], z_outer_recv.at[0], me, z_core).wait_send()
+
         @pl.loop(0, chunks)
         def _(c):
-            z_raw(c).wait_send()
             z_back(c).wait_recv()
 
     @pl.when(inner)
     def _():
-        @pl.loop(0, chunks)
-        def _(c):
-            z_cross(c).wait_send()
-            z_back(c).wait_send()
+        remote(own, own, z_send.at[0], z_outer_recv.at[0], me, z_mate).wait_send()
+        remote(own, own, z_send.at[1], z_outer_recv.at[0], me, z_edge).wait_send()
+
+
+def finish_kernel(
+    result_in, d_in_in, gains_in, sum_in,
+    result_ref, d_in_ref, gain1_ref, qkv_ref, out_ref, gain2_ref, up_ref, down_ref,
+    staged, gains, sems,
+):
+    rows, width = result_in.shape
+    slab, part = down_ref.shape[0], out_ref.shape[0]
+    targets = [down_ref]
+    starts = [0]
+    sizes = [slab]
+    for ref, tall in ((up_ref, rows), (out_ref, part), (qkv_ref, rows)):
+        for k in range(ref.shape[1] // width):
+            starts.append(starts[-1] + sizes[-1])
+            sizes.append(tall)
+            targets.append(ref.at[:, pl.ds(k * width, width)])
+    copies = [
+        pltpu.make_async_copy(result_in, result_ref.at[0], sems.at[0]),
+        pltpu.make_async_copy(d_in_in, d_in_ref.at[0], sems.at[1]),
+    ]
+    for copy in copies:
+        copy.start()
+    for k, (first, size, target) in enumerate(zip(starts, sizes, targets)):
+        at = pl.ds(first, size)
+        staged[at, :] = sum_in[at, :].astype(jnp.float32)
+        copy = pltpu.make_async_copy(staged.at[at], target, sems.at[2 + k])
+        copy.start()
+        copies.append(copy)
+    gain1_ref[...] = gains_in[0]
+    gain2_ref[...] = gains_in[1]
+    for copy in copies:
+        copy.wait()
 
 
 def shards_by_heads(frames, norm1_gain, w_qkv, w_out, norm2_gain, w_up, w_down, lengths, cotangent):
@@ -981,33 +1006,26 @@
         + [low_array(width, 3 * part), low_array(width, width), low_array(width, ff), low_array(ff, width)]
         + [low_array(total, 3 * part)]
         + [low_array(local, total, part)] * 4
-        + [low_array(local, total, total), wide_array(total, QBLOCK), wide_array(part, total)]
+        + [low_array(local, total, total), wide_array(part, total)]
         + [low_array(total, part), low_array(rows, width)]
         + [wide_array(rows, width)] * 4
         + [low_array(rows, width), low_array(total, part)]
         + [low_array(total, slab)] * 3
         + [low_array(total, 3 * part)] * 2
         + [low_array(rows, 3 * width)]
-        + [wide_array(total, part)] * 2
         + [low_array(own_rows, width)] * 2
         + [wide_array(count, 8, part)] * 2
         + [wide_array(planes, 8, part)]
-        + [copies(9), copies(4, 13), copies(4, 13)]
-        + [copies(count)] * 4
-        + [copies(3, count)] * 2
-        + [copies(count)] * 2
-        + [copies(3, count)] * 2
-        + [copies(count)] * 2
-        + [copies(planes)] * 2
-        + [copies(chunks)] * 5
-    )
-    result, d_in, gains, sums = pl.pallas_call(
+        + [copies(9), copies(4), copies(4, 10), copies(7), copies(7), copies(2)]
+        + [copies(chunks)] * 2
+    )
+    kept = pl.pallas_call(
         functools.partial(layer_kernel, count, planes),
         out_shape=(
-            jax.ShapeDtypeStruct((rows, width), bf16),
-            jax.ShapeDtypeStruct((rows, width), f32),
-            jax.ShapeDtypeStruct((8, part), f32),
-            jax.ShapeDtypeStruct((own_rows, width), bf16),
+            KEEP((rows, width), bf16),
+            KEEP((rows, width), f32),
+            KEEP((8, part), f32),
+            KEEP((own_rows, width), bf16),
         ),
         in_specs=[anywhere, vmem, anywhere, anywhere, vmem, anywhere, anywhere, smem, anywhere],
         out_specs=(vmem, vmem, vmem, vmem),
@@ -1015,16 +1033,21 @@
         compiler_params=pltpu.CompilerParams(
             collective_id=0, has_side_effects=True, vmem_limit_bytes=60 * 2**20),
     )(frames, norm1_gain[None], w_qkv, w_out, norm2_gain[None], w_up, w_down, lengths, cotangent)
-
-    def from_blocks(first, number):
-        pieces = sums[first : first + number * rows].reshape(number, rows, width)
-        return pieces.swapaxes(0, 1).reshape(rows, number * width).astype(f32)
-
-    grad_down = sums[:slab].astype(f32)
-    grad_up = from_blocks(slab, blocks)
-    grad_out = sums[slab + rows * blocks :][:part].astype(f32)
-    grad_qkv = from_blocks(slab + rows * blocks + part, 3)
-    return (result[None], d_in[None], gains[0], grad_qkv, grad_out, gains[1], grad_up, grad_down)
+    return pl.pallas_call(
+        finish_kernel,
+        out_shape=tuple(
+            jax.ShapeDtypeStruct(shape, kind)
+            for shape, kind in (
+                ((1, rows, width), bf16), ((1, rows, width), f32), ((part,), f32),
+                ((part, 3 * width), f32), ((part, width), f32), ((part,), f32),
+                ((part, ff), f32), ((slab, width), f32),
+            )
+        ),
+        in_specs=[vmem] * 4,
+        out_specs=(anywhere, anywhere, vmem, anywhere, anywhere, vmem, anywhere, anywhere),
+        scratch_shapes=[wide_array(own_rows, width), wide_array(8, part), copies(11)],
+        compiler_params=pltpu.CompilerParams(vmem_limit_bytes=24 * 2**20),
+    )(*kept)
 
 
 def solution(mesh):

time: 159 us -> 140 us (0.88); the launches traced: 159 us -> 137 us
  Pallas kernels: 145 us -> 137 us
  local copies, waits for them, and re-layouts: 7.3 us -> 0 us
  other arithmetic: 5.21 us -> 0 us
    pallas_call x1, Pallas kernels: 145 us -> 133 us  [shards_by_heads(): pl.pallas_call(functools.partial(layer_kernel, count, planes), out_shape=...]
    convert_element_type x2 -> x0, other arithmetic: 4.97 us -> none  [the longest x1 3.18 us: shards_by_heads(): grad_down = sums[:slab].astype(f32)]
    pallas_call x0 -> x1, Pallas kernels: none -> 3.5 us  [shards_by_heads(): pl.pallas_call(finish_kernel, out_shape=tuple((jax.ShapeDtypeStruct(shape...]
    unnamed x7 -> x0, local copies, waits for them, and re-layouts: 3.12 us -> none
    convert_element_type x2 -> x0, local copies, waits for them, and re-layouts: 1.72 us -> none  [from_blocks(): return pieces.swapaxes(0, 1).reshape(rows, number * width).astype(f32)]
where the time goes in v4:
time: 140 us; the launch traced here: 137 us
  Pallas kernels  137 us (98%)
    pallas_call x1, Pallas kernels, shards_by_heads(): pl.pallas_call(functools.partial(layer_kernel, count, planes), out_shape=...  133 us
    pallas_call x1, Pallas kernels, shards_by_heads(): pl.pallas_call(finish_kernel, out_shape=tuple((jax.ShapeDtypeStruct(shape...  3.5 us

profile of v4, /device:TPU:0, one launch (start us, length us, event | category | flops | bytes accessed | tf_op | source)
XLA Modules:
  0.0 137.4 jit_solution(6652122986635447399)
XLA Ops:
  0.6 133.1 %shard_map.152 = (bf16[128,1024]{1,0:T(8,128)(2,1)S(1)}, f32[128,1024]{1,0:T(8,128)S(1)}, f32[8,128]{1,0:T(8,128)S(1)}, bf16[1536,1024]{1,0:T(8,128)(2,1)S(1)}) custom-call(bf16[1,128,1024]{2,1,0:T(8,128)(2,1)} %frames_in.1, f32[1,1024]{1,0:T(1,128)} %bitcast.2, bf16[1024,3072]{1,0:T(8,128)(2,1)} %w_qkv_in.1, bf16[1024,1024]{1,0:T(8,128)(2,1)} %w_out_in.1, ...), custom_call_target="tpu_custom_call" | custom-call | tf_op jit(solution)/shard_map/pallas_call | solution.py:1022
  133.7 3.5 %shard_map.153 = (bf16[1,128,1024]{2,1,0:T(8,128)(2,1)}, f32[1,128,1024]{2,1,0:T(8,128)}, f32[128]{0:T(128)}, f32[128,3072]{1,0:T(8,128)}, f32[128,1024]{1,0:T(8...) custom-call(bf16[128,1024]{1,0:T(8,128)(2,1)S(1)} %get-tuple-element.12.result_in, ...), custom_call_target="tpu_custom_call" | custom-call | tf_op jit(solution)/shard_map/pallas_call | solution.py:1036

commit v5 on v4

--- a/solution.py
+++ b/solution.py
@@ -313,7 +313,7 @@
 
 MESH = pl.DeviceIdType.MESH
 ZROWS = 32
-ZLAG = 2
+ZLAG = 3
 QBLOCK = 256
 KEEP = pltpu.VMEM
 
@@ -371,7 +371,7 @@
     frames_in, gain1_ref, w_qkv_in, w_out_in, gain2_ref, w_up_in, w_down_in, lengths_ref, cot_in,
     result_ref, d_in_ref, gains_ref, sum_ref,
     frames_all, hidden1_all, cot_all, hidden2_all, attn_all,
-    w_heads, w_out, w_up, w_down,
+    w_heads, w_out, w_up, w_down, w_up_s, w_down_s, active_rows, slope_rows,
     mixed, q_pad, k_pad, v_pad, g_pad, shares, o_turned, o_heads, o_rows,
     middle, acc_a, acc_b, grad_mid, g_rows, g_heads,
     active_s, slope_s, up_stage, mixed_grad, mixed_stage, mixed_rows,
@@ -424,9 +424,34 @@
         for k in range(3)
     ] + [
         pltpu.make_async_copy(w_out_in, w_out, load_sem.at[5]),
-        pltpu.make_async_copy(w_up_in, w_up, load_sem.at[6]),
-        pltpu.make_async_copy(w_down_in, w_down, load_sem.at[7]),
+        pltpu.make_async_copy(w_up_in.at[:, span(me * slab, slab)], w_up_s, load_sem.at[6]),
+        pltpu.make_async_copy(w_down_in.at[span(me * slab, slab)], w_down_s, load_sem.at[7]),
     ]
+
+    def load_up(wait=False):
+        if wait:
+            pltpu.make_async_copy(w_up_in, w_up, load_sem.at[9]).wait()
+            return
+
+        @pl.loop(0, ff // part)
+        def _(n):
+            k, s = lax.div(n, count), lax.rem(n, count)
+            pltpu.make_async_copy(
+                w_up_in.at[:, span(s * slab + k * part, part)],
+                w_up.at[:, span(k * width + s * part, part)], load_sem.at[9]).start()
+
+    def load_down(wait=False):
+        if wait:
+            pltpu.make_async_copy(w_down_in, w_down, load_sem.at[10]).wait()
+            return
+
+        @pl.loop(0, ff // part)
+        def _(n):
+            k, s = lax.div(n, count), lax.rem(n, count)
+            pltpu.make_async_copy(
+                w_down_in.at[span(s * slab + k * part, part)],
+                w_down.at[span(k * width + s * part, part)], load_sem.at[10]).start()
+
     load_qkv = pltpu.make_async_copy(w_qkv_in, w_up.at[:, pl.ds(0, 3 * width)], load_sem.at[8])
     for load in loads[:5]:
         load.start()
@@ -541,6 +566,10 @@
                     z_join(c)
                     z_close(c - ZLAG)
 
+    def z_upto(number):
+        if number > z_done[0]:
+            z_inner(number - z_done[0])
+
     def z_outer(first, last):
         @pl.when(outer)
         def _():
@@ -549,8 +578,11 @@
                 z_raw(c).start()
 
     f_start(0, 1, 3, 2, 4)
-    for load in loads[5:]:
-        load.start()
+    loads[5].start()
+    load_up()
+    load_down()
+    loads[6].start()
+    loads[7].start()
     pair = 2 * rows
     lane_head = lax.broadcasted_iota(jnp.int32, (pair, part), 1) // HEAD_DIM
     gain1 = gain1_ref[...]
@@ -631,6 +663,11 @@
             shares[head, keys, at] = share
             value = dot_tn(v_pad[head, keys, :], share)
             turned = value if turned is None else turned + value
+        if i == 1:
+            c_wait(1)
+            c_start(5, 7)
+            c_wait(3)
+            c_start(6, 9)
         o_turned[:, at] = turned
         o_heads[at, :] = low(turned.T)
         for k in range(per_block):
@@ -644,91 +681,69 @@
             def _():
                 o_rows[:, span(me * part, part)] = o_heads[mine, :]
 
-    c_wait(1)
-    c_start(5, 7)
-    c_wait(3)
-    c_start(6, 9)
+    c_wait(2)
+    c_start(8)
+    c_wait(4)
+    c_start(10)
     loads[5].wait()
     o_wait()
     middle_own = wide(frames_all[mine, :]) + dot(o_rows[...], w_out[...])
     middle[...] = middle_own
-    hidden2_all[mine, :] = low(middle_own * norm_scale(middle_own) * gain2)
-    h_start(0, 1, 3, 2, 4)
-
-    c_wait(2)
-    c_start(8)
-    c_wait(4)
-    c_start(10)
+    hidden2_own = low(middle_own * norm_scale(middle_own) * gain2)
+    hidden2_all[mine, :] = hidden2_own
+
+    load_up(wait=True)
+    tiles = ff // width
+    pieces = []
+    for k in range(tiles):
+        tile = pl.ds(k * width, width)
+        active, slope = gelu_parts(dot(hidden2_own, w_up[:, tile]))
+        active_rows[:, tile] = low(active)
+        slope_rows[:, tile] = low(slope)
+        if k < tiles - 1:
+            def a_pairs(target, source, k=k):
+                yield (
+                    active_rows.at[:, span(k * width + target * part, part)],
+                    active_s.at[span(source * rows, rows), pl.ds(k * part, part)],
+                )
+
+            pieces.append(swap(7 + k, a_pairs, o_heads.at[pl.ds(0, total - rows)]))
+            others(pieces[k][0])
+            active_s[mine, pl.ds(k * part, part)] = active_rows[:, span(k * width + me * part, part)]
+        if k == tiles - 2:
+            h_start(0, 1, 3, 2, 4)
     loads[1].wait()
-    loads[6].wait()
-    loads[7].wait()
-    acc_a[...] = middle_own
+    load_down(wait=True)
     acc_b[...] = jnp.zeros_like(acc_b)
 
-    def ff_tile(t):
-        at = span(t * width, width)
-        active, slope = gelu_parts(dot(hidden2_all[mine, :], w_up[:, at]))
-        acc_a[...] += dot(low(active), w_down[at, :])
-        grad = low(dot_nt(cot_all[mine, :], w_down[at, :]) * slope)
-        acc_b[...] += dot_nt(grad, w_up[:, at])
-
-    tiles = ff // width
-    pl.loop(0, tiles // 2)(ff_tile)
-    h_wait(1)
-    h_start(5, 7)
-    h_wait(3)
-    h_start(6, 9)
+    def back_tile(k):
+        tile = span(k * width, width)
+        grad = low(dot_nt(cot_all[mine, :], w_down[tile, :]) * wide(slope_rows[:, tile]))
+        acc_b[...] += dot_nt(grad, w_up[:, tile])
+
+    def down_piece(k):
+        at = pl.ds(k * part, part)
+        own[at, :] = low(dot_tn(active_s[:, at], cot_all[...]))
+        z_outer(k * (part // ZROWS), (k + 1) * (part // ZROWS))
+
+    back_tile(0)
     c_wait(5)
     c_start(11)
     c_wait(6)
     c_start(12)
-    pl.loop(tiles // 2, tiles - 1)(ff_tile)
-    h_wait(2)
-    h_start(8)
-    h_wait(4)
-    h_start(10)
-    pl.loop(tiles - 1, tiles)(ff_tile)
-    h_wait(5)
-    h_start(11)
-    h_wait(6)
-    h_start(12)
-
-    slab_at = span(me * slab, slab)
-
-    def slab_chip(index):
-        at = chip(index)
-        active, slope = gelu_parts(dot(hidden2_all[at, :], w_up[:, slab_at]))
-        active_s[at, :] = low(active)
-        slope_s[at, :] = low(slope)
-
-    h_wait(0)
-    slab_chip(me)
-    h_wait(7)
-    slab_chip(over_x)
-    h_wait(9)
-    slab_chip(over_y)
-    h_wait(11)
-    slab_chip(corner)
+    back_tile(1)
+    c_wait(0, 7, 9, 11)
+    pieces[0][1]()
+    down_piece(0)
+    back_tile(2)
+    pieces[1][1]()
+    down_piece(1)
+    back_tile(3)
     load_qkv.start()
-    c_wait(0, 7, 9, 11)
-
-    down_rows, up_rows = slab, rows * (ff // width)
-    down_at, up_at = 0, down_rows
-    out_at = up_at + up_rows
-    mixed_at = out_at + part
-    slabs = width // slab
-
-    @pl.loop(0, slab // part)
-    def _(t):
-        at = span(down_at + t * part, part)
-        own[at, :] = low(dot_tn(active_s[:, span(t * part, part)], cot_all[...]))
-
-        @pl.when(outer)
-        def _():
-            for c in range(part // ZROWS):
-                z_raw(t * (part // ZROWS) + c).start()
-
-    result_ref[...] = low(acc_a[...])
+    pieces[2][1]()
+    down_piece(2)
+    z_upto(1)
+
     middle_own = middle[...]
     back2, gain2_part = norm_back(middle_own, norm_scale(middle_own), gain2, acc_b[...])
     gain_out[...] = jnp.zeros_like(gain_out)
@@ -739,6 +754,17 @@
     attn_own = low(grad_mid_own)
     attn_all[mine, :] = attn_own
     g_rows[...] = low(dot_nt(attn_own, w_out[...]))
+    acc_a[...] = middle[...]
+    for k in range(tiles):
+        tile = pl.ds(k * width, width)
+        acc_a[...] += dot(active_rows[:, tile], w_down[tile, :])
+    result_ref[...] = low(acc_a[...])
+    z_upto(3)
+
+    h_wait(1)
+    h_start(5, 7)
+    h_wait(3)
+    h_start(6, 9)
 
     def g_pairs(target, source):
         yield g_rows.at[:, span(target * part, part)], g_heads.at[span(source * rows, rows)]
@@ -746,34 +772,83 @@
     g_start, g_wait, g_finish = swap(1, g_pairs, g_heads.at[pl.ds(0, total - rows)])
     others(g_start)
     g_heads[mine, :] = g_rows[:, span(me * part, part)]
-
+    loads[6].wait()
+    loads[7].wait()
     for c in range(0, count, 2):
         at = span(c * rows, pair)
-        slope_s[at, :] = low(dot_nt(cot_all[at, :], w_down[slab_at, :]) * wide(slope_s[at, :]))
-
-    def u_pairs(target, source):
-        yield (
-            up_stage.at[span(target * rows, rows)],
-            own.at[span(up_at + lax.div(source, slabs) * rows, rows),
-                   span(lax.rem(source, slabs) * slab, slab)],
-        )
-
-    u_start, u_wait, u_finish = swap(2, u_pairs, up_stage.at[pl.ds(0, total - rows)])
-    z_inner(1)
-
-    @pl.loop(0, count // 2)
-    def _(c):
-        at = span(c * pair, pair)
+        slope_s[at, :] = low(dot_nt(cot_all[at, :], w_down_s[...]))
+    z_upto(4)
+    last_piece = pl.ds((tiles - 1) * part, part)
+
+    def slab_chip(index):
+        at = chip(index)
+        active, slope = gelu_parts(dot(hidden2_all[at, :], w_up_s[...]))
+        active_s[at, last_piece] = low(active[:, (tiles - 1) * part :])
+        slope_s[at, :] = low(wide(slope_s[at, :]) * slope)
+
+    h_wait(0)
+    slab_chip(me)
+    h_wait(2)
+    h_start(8)
+    h_wait(4)
+    h_start(10)
+    h_wait(7)
+    slab_chip(over_x)
+    h_wait(9)
+    slab_chip(over_y)
+    z_upto(6)
+    h_wait(5)
+    h_start(11)
+    h_wait(6)
+    h_start(12)
+    h_wait(11)
+    slab_chip(corner)
+    down_piece(tiles - 1)
+
+    up_at = slab
+    mixed_at = up_at + rows * tiles
+    out_at = mixed_at + rows * 3
+    slabs = width // slab
+    near, middle_up, far, mixed_z, out_z = (
+        up_at // ZROWS, (up_at + rows) // ZROWS, (up_at + 3 * rows) // ZROWS,
+        mixed_at // ZROWS, out_at // ZROWS,
+    )
+
+    def distance(one, other):
+        one, other = lax.div(one, 2), lax.div(other, 2)
+        return lax.rem(one + other, 2) + 2 * lax.rem(lax.div(one, 2) + lax.div(other, 2), 2)
+
+    def u_place(target, source):
+        return (span(up_at + distance(target, source) * rows, rows),
+                span(lax.rem(source, slabs) * slab, slab))
+
+    u_sems = (10, 11, 11, 12)
+
+    def u_send(target, near_by):
+        here = up_stage.at[span(target * rows, rows)]
+        remote(here, own.at[u_place(target, me)], swap_send.at[2], swap_recv.at[u_sems[near_by]],
+               target).start()
+
+    def u_wait(number, blocks):
+        some = up_stage.at[pl.ds(0, blocks * rows)]
+        remote(some, some, swap_send.at[2], swap_recv.at[number], mate).wait_recv()
+
+    def u_finish():
+        some = up_stage.at[pl.ds(0, total - rows)]
+        remote(some, some, swap_send.at[2], swap_recv.at[2], mate).wait_send()
+
+    for near_by, index in ((1, over_x), (2, over_y), (3, corner), (0, me)):
+        at = chip(index)
         up_stage[at, :] = low(dot_tn(hidden2_all[:, at], slope_s[...]))
-        for s in (2 * c, 2 * c + 1):
-            @pl.when(s != me)
-            def _():
-                u_start(s)
-
-    own[span(up_at + lax.div(me, slabs) * rows, rows), span(lax.rem(me, slabs) * slab, slab)] = (
-        up_stage[mine, :])
-    a_start(0, 1, 3, 2, 4)
-    z_inner(2)
+        if near_by:
+            u_send(index, near_by)
+            u_send(flip(index, 1), near_by)
+        else:
+            u_send(mate, near_by)
+            own[u_place(me, me)] = up_stage[mine, :]
+    z_upto(9)
+    u_wait(u_sems[0], 1)
+    z_outer(near, middle_up)
 
     g_wait()
     for c in range(count // 2):
@@ -790,7 +865,7 @@
             value = dot(shares[head, keys, late(j)], g_pad[head, late(j), :])
             grad = value if grad is None else grad + value
         mixed_grad[keys, values_at] = low(grad)
-    z_inner(2)
+    z_upto(10)
     for i in range(query_blocks):
         at, keys = pl.ds(i * QBLOCK, QBLOCK), pl.ds(0, (i + 1) * QBLOCK)
         product = wide(g_heads[at, :]).T * o_turned[:, at]
@@ -804,7 +879,7 @@
             value = dot_tn(k_pad[head, keys, :], grad_score)
             turned = value if turned is None else turned + value
         mixed_grad[at, pl.ds(0, part)] = low((turned * factor).T)
-        z_inner(1)
+        z_upto((10, 11, 12, 13)[min(i, 3)])
     for j in range(query_blocks):
         keys = pl.ds(j * QBLOCK, QBLOCK)
         grad = None
@@ -812,7 +887,7 @@
             value = dot(shares[head, keys, late(j)], q_pad[head, late(j), :])
             grad = value if grad is None else grad + value
         mixed_grad[keys, keys_at] = low(grad)
-    z_inner(2)
+    z_upto(15)
 
     def s_pairs(target, source):
         for k in range(3):
@@ -831,45 +906,49 @@
     s_start, s_wait, s_finish = swap(3, s_pairs, mixed_stage.at[pl.ds(0, total - rows)])
     m_start, m_wait, m_finish = swap(4, m_pairs, mixed_grad.at[pl.ds(0, total - rows)])
 
-    @pl.loop(0, count // 2)
-    def _(c):
-        at = span(c * pair, pair)
+    for index in (over_x, over_y, corner, me):
+        at = chip(index)
         mixed_stage[at, :] = low(dot_tn(hidden1_all[:, at], mixed_grad[...]))
-        for s in (2 * c, 2 * c + 1):
-            @pl.when(s != me)
-            def _():
-                s_start(s)
-
+        if index is not me:
+            s_start(index)
+            s_start(flip(index, 1))
+        else:
+            s_start(mate)
     for k in range(3):
         own[span(mixed_at + k * rows, rows), span(me * part, part)] = (
             mixed_stage[mine, pl.ds(k * part, part)])
         mixed_rows[:, span(k * width + me * part, part)] = mixed_grad[mine, pl.ds(k * part, part)]
+    a_start(0, 1, 3, 2, 4)
+    z_upto(17)
+    u_wait(u_sems[1], 4)
+    z_outer(middle_up, far)
+    z_upto(21)
+    u_wait(u_sems[3], 2)
+    z_outer(far, mixed_z)
+    z_upto(27)
+    s_wait()
+    z_outer(mixed_z, out_z)
+
     a_wait(1)
     a_start(5, 7)
     a_wait(3)
     a_start(6, 9)
+    others(m_start)
+    z_upto(30)
     a_wait(2)
     a_start(8)
     a_wait(4)
     a_start(10)
-    others(m_start)
-    z_inner(2)
-    u_wait()
-    z_outer(up_at // ZROWS, out_at // ZROWS)
-    z_inner(2)
-
+    z_upto(34)
     a_wait(5)
     a_start(11)
     a_wait(6)
     a_start(12)
-    z_inner(2)
+    z_upto(36)
     a_wait(0, 7, 9, 11)
     own[pl.ds(out_at, part), :] = low(dot(low(o_turned[...]), attn_all[...]))
-    z_outer(out_at // ZROWS, mixed_at // ZROWS)
-    z_inner(4)
-    s_wait()
-    z_outer(mixed_at // ZROWS, chunks)
-    z_inner(6)
+    z_outer(out_z, chunks)
+    z_upto(40)
 
     load_qkv.wait()
     m_wait()
@@ -883,7 +962,6 @@
     frames_own = wide(frames_all[mine, :])
     back1, gain1_part = norm_back(frames_own, norm_scale(frames_own), gain1, acc_a[...])
     d_in_ref[...] = grad_mid[...] + back1
-    z_inner(2)
 
     for s in range(count):
         gain_out[s, 0:1, :] = gain1_part[:, s * part : (s + 1) * part]
@@ -899,7 +977,7 @@
 
     others(n_start)
     gain_in[me] = gain_out[me]
-    z_inner(4)
+    z_upto(44)
     n_wait()
     gain_sum = gain_in[0]
     for s in range(1, count):
@@ -910,7 +988,7 @@
     def _(step):
         nz_copy(lax.rem(plane + step, planes), plane).start()
 
-    z_inner(chunks - z_done[0])
+    z_upto(chunks)
     gains_all = gain_z.at[pl.ds(0, planes - 1)]
     all_gains = remote(gains_all, gains_all, swap_send.at[6], swap_recv.at[6], mate)
     all_gains.wait_recv()
@@ -930,6 +1008,8 @@
         o_finish, g_finish, u_finish, s_finish, m_finish, n_finish,
     ):
         finish()
+    for piece in pieces:
+        piece[2]()
     all_gains.wait_send()
 
     @pl.when(outer)
@@ -953,14 +1033,19 @@
 ):
     rows, width = result_in.shape
     slab, part = down_ref.shape[0], out_ref.shape[0]
+    here = lax.div(lax.axis_index("sq"), 2)
     targets = [down_ref]
     starts = [0]
     sizes = [slab]
-    for ref, tall in ((up_ref, rows), (out_ref, part), (qkv_ref, rows)):
+    for ref, tall in ((up_ref, rows), (qkv_ref, rows), (out_ref, part)):
         for k in range(ref.shape[1] // width):
             starts.append(starts[-1] + sizes[-1])
             sizes.append(tall)
-            targets.append(ref.at[:, pl.ds(k * width, width)])
+            block = k
+            if ref is up_ref:
+                low_bit, high_bit = lax.rem(here, 2), lax.div(here, 2)
+                block = lax.rem(low_bit + k, 2) + 2 * lax.rem(high_bit + k // 2, 2)
+            targets.append(ref.at[:, span(block * width, width)])
     copies = [
         pltpu.make_async_copy(result_in, result_ref.at[0], sems.at[0]),
         pltpu.make_async_copy(d_in_in, d_in_ref.at[0], sems.at[1]),
@@ -1004,6 +1089,7 @@
     scratch = (
         [low_array(total, width)] * 5
         + [low_array(width, 3 * part), low_array(width, width), low_array(width, ff), low_array(ff, width)]
+        + [low_array(width, slab), low_array(slab, width), low_array(rows, ff), low_array(rows, ff)]
         + [low_array(total, 3 * part)]
         + [low_array(local, total, part)] * 4
         + [low_array(local, total, total), wide_array(part, total)]
@@ -1016,7 +1102,7 @@
         + [low_array(own_rows, width)] * 2
         + [wide_array(count, 8, part)] * 2
         + [wide_array(planes, 8, part)]
-        + [copies(9), copies(4), copies(4, 10), copies(7), copies(7), copies(2)]
+        + [copies(11), copies(4), copies(4, 10), copies(13), copies(13), copies(2)]
         + [copies(chunks)] * 2
     )
     kept = pl.pallas_call(

time: 140 us -> 126 us (0.900); the launches traced: 137 us -> 126 us
  Pallas kernels: 137 us -> 125 us
    pallas_call x1, Pallas kernels: 133 us -> 121 us  [shards_by_heads(): pl.pallas_call(functools.partial(layer_kernel, count, planes), out_shape=...]
where the time goes in v5:
time: 126 us
  Pallas kernels  125 us (99%)
    pallas_call x1, Pallas kernels, shards_by_heads(): pl.pallas_call(functools.partial(layer_kernel, count, planes), out_shape=...  121 us
    pallas_call x1, Pallas kernels, shards_by_heads(): pl.pallas_call(finish_kernel, out_shape=tuple((jax.ShapeDtypeStruct(shape...  3.5 us

profile of v5, /device:TPU:0, one launch (start us, length us, event | category | flops | bytes accessed | tf_op | source)
XLA Modules:
  0.0 125.6 jit_solution(15337665456232077554)
XLA Ops:
  0.6 121.2 %shard_map.152 = (bf16[128,1024]{1,0:T(8,128)(2,1)S(1)}, f32[128,1024]{1,0:T(8,128)S(1)}, f32[8,128]{1,0:T(8,128)S(1)}, bf16[1536,1024]{1,0:T(8,128)(2,1)S(1)}) custom-call(bf16[1,128,1024]{2,1,0:T(8,128)(2,1)} %frames_in.1, f32[1,1024]{1,0:T(1,128)} %bitcast.2, bf16[1024,3072]{1,0:T(8,128)(2,1)} %w_qkv_in.1, bf16[1024,1024]{1,0:T(8,128)(2,1)} %w_out_in.1, ...), custom_call_target="tpu_custom_call" | custom-call | tf_op jit(solution)/shard_map/pallas_call | solution.py:1108
  121.9 3.5 %shard_map.153 = (bf16[1,128,1024]{2,1,0:T(8,128)(2,1)}, f32[1,128,1024]{2,1,0:T(8,128)}, f32[128]{0:T(128)}, f32[128,3072]{1,0:T(8,128)}, f32[128,1024]{1,0:T(8...) custom-call(bf16[128,1024]{1,0:T(8,128)(2,1)S(1)} %get-tuple-element.12.result_in, ...), custom_call_target="tpu_custom_call" | custom-call | tf_op jit(solution)/shard_map/pallas_call | solution.py:1122

commit v6 on v5

--- a/solution.py
+++ b/solution.py
@@ -312,8 +312,7 @@
 
 
 MESH = pl.DeviceIdType.MESH
-ZROWS = 32
-ZLAG = 3
+UNIT = 32
 QBLOCK = 256
 KEEP = pltpu.VMEM
 
@@ -344,6 +343,12 @@
 
 def span(start, size):
     return pl.ds(pl.multiple_of(start, size), size)
+
+
+def chain_table(count):
+    sizes = [UNIT] * (count // UNIT)
+    starts = [sum(sizes[:k]) for k in range(len(sizes))]
+    return list(zip(starts, sizes))
 
 
 def norm_scale(values):
@@ -524,58 +529,55 @@
     h_start, h_wait, h_finish = gather(2, hidden2_all)
     a_start, a_wait, a_finish = gather(3, attn_all)
 
+    table = chain_table(own.shape[0])
+
     def z_raw(c):
-        at = span(c * ZROWS, ZROWS)
+        at = pl.ds(*table[c])
         return remote(own.at[at], sum_ref.at[at], z_send.at[0], z_outer_recv.at[c], me, z_core)
 
     def z_cross(c):
-        at = span(c * ZROWS, ZROWS)
+        at = pl.ds(*table[c])
         return remote(own.at[at], cross_in.at[at], z_send.at[0], z_cross_recv.at[c], me, z_mate)
 
     def z_back(c):
-        at = span(c * ZROWS, ZROWS)
+        at = pl.ds(*table[c])
         return remote(sum_ref.at[at], sum_ref.at[at], z_send.at[1], z_outer_recv.at[c], me, z_edge)
 
     def z_join(c):
-        at = span(c * ZROWS, ZROWS)
+        at = pl.ds(*table[c])
         z_raw(c).wait_recv()
         own[at, :] = low(wide(own[at, :]) + wide(sum_ref[at, :]))
         z_cross(c).start()
 
     def z_close(c):
-        at = span(c * ZROWS, ZROWS)
+        at = pl.ds(*table[c])
         z_cross(c).wait_recv()
         sum_ref[at, :] = low(wide(own[at, :]) + wide(cross_in[at, :]))
         z_back(c).start()
 
-    chunks = own.shape[0] // ZROWS
-    z_done = [0]
-
-    def z_inner(number):
-        first, last = z_done[0], z_done[0] + number
-        z_done[0] = last
-
-        @pl.when(inner)
-        def _():
-            split = min(max(first, ZLAG), last)
-            for c in range(first, split):
-                z_join(c)
-            if last > split:
-                @pl.loop(split, last)
-                def _(c):
-                    z_join(c)
-                    z_close(c - ZLAG)
-
-    def z_upto(number):
-        if number > z_done[0]:
-            z_inner(number - z_done[0])
+    z_joined, z_closed = [0], [0]
+
+    def z_upto(units):
+        todo = []
+        while z_joined[0] < len(table) and sum(table[z_joined[0]]) <= units * UNIT:
+            todo.append((z_join, z_joined[0]))
+            end = sum(table[z_joined[0]])
+            z_joined[0] += 1
+            while sum(table[z_closed[0]]) + 3 * UNIT <= end:
+                todo.append((z_close, z_closed[0]))
+                z_closed[0] += 1
+        if todo:
+            @pl.when(inner)
+            def _():
+                for step, c in todo:
+                    step(c)
 
     def z_outer(first, last):
         @pl.when(outer)
         def _():
-            @pl.loop(first, last)
-            def _(c):
-                z_raw(c).start()
+            for c, (start, size) in enumerate(table):
+                if first <= start < last:
+                    z_raw(c).start()
 
     f_start(0, 1, 3, 2, 4)
     loads[5].start()
@@ -593,10 +595,13 @@
 
     def padded(ref, at, values):
         for head in range(local):
-            ref[head, at, :] = low(jnp.where(lane_head == head, values, 0.0))
+            on = lane_head[: values.shape[0]] == head
+            ref[head, at, :] = low(jnp.where(on, values, 0.0))
 
     def qkv_chip(index):
-        at = chip(index)
+        qkv_rows(chip(index), pair)
+
+    def qkv_rows(at, _):
         values = wide(frames_all[at, :])
         hidden = low(values * norm_scale(values) * gain1)
         hidden1_all[at, :] = hidden
@@ -628,8 +633,9 @@
     f_start(11)
     f_wait(6)
     f_start(12)
+    qkv_rows(span(corner * rows, rows), rows)
     f_wait(11)
-    qkv_chip(corner)
+    qkv_rows(span(flip(corner, 1) * rows, rows), rows)
 
     ends, running = [], None
     for item in range(lengths_ref.shape[1]):
@@ -724,25 +730,34 @@
     def down_piece(k):
         at = pl.ds(k * part, part)
         own[at, :] = low(dot_tn(active_s[:, at], cot_all[...]))
-        z_outer(k * (part // ZROWS), (k + 1) * (part // ZROWS))
-
+        z_outer(k * part, (k + 1) * part)
+
+    def out_tile(k):
+        tile = pl.ds(k * width, width)
+        acc_a[...] += dot(active_rows[:, tile], w_down[tile, :])
+
+    acc_a[...] = middle_own
     back_tile(0)
     c_wait(5)
     c_start(11)
     c_wait(6)
     c_start(12)
-    back_tile(1)
+    for k in range(tiles - 1):
+        out_tile(k)
     c_wait(0, 7, 9, 11)
     pieces[0][1]()
     down_piece(0)
-    back_tile(2)
+    back_tile(1)
     pieces[1][1]()
     down_piece(1)
+    back_tile(2)
+    z_upto(1)
+    pieces[2][1]()
+    down_piece(2)
+    z_upto(2)
     back_tile(3)
     load_qkv.start()
-    pieces[2][1]()
-    down_piece(2)
-    z_upto(1)
+    z_upto(4)
 
     middle_own = middle[...]
     back2, gain2_part = norm_back(middle_own, norm_scale(middle_own), gain2, acc_b[...])
@@ -754,12 +769,9 @@
     attn_own = low(grad_mid_own)
     attn_all[mine, :] = attn_own
     g_rows[...] = low(dot_nt(attn_own, w_out[...]))
-    acc_a[...] = middle[...]
-    for k in range(tiles):
-        tile = pl.ds(k * width, width)
-        acc_a[...] += dot(active_rows[:, tile], w_down[tile, :])
+    out_tile(tiles - 1)
     result_ref[...] = low(acc_a[...])
-    z_upto(3)
+    z_upto(5)
 
     h_wait(1)
     h_start(5, 7)
@@ -777,7 +789,7 @@
     for c in range(0, count, 2):
         at = span(c * rows, pair)
         slope_s[at, :] = low(dot_nt(cot_all[at, :], w_down_s[...]))
-    z_upto(4)
+    z_upto(7)
     last_piece = pl.ds((tiles - 1) * part, part)
 
     def slab_chip(index):
@@ -796,23 +808,21 @@
     slab_chip(over_x)
     h_wait(9)
     slab_chip(over_y)
-    z_upto(6)
+    z_upto(9)
     h_wait(5)
     h_start(11)
     h_wait(6)
     h_start(12)
+    z_upto(10)
     h_wait(11)
     slab_chip(corner)
     down_piece(tiles - 1)
+    z_upto(11)
 
     up_at = slab
     mixed_at = up_at + rows * tiles
     out_at = mixed_at + rows * 3
     slabs = width // slab
-    near, middle_up, far, mixed_z, out_z = (
-        up_at // ZROWS, (up_at + rows) // ZROWS, (up_at + 3 * rows) // ZROWS,
-        mixed_at // ZROWS, out_at // ZROWS,
-    )
 
     def distance(one, other):
         one, other = lax.div(one, 2), lax.div(other, 2)
@@ -846,9 +856,10 @@
         else:
             u_send(mate, near_by)
             own[u_place(me, me)] = up_stage[mine, :]
-    z_upto(9)
+        if near_by in (2, 0):
+            z_upto(12 if near_by else 13)
     u_wait(u_sems[0], 1)
-    z_outer(near, middle_up)
+    z_outer(up_at, up_at + rows)
 
     g_wait()
     for c in range(count // 2):
@@ -865,7 +876,7 @@
             value = dot(shares[head, keys, late(j)], g_pad[head, late(j), :])
             grad = value if grad is None else grad + value
         mixed_grad[keys, values_at] = low(grad)
-    z_upto(10)
+    z_upto(14)
     for i in range(query_blocks):
         at, keys = pl.ds(i * QBLOCK, QBLOCK), pl.ds(0, (i + 1) * QBLOCK)
         product = wide(g_heads[at, :]).T * o_turned[:, at]
@@ -879,7 +890,7 @@
             value = dot_tn(k_pad[head, keys, :], grad_score)
             turned = value if turned is None else turned + value
         mixed_grad[at, pl.ds(0, part)] = low((turned * factor).T)
-        z_upto((10, 11, 12, 13)[min(i, 3)])
+        z_upto(14 + i // 2 if i < query_blocks - 1 else 16)
     for j in range(query_blocks):
         keys = pl.ds(j * QBLOCK, QBLOCK)
         grad = None
@@ -887,7 +898,7 @@
             value = dot(shares[head, keys, late(j)], q_pad[head, late(j), :])
             grad = value if grad is None else grad + value
         mixed_grad[keys, keys_at] = low(grad)
-    z_upto(15)
+    z_upto(17)
 
     def s_pairs(target, source):
         for k in range(3):
@@ -919,45 +930,49 @@
             mixed_stage[mine, pl.ds(k * part, part)])
         mixed_rows[:, span(k * width + me * part, part)] = mixed_grad[mine, pl.ds(k * part, part)]
     a_start(0, 1, 3, 2, 4)
-    z_upto(17)
+    z_upto(19)
     u_wait(u_sems[1], 4)
-    z_outer(middle_up, far)
-    z_upto(21)
+    z_outer(up_at + rows, up_at + 3 * rows)
+    z_upto(26)
     u_wait(u_sems[3], 2)
-    z_outer(far, mixed_z)
-    z_upto(27)
+    z_outer(up_at + 3 * rows, mixed_at)
+    z_upto(31)
     s_wait()
-    z_outer(mixed_z, out_z)
+    z_outer(mixed_at, out_at)
+
+    z_upto(33)
 
     a_wait(1)
     a_start(5, 7)
     a_wait(3)
     a_start(6, 9)
     others(m_start)
-    z_upto(30)
+    z_upto(35)
     a_wait(2)
     a_start(8)
     a_wait(4)
     a_start(10)
-    z_upto(34)
+    z_upto(38)
     a_wait(5)
     a_start(11)
     a_wait(6)
     a_start(12)
-    z_upto(36)
+    z_upto(39)
     a_wait(0, 7, 9, 11)
     own[pl.ds(out_at, part), :] = low(dot(low(o_turned[...]), attn_all[...]))
-    z_outer(out_z, chunks)
-    z_upto(40)
+    z_outer(out_at, own.shape[0])
+    z_upto(43)
 
     load_qkv.wait()
     m_wait()
     acc_a[...] = jnp.zeros_like(acc_a)
-
-    @pl.loop(0, 3)
-    def _(k):
-        at = span(k * width, width)
-        acc_a[...] += dot_nt(mixed_rows[:, at], w_up[:, at])
+    for k in range(3):
+        @pl.loop(k, k + 1)
+        def _(k):
+            at = span(k * width, width)
+            acc_a[...] += dot_nt(mixed_rows[:, at], w_up[:, at])
+
+        z_upto(44 + k // 2)
 
     frames_own = wide(frames_all[mine, :])
     back1, gain1_part = norm_back(frames_own, norm_scale(frames_own), gain1, acc_a[...])
@@ -977,7 +992,7 @@
 
     others(n_start)
     gain_in[me] = gain_out[me]
-    z_upto(44)
+    z_upto(46)
     n_wait()
     gain_sum = gain_in[0]
     for s in range(1, count):
@@ -988,7 +1003,7 @@
     def _(step):
         nz_copy(lax.rem(plane + step, planes), plane).start()
 
-    z_upto(chunks)
+    z_upto(own.shape[0] // UNIT)
     gains_all = gain_z.at[pl.ds(0, planes - 1)]
     all_gains = remote(gains_all, gains_all, swap_send.at[6], swap_recv.at[6], mate)
     all_gains.wait_recv()
@@ -999,8 +1014,7 @@
 
     @pl.when(inner)
     def _():
-        @pl.loop(chunks - ZLAG, chunks)
-        def _(c):
+        for c in range(z_closed[0], len(table)):
             z_close(c)
 
     for finish in (
@@ -1016,8 +1030,7 @@
     def _():
         remote(own, own, z_send.at[0], z_outer_recv.at[0], me, z_core).wait_send()
 
-        @pl.loop(0, chunks)
-        def _(c):
+        for c in range(len(table)):
             z_back(c).wait_recv()
 
     @pl.when(inner)
@@ -1034,9 +1047,9 @@
     rows, width = result_in.shape
     slab, part = down_ref.shape[0], out_ref.shape[0]
     here = lax.div(lax.axis_index("sq"), 2)
-    targets = [down_ref]
-    starts = [0]
-    sizes = [slab]
+    starts = list(range(0, slab, part))
+    sizes = [part] * len(starts)
+    targets = [down_ref.at[pl.ds(start, part)] for start in starts]
     for ref, tall in ((up_ref, rows), (qkv_ref, rows), (out_ref, part)):
         for k in range(ref.shape[1] // width):
             starts.append(starts[-1] + sizes[-1])
@@ -1073,7 +1086,7 @@
     bf16, f32 = jnp.bfloat16, jnp.float32
     blocks = ff // width
     own_rows = slab + rows * blocks + part + rows * 3
-    chunks = own_rows // ZROWS
+    chunks = len(chain_table(own_rows))
     vmem, anywhere = pl.BlockSpec(memory_space=pltpu.VMEM), pl.BlockSpec(memory_space=pl.ANY)
     smem = pl.BlockSpec(memory_space=pltpu.SMEM)
 
@@ -1131,7 +1144,7 @@
         ),
         in_specs=[vmem] * 4,
         out_specs=(anywhere, anywhere, vmem, anywhere, anywhere, vmem, anywhere, anywhere),
-        scratch_shapes=[wide_array(own_rows, width), wide_array(8, part), copies(11)],
+        scratch_shapes=[wide_array(own_rows, width), wide_array(8, part), copies(2 + slab // part + 2 * blocks)],
         compiler_params=pltpu.CompilerParams(vmem_limit_bytes=24 * 2**20),
     )(*kept)
 

time: 126 us -> 123 us (0.976)
  Pallas kernels: 125 us -> 122 us
    pallas_call x1, Pallas kernels: 121 us -> 118 us  [shards_by_heads(): pl.pallas_call(functools.partial(layer_kernel, count, planes), out_shape=...]
where the time goes in v6:
time: 123 us; the launch traced here: 122 us
  Pallas kernels  122 us (99%)
    pallas_call x1, Pallas kernels, shards_by_heads(): pl.pallas_call(functools.partial(layer_kernel, count, planes), out_shape=...  118 us
    pallas_call x1, Pallas kernels, shards_by_heads(): pl.pallas_call(finish_kernel, out_shape=tuple((jax.ShapeDtypeStruct(shape...  3.53 us

profile of v6, /device:TPU:0, one launch (start us, length us, event | category | flops | bytes accessed | tf_op | source)
XLA Modules:
  0.0 122.4 jit_solution(8885186178589085390)
XLA Ops:
  0.6 118.1 %shard_map.152 = (bf16[128,1024]{1,0:T(8,128)(2,1)S(1)}, f32[128,1024]{1,0:T(8,128)S(1)}, f32[8,128]{1,0:T(8,128)S(1)}, bf16[1536,1024]{1,0:T(8,128)(2,1)S(1)}) custom-call(bf16[1,128,1024]{2,1,0:T(8,128)(2,1)} %frames_in.1, f32[1,1024]{1,0:T(1,128)} %bitcast.2, bf16[1024,3072]{1,0:T(8,128)(2,1)} %w_qkv_in.1, bf16[1024,1024]{1,0:T(8,128)(2,1)} %w_out_in.1, ...), custom_call_target="tpu_custom_call" | custom-call | tf_op jit(solution)/shard_map/pallas_call | solution.py:1121
  118.7 3.5 %shard_map.153 = (bf16[1,128,1024]{2,1,0:T(8,128)(2,1)}, f32[1,128,1024]{2,1,0:T(8,128)}, f32[128]{0:T(128)}, f32[128,3072]{1,0:T(8,128)}, f32[128,1024]{1,0:T(8...) custom-call(bf16[128,1024]{1,0:T(8,128)(2,1)S(1)} %get-tuple-element.12.result_in, ...), custom_call_target="tpu_custom_call" | custom-call | tf_op jit(solution)/shard_map/pallas_call | solution.py:1135

commit v7 on v6

--- a/solution.py
+++ b/solution.py
@@ -416,6 +416,14 @@
         def _(step):
             body(lax.rem(me + step, count))
 
+    barrier = pltpu.get_barrier_semaphore()
+    for step in range(1, planes):
+        pl.semaphore_signal(
+            barrier, inc=1, device_id=(lax.rem(plane + step, planes), me), device_id_type=MESH)
+    for step in range(1, count):
+        pl.semaphore_signal(
+            barrier, inc=1, device_id=(plane, lax.rem(me + step, count)), device_id_type=MESH)
+
     mine = span(me * rows, rows)
     loads = [
         pltpu.make_async_copy(frames_in.at[0], frames_all.at[mine], load_sem.at[0]),
@@ -460,16 +468,7 @@
     load_qkv = pltpu.make_async_copy(w_qkv_in, w_up.at[:, pl.ds(0, 3 * width)], load_sem.at[8])
     for load in loads[:5]:
         load.start()
-
-    barrier = pltpu.get_barrier_semaphore()
-    others(lambda s: pl.semaphore_signal(
-        barrier, inc=1, device_id=(plane, s), device_id_type=MESH))
-
-    @pl.loop(1, planes)
-    def _(step):
-        pl.semaphore_signal(
-            barrier, inc=1, device_id=(lax.rem(plane + step, planes), me), device_id_type=MESH)
-
+    loads[0].wait()
     pl.semaphore_wait(barrier, count - 1 + planes - 1)
 
     def slots(index):
@@ -524,7 +523,7 @@
 
         return start, wait, finish
 
-    f_start, f_wait, f_finish = gather(0, frames_all, frames_in.at[0])
+    f_start, f_wait, f_finish = gather(0, frames_all)
     c_start, c_wait, c_finish = gather(1, cot_all, cot_in.at[0])
     h_start, h_wait, h_finish = gather(2, hidden2_all)
     a_start, a_wait, a_finish = gather(3, attn_all)
@@ -572,6 +571,15 @@
                 for step, c in todo:
                     step(c)
 
+    def z_closes(number):
+        first = z_closed[0]
+        z_closed[0] = min(first + number, len(table))
+
+        @pl.when(inner)
+        def _():
+            for c in range(first, z_closed[0]):
+                z_close(c)
+
     def z_outer(first, last):
         @pl.when(outer)
         def _():
@@ -611,7 +619,6 @@
         padded(k_pad, at, wide(projected[:, part : 2 * part]))
         padded(v_pad, at, wide(projected[:, 2 * part :]))
 
-    loads[0].wait()
     for k in range(3):
         loads[2 + k].wait()
     f_wait(0)
@@ -757,6 +764,10 @@
     z_upto(2)
     back_tile(3)
     load_qkv.start()
+    h_wait(1)
+    h_start(5, 7)
+    h_wait(3)
+    h_start(6, 9)
     z_upto(4)
 
     middle_own = middle[...]
@@ -769,14 +780,8 @@
     attn_own = low(grad_mid_own)
     attn_all[mine, :] = attn_own
     g_rows[...] = low(dot_nt(attn_own, w_out[...]))
-    out_tile(tiles - 1)
-    result_ref[...] = low(acc_a[...])
     z_upto(5)
 
-    h_wait(1)
-    h_start(5, 7)
-    h_wait(3)
-    h_start(6, 9)
 
     def g_pairs(target, source):
         yield g_rows.at[:, span(target * part, part)], g_heads.at[span(source * rows, rows)]
@@ -793,7 +798,9 @@
     last_piece = pl.ds((tiles - 1) * part, part)
 
     def slab_chip(index):
-        at = chip(index)
+        slab_rows(chip(index))
+
+    def slab_rows(at):
         active, slope = gelu_parts(dot(hidden2_all[at, :], w_up_s[...]))
         active_s[at, last_piece] = low(active[:, (tiles - 1) * part :])
         slope_s[at, :] = low(wide(slope_s[at, :]) * slope)
@@ -813,9 +820,10 @@
     h_start(11)
     h_wait(6)
     h_start(12)
+    slab_rows(span(corner * rows, rows))
     z_upto(10)
     h_wait(11)
-    slab_chip(corner)
+    slab_rows(span(flip(corner, 1) * rows, rows))
     down_piece(tiles - 1)
     z_upto(11)
 
@@ -890,7 +898,7 @@
             value = dot_tn(k_pad[head, keys, :], grad_score)
             turned = value if turned is None else turned + value
         mixed_grad[at, pl.ds(0, part)] = low((turned * factor).T)
-        z_upto(14 + i // 2 if i < query_blocks - 1 else 16)
+        z_upto(14 + i)
     for j in range(query_blocks):
         keys = pl.ds(j * QBLOCK, QBLOCK)
         grad = None
@@ -898,7 +906,9 @@
             value = dot(shares[head, keys, late(j)], q_pad[head, late(j), :])
             grad = value if grad is None else grad + value
         mixed_grad[keys, keys_at] = low(grad)
-    z_upto(17)
+        if j == 1:
+            z_upto(18)
+    z_upto(19)
 
     def s_pairs(target, source):
         for k in range(3):
@@ -930,34 +940,39 @@
             mixed_stage[mine, pl.ds(k * part, part)])
         mixed_rows[:, span(k * width + me * part, part)] = mixed_grad[mine, pl.ds(k * part, part)]
     a_start(0, 1, 3, 2, 4)
-    z_upto(19)
+    z_upto(20)
+    out_tile(tiles - 1)
+    result_ref[...] = low(acc_a[...])
     u_wait(u_sems[1], 4)
     z_outer(up_at + rows, up_at + 3 * rows)
-    z_upto(26)
+    z_upto(27)
     u_wait(u_sems[3], 2)
     z_outer(up_at + 3 * rows, mixed_at)
     z_upto(31)
     s_wait()
     z_outer(mixed_at, out_at)
-
-    z_upto(33)
+    z_upto(34)
 
     a_wait(1)
     a_start(5, 7)
     a_wait(3)
     a_start(6, 9)
-    others(m_start)
-    z_upto(35)
+    for first in (1, 4):
+        @pl.loop(first, (4, count)[first // 4])
+        def _(step):
+            m_start(lax.rem(me + step, count))
+
+        z_upto((35, 37)[first // 4])
     a_wait(2)
     a_start(8)
     a_wait(4)
     a_start(10)
-    z_upto(38)
+    z_upto(39)
     a_wait(5)
     a_start(11)
     a_wait(6)
     a_start(12)
-    z_upto(39)
+    z_upto(41)
     a_wait(0, 7, 9, 11)
     own[pl.ds(out_at, part), :] = low(dot(low(o_turned[...]), attn_all[...]))
     z_outer(out_at, own.shape[0])
@@ -977,6 +992,7 @@
     frames_own = wide(frames_all[mine, :])
     back1, gain1_part = norm_back(frames_own, norm_scale(frames_own), gain1, acc_a[...])
     d_in_ref[...] = grad_mid[...] + back1
+    z_upto(46)
 
     for s in range(count):
         gain_out[s, 0:1, :] = gain1_part[:, s * part : (s + 1) * part]
@@ -992,7 +1008,8 @@
 
     others(n_start)
     gain_in[me] = gain_out[me]
-    z_upto(46)
+    z_upto(own.shape[0] // UNIT)
+    z_closes(1)
     n_wait()
     gain_sum = gain_in[0]
     for s in range(1, count):
@@ -1003,7 +1020,7 @@
     def _(step):
         nz_copy(lax.rem(plane + step, planes), plane).start()
 
-    z_upto(own.shape[0] // UNIT)
+    z_closes(len(table))
     gains_all = gain_z.at[pl.ds(0, planes - 1)]
     all_gains = remote(gains_all, gains_all, swap_send.at[6], swap_recv.at[6], mate)
     all_gains.wait_recv()
@@ -1011,11 +1028,6 @@
     for p in range(1, planes):
         gain_sum = gain_sum + gain_z[p]
     gains_ref[...] = gain_sum
-
-    @pl.when(inner)
-    def _():
-        for c in range(z_closed[0], len(table)):
-            z_close(c)
 
     for finish in (
         f_finish, c_finish, h_finish, a_finish,

time: 123 us -> 122 us (level)
  no operation moved by 1% of the time
where the time goes in v7:
time: 122 us
  Pallas kernels  121 us (99%)
    pallas_call x1, Pallas kernels, shards_by_heads(): pl.pallas_call(functools.partial(layer_kernel, count, planes), out_shape=...  117 us
    pallas_call x1, Pallas kernels, shards_by_heads(): pl.pallas_call(finish_kernel, out_shape=tuple((jax.ShapeDtypeStruct(shape...  3.53 us

profile of v7, /device:TPU:0, one launch (start us, length us, event | category | flops | bytes accessed | tf_op | source)
XLA Modules:
  0.0 121.8 jit_solution(16909317619452148412)
XLA Ops:
  0.6 117.4 %shard_map.152 = (bf16[128,1024]{1,0:T(8,128)(2,1)S(1)}, f32[128,1024]{1,0:T(8,128)S(1)}, f32[8,128]{1,0:T(8,128)S(1)}, bf16[1536,1024]{1,0:T(8,128)(2,1)S(1)}) custom-call(bf16[1,128,1024]{2,1,0:T(8,128)(2,1)} %frames_in.1, f32[1,1024]{1,0:T(1,128)} %bitcast.2, bf16[1024,3072]{1,0:T(8,128)(2,1)} %w_qkv_in.1, bf16[1024,1024]{1,0:T(8,128)(2,1)} %w_out_in.1, ...), custom_call_target="tpu_custom_call" | custom-call | tf_op jit(solution)/shard_map/pallas_call | solution.py:1133
  118.1 3.5 %shard_map.153 = (bf16[1,128,1024]{2,1,0:T(8,128)(2,1)}, f32[1,128,1024]{2,1,0:T(8,128)}, f32[128]{0:T(128)}, f32[128,3072]{1,0:T(8,128)}, f32[128,1024]{1,0:T(8...) custom-call(bf16[128,1024]{1,0:T(8,128)(2,1)S(1)} %get-tuple-element.12.result_in, ...), custom_call_target="tpu_custom_call" | custom-call | tf_op jit(solution)/shard_map/pallas_call | solution.py:1147

commit v8 on v7

--- a/solution.py
+++ b/solution.py
@@ -313,6 +313,7 @@
 
 MESH = pl.DeviceIdType.MESH
 UNIT = 32
+RING = 12
 QBLOCK = 256
 KEEP = pltpu.VMEM
 
@@ -376,7 +377,7 @@
     frames_in, gain1_ref, w_qkv_in, w_out_in, gain2_ref, w_up_in, w_down_in, lengths_ref, cot_in,
     result_ref, d_in_ref, gains_ref, sum_ref,
     frames_all, hidden1_all, cot_all, hidden2_all, attn_all,
-    w_heads, w_out, w_up, w_down, w_up_s, w_down_s, active_rows, slope_rows,
+    w_heads, w_out, w_up, w_down, w_up_s, w_down_s, active_rows, slope_rows, grad_rows,
     mixed, q_pad, k_pad, v_pad, g_pad, shares, o_turned, o_heads, o_rows,
     middle, acc_a, acc_b, grad_mid, g_rows, g_heads,
     active_s, slope_s, up_stage, mixed_grad, mixed_stage, mixed_rows,
@@ -468,6 +469,7 @@
     load_qkv = pltpu.make_async_copy(w_qkv_in, w_up.at[:, pl.ds(0, 3 * width)], load_sem.at[8])
     for load in loads[:5]:
         load.start()
+    load_down()
     loads[0].wait()
     pl.semaphore_wait(barrier, count - 1 + planes - 1)
 
@@ -536,7 +538,7 @@
 
     def z_cross(c):
         at = pl.ds(*table[c])
-        return remote(own.at[at], cross_in.at[at], z_send.at[0], z_cross_recv.at[c], me, z_mate)
+        return remote(own.at[at], cross_in.at[at], z_send.at[0], z_cross_recv.at[c % RING], me, z_mate)
 
     def z_back(c):
         at = pl.ds(*table[c])
@@ -590,7 +592,6 @@
     f_start(0, 1, 3, 2, 4)
     loads[5].start()
     load_up()
-    load_down()
     loads[6].start()
     loads[7].start()
     pair = 2 * rows
@@ -623,11 +624,23 @@
         loads[2 + k].wait()
     f_wait(0)
     qkv_chip(me)
+    loads[1].wait()
+    load_down(wait=True)
+
+    def active_grad(k):
+        tile = pl.ds(k * width, width)
+        grad_rows[:, tile] = low(dot_nt(cot_all[mine, :], w_down[tile, :]))
+
+    tiles = ff // width
+    for k in range(tiles // 2):
+        active_grad(k)
     f_wait(1)
     f_start(5, 7)
     f_wait(3)
     f_start(6, 9)
     c_start(0, 1, 3, 2, 4)
+    for k in range(tiles // 2, tiles):
+        active_grad(k)
     f_wait(2)
     f_start(8)
     f_wait(4)
@@ -706,7 +719,6 @@
     hidden2_all[mine, :] = hidden2_own
 
     load_up(wait=True)
-    tiles = ff // width
     pieces = []
     for k in range(tiles):
         tile = pl.ds(k * width, width)
@@ -725,13 +737,11 @@
             active_s[mine, pl.ds(k * part, part)] = active_rows[:, span(k * width + me * part, part)]
         if k == tiles - 2:
             h_start(0, 1, 3, 2, 4)
-    loads[1].wait()
-    load_down(wait=True)
     acc_b[...] = jnp.zeros_like(acc_b)
 
     def back_tile(k):
         tile = span(k * width, width)
-        grad = low(dot_nt(cot_all[mine, :], w_down[tile, :]) * wide(slope_rows[:, tile]))
+        grad = low(wide(grad_rows[:, tile]) * wide(slope_rows[:, tile]))
         acc_b[...] += dot_nt(grad, w_up[:, tile])
 
     def down_piece(k):
@@ -794,7 +804,7 @@
     for c in range(0, count, 2):
         at = span(c * rows, pair)
         slope_s[at, :] = low(dot_nt(cot_all[at, :], w_down_s[...]))
-    z_upto(7)
+    z_upto(6)
     last_piece = pl.ds((tiles - 1) * part, part)
 
     def slab_chip(index):
@@ -815,17 +825,17 @@
     slab_chip(over_x)
     h_wait(9)
     slab_chip(over_y)
-    z_upto(9)
+    z_upto(7)
     h_wait(5)
     h_start(11)
     h_wait(6)
     h_start(12)
     slab_rows(span(corner * rows, rows))
-    z_upto(10)
+    z_upto(9)
     h_wait(11)
     slab_rows(span(flip(corner, 1) * rows, rows))
     down_piece(tiles - 1)
-    z_upto(11)
+    z_upto(10)
 
     up_at = slab
     mixed_at = up_at + rows * tiles
@@ -865,7 +875,7 @@
             u_send(mate, near_by)
             own[u_place(me, me)] = up_stage[mine, :]
         if near_by in (2, 0):
-            z_upto(12 if near_by else 13)
+            z_upto(11 if near_by else 13)
     u_wait(u_sems[0], 1)
     z_outer(up_at, up_at + rows)
 
@@ -1114,7 +1124,8 @@
     scratch = (
         [low_array(total, width)] * 5
         + [low_array(width, 3 * part), low_array(width, width), low_array(width, ff), low_array(ff, width)]
-        + [low_array(width, slab), low_array(slab, width), low_array(rows, ff), low_array(rows, ff)]
+        + [low_array(width, slab), low_array(slab, width)]
+        + [low_array(rows, ff)] * 3
         + [low_array(total, 3 * part)]
         + [low_array(local, total, part)] * 4
         + [low_array(local, total, total), wide_array(part, total)]
@@ -1128,7 +1139,7 @@
         + [wide_array(count, 8, part)] * 2
         + [wide_array(planes, 8, part)]
         + [copies(11), copies(4), copies(4, 10), copies(13), copies(13), copies(2)]
-        + [copies(chunks)] * 2
+        + [copies(chunks), copies(RING)]
     )
     kept = pl.pallas_call(
         functools.partial(layer_kernel, count, planes),

time: 122 us -> 121 us (level)
  no operation moved by 1% of the time
where the time goes in v8:
time: 121 us
  Pallas kernels  120 us (99%)
    pallas_call x1, Pallas kernels, shards_by_heads(): pl.pallas_call(functools.partial(layer_kernel, count, planes), out_shape=...  117 us
    pallas_call x1, Pallas kernels, shards_by_heads(): pl.pallas_call(finish_kernel, out_shape=tuple((jax.ShapeDtypeStruct(shape...  3.53 us

profile of v8, /device:TPU:0, one launch (start us, length us, event | category | flops | bytes accessed | tf_op | source)
XLA Modules:
  0.0 121.2 jit_solution(7970192820529302794)
XLA Ops:
  0.6 116.8 %shard_map.152 = (bf16[128,1024]{1,0:T(8,128)(2,1)S(1)}, f32[128,1024]{1,0:T(8,128)S(1)}, f32[8,128]{1,0:T(8,128)S(1)}, bf16[1536,1024]{1,0:T(8,128)(2,1)S(1)}) custom-call(bf16[1,128,1024]{2,1,0:T(8,128)(2,1)} %frames_in.1, f32[1,1024]{1,0:T(1,128)} %bitcast.2, bf16[1024,3072]{1,0:T(8,128)(2,1)} %w_qkv_in.1, bf16[1024,1024]{1,0:T(8,128)(2,1)} %w_out_in.1, ...), custom_call_target="tpu_custom_call" | custom-call | tf_op jit(solution)/shard_map/pallas_call | solution.py:1144
  117.5 3.5 %shard_map.153 = (bf16[1,128,1024]{2,1,0:T(8,128)(2,1)}, f32[1,128,1024]{2,1,0:T(8,128)}, f32[128]{0:T(128)}, f32[128,3072]{1,0:T(8,128)}, f32[128,1024]{1,0:T(8...) custom-call(bf16[128,1024]{1,0:T(8,128)(2,1)S(1)} %get-tuple-element.12.result_in, ...), custom_call_target="tpu_custom_call" | custom-call | tf_op jit(solution)/shard_map/pallas_call | solution.py:1158

commit v9 on v8

--- a/solution.py
+++ b/solution.py
@@ -534,7 +534,7 @@
 
     def z_raw(c):
         at = pl.ds(*table[c])
-        return remote(own.at[at], sum_ref.at[at], z_send.at[0], z_outer_recv.at[c], me, z_core)
+        return remote(own.at[at], sum_ref.at[at], z_send.at[0], z_outer_recv.at[c % (2 * RING)], me, z_core)
 
     def z_cross(c):
         at = pl.ds(*table[c])
@@ -542,7 +542,7 @@
 
     def z_back(c):
         at = pl.ds(*table[c])
-        return remote(sum_ref.at[at], sum_ref.at[at], z_send.at[1], z_outer_recv.at[c], me, z_edge)
+        return remote(sum_ref.at[at], sum_ref.at[at], z_send.at[1], z_outer_recv.at[c % (2 * RING)], me, z_edge)
 
     def z_join(c):
         at = pl.ds(*table[c])
@@ -587,6 +587,8 @@
         def _():
             for c, (start, size) in enumerate(table):
                 if first <= start < last:
+                    if c >= 2 * RING:
+                        z_back(c - 2 * RING).wait_recv()
                     z_raw(c).start()
 
     f_start(0, 1, 3, 2, 4)
@@ -1052,7 +1054,7 @@
     def _():
         remote(own, own, z_send.at[0], z_outer_recv.at[0], me, z_core).wait_send()
 
-        for c in range(len(table)):
+        for c in range(len(table) - 2 * RING, len(table)):
             z_back(c).wait_recv()
 
     @pl.when(inner)
@@ -1108,7 +1110,6 @@
     bf16, f32 = jnp.bfloat16, jnp.float32
     blocks = ff // width
     own_rows = slab + rows * blocks + part + rows * 3
-    chunks = len(chain_table(own_rows))
     vmem, anywhere = pl.BlockSpec(memory_space=pltpu.VMEM), pl.BlockSpec(memory_space=pl.ANY)
     smem = pl.BlockSpec(memory_space=pltpu.SMEM)
 
@@ -1139,7 +1140,7 @@
         + [wide_array(count, 8, part)] * 2
         + [wide_array(planes, 8, part)]
         + [copies(11), copies(4), copies(4, 10), copies(13), copies(13), copies(2)]
-        + [copies(chunks), copies(RING)]
+        + [copies(2 * RING), copies(RING)]
     )
     kept = pl.pallas_call(
         functools.partial(layer_kernel, count, planes),

time: 121 us -> 121 us (level)
  no operation moved by 1% of the time
where the time goes in v9:
time: 121 us
  Pallas kernels  120 us (99%)
    pallas_call x1, Pallas kernels, shards_by_heads(): pl.pallas_call(functools.partial(layer_kernel, count, planes), out_shape=...  117 us
    pallas_call x1, Pallas kernels, shards_by_heads(): pl.pallas_call(finish_kernel, out_shape=tuple((jax.ShapeDtypeStruct(shape...  3.53 us

profile of v9, /device:TPU:0, one launch (start us, length us, event | category | flops | bytes accessed | tf_op | source)
XLA Modules:
  0.0 121.0 jit_solution(10260372289631161857)
XLA Ops:
  0.6 116.6 %shard_map.152 = (bf16[128,1024]{1,0:T(8,128)(2,1)S(1)}, f32[128,1024]{1,0:T(8,128)S(1)}, f32[8,128]{1,0:T(8,128)S(1)}, bf16[1536,1024]{1,0:T(8,128)(2,1)S(1)}) custom-call(bf16[1,128,1024]{2,1,0:T(8,128)(2,1)} %frames_in.1, f32[1,1024]{1,0:T(1,128)} %bitcast.2, bf16[1024,3072]{1,0:T(8,128)(2,1)} %w_qkv_in.1, bf16[1024,1024]{1,0:T(8,128)(2,1)} %w_out_in.1, ...), custom_call_target="tpu_custom_call" | custom-call | tf_op jit(solution)/shard_map/pallas_call | solution.py:1145
  117.3 3.5 %shard_map.153 = (bf16[1,128,1024]{2,1,0:T(8,128)(2,1)}, f32[1,128,1024]{2,1,0:T(8,128)}, f32[128]{0:T(128)}, f32[128,3072]{1,0:T(8,128)}, f32[128,1024]{1,0:T(8...) custom-call(bf16[128,1024]{1,0:T(8,128)(2,1)S(1)} %get-tuple-element.12.result_in, ...), custom_call_target="tpu_custom_call" | custom-call | tf_op jit(solution)/shard_map/pallas_call | solution.py:1159
